TPU v7x, 128 devices: a whole 4x4x4 slice. The times are simulated.
128 devices in a mesh: tm: 4 (over z_lo, core), strip: 32 (over y, z_hi, x).
Axes of the slice: x: 4, y: 4, z: 4 (z_hi: 2, z_lo: 2; z = z_hi * 2 + z_lo), core: 2. Of those that a mesh axis runs over, the one named last changes fastest.
Arguments:
- screen_vec: float32 [4, 4096, 4096], P('tm', 'strip'), may hold values from -8 to 8
- prior_scale: float32 [4], P('tm'), may hold values from 0.5 to 2
- flow_weight: float32 [4], P('tm'), may hold values from 0.5 to 2
- wind: int32 [4, 2], P('tm'), may hold values from -32 to 32, as said below
- pierce_point_strip: int32 [4, 4096, 64, 1], P('tm', 'strip'), may hold values from 0 to 31; in each aligned block of 8192 rows (0 to 8191, 8192 to 16383, ..., all dimensions but the last counted through in order) at most 512 rows name the same one
- pierce_block: int32 [4, 4096, 64], P('tm', 'strip'), may hold values from 0 to 4095
- pierce_weights: bfloat16 [4, 4096, 64, 128], P('tm', 'strip'), may hold values from -1.5 to 1.5
- noise_prec: float32 [4, 4096, 64], P('tm', 'strip'), may hold values from 1 to 16
Outputs:
- hessian_vec: float32 [4, 4096, 4096], P('tm', 'strip')
Inputs may be any that keep to these rules, and one draw needn't show every extreme that they name: `pierce_point_strip`: among the pierce points of one slot and one group of 128 antennas (the rows of one device), at most 512 lie in one strip. `wind`: row shifts are never zero.
All inputs are finite; a program needn't handle non-finite values.
Results may differ from a plain program's by a relative error of at most 0.0015.
Values may be sent and summed in bfloat16 or wider, within the bound.
A program may use at most 192 MiB of HBM per device.

v0:
```python
import math

import jax
import jax.numpy as jnp
from jax import lax
from jax.sharding import PartitionSpec as P

WIND = 32


KZERO = 2.0
EXACT_MODE = lax.Precision.HIGHEST


def extended(block, sides, width):
    for axis, dim in sides:
        count = lax.axis_size(axis)
        forward = [(i, i + 1) for i in range(count - 1)]
        forward.append((count - 1, 0))
        backward = [(target, source) for source, target in forward]
        low = lax.ppermute(
            lax.slice_in_dim(block, block.shape[dim] - width, None, axis=dim), axis, forward
        )
        high = lax.ppermute(lax.slice_in_dim(block, 0, width, axis=dim), axis, backward)
        block = jnp.concatenate([low, block, high], axis=dim)
    return block


def from_behind(value, axis, steps):
    count = lax.axis_size(axis)
    leading, last = (max(0, -steps), min(count, count - steps))
    return lax.ppermute(value, axis, [(source, source + steps) for source in range(leading, last)])


def amplitude(freq_rows, freq_cols, side):
    fold_rows = jnp.minimum(freq_rows, side - freq_rows).astype(jnp.float32)
    fold_cols = jnp.minimum(freq_cols, side - freq_cols).astype(jnp.float32)
    radius = (fold_rows * fold_rows + fold_cols * fold_cols) / (KZERO * KZERO)
    return side / (2.0 * KZERO) * jnp.power(1.0 + radius, -11.0 / 12.0)


def spectral(side, col_start, col_count, slot_scale):
    freq_rows = jnp.arange(side, dtype=jnp.int32)[:, None]
    freq_cols = col_start + jnp.arange(col_count, dtype=jnp.int32)[None, :]
    return amplitude(freq_rows, freq_cols, side) * (slot_scale / (side * side))


def tables(side, sign):
    radix = math.isqrt(side)
    digits = jnp.arange(radix, dtype=jnp.int32)
    product = digits[:, None] * digits[None, :]
    small_angle = sign * 2.0 * math.pi * (product % radix).astype(jnp.float32) / radix
    twist_angle = sign * 2.0 * math.pi * product.astype(jnp.float32) / side
    return (jnp.cos(small_angle), jnp.sin(small_angle), jnp.cos(twist_angle), jnp.sin(twist_angle))


def complex_einsum(form, left_re, left_im, right_re, right_im):
    real_part = jnp.einsum(form, left_re, right_re, precision=EXACT_MODE) - jnp.einsum(
        form, left_im, right_im, precision=EXACT_MODE
    )
    imag_part = jnp.einsum(form, left_re, right_im, precision=EXACT_MODE) + jnp.einsum(
        form, left_im, right_re, precision=EXACT_MODE
    )
    return (real_part, imag_part)


def transform_last(real_in, imag_in, sign):
    side = real_in.shape[-1]
    radix = math.isqrt(side)
    leading = real_in.shape[:-1]
    mat_re, mat_im, twist_re, twist_im = tables(side, sign)
    split_re = real_in.reshape(leading + (radix, radix))
    split_im = imag_in.reshape(leading + (radix, radix))
    section_re, section_im = complex_einsum("...ab,ak->...kb", split_re, split_im, mat_re, mat_im)
    turned_re = section_re * twist_re - section_im * twist_im
    turned_im = section_re * twist_im + section_im * twist_re
    final_re, final_im = complex_einsum("...kb,bm->...mk", turned_re, turned_im, mat_re, mat_im)
    return (final_re.reshape(leading + (side,)), final_im.reshape(leading + (side,)))


def transform_first(real_in, imag_in, sign):
    side = real_in.shape[0]
    radix = math.isqrt(side)
    trailing = real_in.shape[1:]
    mat_re, mat_im, twist_re, twist_im = tables(side, sign)
    split_re = real_in.reshape((radix, radix) + trailing)
    split_im = imag_in.reshape((radix, radix) + trailing)
    section_re, section_im = complex_einsum("abc,ak->kbc", split_re, split_im, mat_re, mat_im)
    turned_re = section_re * twist_re[:, :, None] - section_im * twist_im[:, :, None]
    turned_im = section_re * twist_im[:, :, None] + section_im * twist_re[:, :, None]
    final_re, final_im = complex_einsum("kbc,bm->mkc", turned_re, turned_im, mat_re, mat_im)
    return (final_re.reshape((side,) + trailing), final_im.reshape((side,) + trailing))


def whiten(screen_in, slot_scale):
    side = screen_in.shape[1]
    strip_index = lax.axis_index("strip")
    rows_re, rows_im = transform_last(screen_in, jnp.zeros_like(screen_in), -1.0)
    cols_re, column_imaginary = (
        lax.all_to_all(rows_re, "strip", split_axis=1, concat_axis=0, tiled=True),
        lax.all_to_all(rows_im, "strip", split_axis=1, concat_axis=0, tiled=True),
    )
    col_count = cols_re.shape[1]
    spec_re, spec_im = transform_first(cols_re, column_imaginary, -1.0)
    scaling = spectral(side, strip_index * col_count, col_count, slot_scale)
    back_re, back_im = transform_first(scaling * spec_re, scaling * spec_im, 1.0)
    full_re, full_im = (
        lax.all_to_all(back_re, "strip", split_axis=0, concat_axis=1, tiled=True),
        lax.all_to_all(back_im, "strip", split_axis=0, concat_axis=1, tiled=True),
    )
    result_re, result_im = transform_last(full_re, full_im, 1.0)
    return result_re


def exchange_values(values):
    return lax.all_to_all(values, "strip", split_axis=0, concat_axis=0, tiled=True)


def misfit(screen, strip_of, block_of, weights, precision_of):
    peers = lax.axis_size("strip")
    antennas, directions, block_width = weights.shape
    points = antennas * directions
    capacity = 2 * points // peers
    target = strip_of.reshape(points)
    block_ids = block_of.reshape(points)
    one_hot = (target[:, None] == jnp.arange(peers, dtype=jnp.int32)[None, :]).astype(jnp.int32)
    position = jnp.sum((jnp.cumsum(one_hot, axis=0) - 1) * one_hot, axis=1)
    send_weights = (
        jnp.zeros((peers, capacity, block_width), jnp.bfloat16)
        .at[target, position]
        .set(weights.reshape(points, block_width))
    )
    send_ids = jnp.zeros((peers, capacity), jnp.int32).at[target, position].set(block_ids)
    recv_weights = lax.all_to_all(send_weights, "strip", split_axis=0, concat_axis=0, tiled=True)
    recv_ids = lax.all_to_all(send_ids, "strip", split_axis=0, concat_axis=0, tiled=True)
    tiles = screen.reshape(-1, block_width)
    flat_ids = recv_ids.reshape(-1)
    flat_weights = recv_weights.reshape(-1, block_width).astype(jnp.float32)
    phases = jnp.sum(tiles[flat_ids] * flat_weights, axis=1).reshape(peers, capacity)
    returned = exchange_values(phases)
    phase_own = returned[target, position].reshape(antennas, directions)
    centre = jnp.sum(precision_of * phase_own, axis=1, keepdims=True) / jnp.sum(
        precision_of, axis=1, keepdims=True
    )
    weighted = precision_of * (phase_own - centre)
    send_resid = (
        jnp.zeros((peers, capacity), jnp.float32).at[target, position].set(weighted.reshape(points))
    )
    recv_resid = exchange_values(send_resid)
    update = jnp.zeros_like(tiles).at[flat_ids].add(flat_weights * recv_resid.reshape(-1, 1))
    return update.reshape(screen.shape)


def wind_margin(values):
    return extended(values, (("strip", 0),), WIND)


def frozen_flow(screen, flow_rate, row_shift, col_shift):
    strip_rows = screen.shape[0]
    keep_mask = (lax.axis_index("tm") < lax.axis_size("tm") - 1).astype(jnp.float32)
    factor = flow_rate * keep_mask
    following_slot = from_behind(screen, "tm", -1)
    widened = wind_margin(screen)
    moved = jnp.roll(
        lax.dynamic_slice_in_dim(widened, WIND - row_shift, strip_rows, 0), col_shift, axis=1
    )
    diff = factor * (following_slot - moved)
    widened_diff = wind_margin(diff)
    pulled = jnp.roll(
        lax.dynamic_slice_in_dim(widened_diff, WIND + row_shift, strip_rows, 0), -col_shift, axis=1
    )
    earlier = from_behind(diff, "tm", 1)
    return earlier - pulled


def local(
    screen_vec,
    prior_scale,
    flow_weight,
    wind,
    pierce_point_strip,
    pierce_block,
    pierce_weights,
    noise_prec,
):
    screen_in = screen_vec[0]
    slot_scale = prior_scale[0]
    screen = whiten(screen_in, slot_scale)
    gradient = misfit(
        screen, pierce_point_strip[0, :, :, 0], pierce_block[0], pierce_weights[0], noise_prec[0]
    )
    gradient = gradient + frozen_flow(screen, flow_weight[0], wind[0, 0], wind[0, 1])
    return (screen_in + whiten(gradient, slot_scale))[None]


def solution(mesh):
    in_specs = (
        P("tm", "strip", None),
        P("tm"),
        P("tm"),
        P("tm", None),
        P("tm", "strip", None, None),
        P("tm", "strip", None),
        P("tm", "strip", None, None),
        P("tm", "strip", None),
    )
    out_specs = P("tm", "strip", None)
    return jax.shard_map(local, mesh=mesh, in_specs=in_specs, out_specs=out_specs, check_vma=False)
```

profile of v0, /device:TPU:1, one launch (start us, length us, event | category | flops | bytes accessed | tf_op | source)
XLA Modules:
  0.0 863.4 jit_solution(10341831363700098001)
XLA Ops:
  26.1 11.4 %all-to-all-start.3 = ((f32[128,32,128]{0,2,1:T(8,128)}), f32[128,32,128]{0,2,1:T(8,128)}, u32[]{:S(2)}, u32[]{:S(2)}) async-start(f32[128,32,128]{0,2,1:T(8,128)} %bitcast.20), calls=%async_computation.3 | async-start | bytes 4194304 | tf_op jit(solution)/shard_map/all_to_all | solution.py:101
  39.1 17.1 %reduce-window.6 = s32[32,64,128]{2,1,0:T(8,128)S(1)} reduce-window(s32[32,64,128]{2,1,0:T(8,128)} %fusion.184, s32[]{:T(128)} %constant.110.clone.1), window={size=1x1x128 pad=0_0x0_0x127_0}, to_apply=%region_0.1 | reduce-window | flops 33292288 | bytes 2097156 | tf_op jit(solution)/shard_map/reduce-window
  67.3 9.4 %all-to-all-start.2 = ((f32[128,32,128]{0,2,1:T(8,128)}), f32[128,32,128]{0,2,1:T(8,128)}, u32[]{:S(2)}, u32[]{:S(2)}) async-start(f32[128,32,128]{0,2,1:T(8,128)} %bitcast.16), calls=%async_computation.2 | async-start | bytes 4194304 | tf_op jit(solution)/shard_map/all_to_all | solution.py:100
  78.1 31.0 %scatter_custom_fusion.1 = s32[16384]{0:T(1024)} fusion(s32[8192]{0:T(1024)S(1)} %broadcast_select_fusion, s32[8192]{0:T(1024)S(1)} %reshape.439, s32[]{:T(128)} %constant.110.clone.1), kind=kCustom, calls=%fused_computation.271 | custom fusion | bytes 65540
  120.2 9.2 %all-to-all-start = ((s32[32,1,512]{2,1,0:T(1,128)}), s32[32,1,512]{2,1,0:T(1,128)S(1)}, u32[]{:S(2)}, u32[]{:S(2)}) async-start(s32[32,1,512]{2,1,0:T(1,128)} %bitcast.5), calls=%async_computation | async-start | bytes 131072 | tf_op jit(solution)/shard_map/all_to_all | solution.py:135
  175.1 9.4 %all-to-all-start.5 = ((f32[32,128,128]{2,1,0:T(8,128)}), f32[32,128,128]{2,1,0:T(8,128)}, u32[]{:S(2)}, u32[]{:S(2)}) async-start(f32[32,128,128]{2,1,0:T(8,128)} %bitcast.279), calls=%async_computation.5 | async-start | bytes 4194304 | tf_op jit(solution)/shard_map/all_to_all | solution.py:109
  194.8 16.0 %all-to-all-done.5 = f32[32,128,128]{2,1,0:T(8,128)} async-done(((f32[32,128,128]{2,1,0:T(8,128)}), f32[32,128,128]{2,1,0:T(8,128)}, u32[]{:S(2)}, u32[]{:S(2)}) %all-to-all-start.5) | async-done | bytes 2097184 | tf_op jit(solution)/shard_map/all_to_all | solution.py:109
  217.1 23.9 %scatter_custom_fusion.2 = bf16[16384,128]{1,0:T(8,128)(2,1)} fusion(s32[8192]{0:T(1024)S(1)} %broadcast_select_fusion, bf16[8192,128]{1,0:T(8,128)(2,1)} %bitcast.291, bf16[]{:T(256)} %constant.126.clone.1), kind=kCustom, calls=%fused_computation.37 | custom fusion | bytes 4194816
  244.7 7.1 all-to-all-start.1
  318.6 54.4 %gather_fusion = f32[16384,128]{1,0:T(8,128)} fusion(f32[4096,128]{1,0:T(8,128)S(1)} %reshape_reshape.3, s32[16384]{0:T(1024)S(1)} %broadcast_clamp_fusion), kind=kCustom, calls=%fused_computation | custom fusion | bytes 16842752 | tf_op jit(solution)/shard_map/gather | solution.py:139
  373.0 6.8 multiply_reduce_fusion
  394.2 65.0 %gather_fusion.1 = f32[8192]{0:T(1024)S(1)} fusion(f32[32,512]{1,0:T(8,128)S(1)} %bitcast.254, s32[8192]{0:T(1024)S(1)} %bitcast.255), kind=kCustom, calls=%fused_computation.1 | custom fusion | bytes 131072 | tf_op jit(solution)/shard_map/gather | solution.py:141
  459.6 31.0 %scatter_custom_fusion.3 = f32[16384]{0:T(1024)} fusion(s32[8192]{0:T(1024)S(1)} %broadcast_select_fusion, f32[8192]{0:T(1024)S(1)} %subtract_multiply_fusion.2, f32[]{:T(128)} %constant.122.clone.1), kind=kCustom, calls=%fused_computation.269 | custom fusion | bytes 65540
  490.6 6.8 all-to-all-start.7
  506.6 6.5 collective-permute-start.5
  513.1 6.9 bitcast_multiply_fusion
  520.0 102.3 %scatter_custom_fusion = f32[4096,128]{1,0:T(8,128)} fusion(s32[16384]{0:T(1024)S(1)} %bitcast.287, f32[16384,128]{1,0:T(8,128)} %bitcast_multiply_fusion, f32[]{:T(128)} %constant.122.clone.1), kind=kCustom, calls=%fused_computation.185 | custom fusion | flops 2097152 | bytes 2097664 | tf_op jit(solution)/shard_map/scatter-add | solution.py:150
  652.6 9.4 %all-to-all-start.9 = ((f32[128,32,128]{0,2,1:T(8,128)}), f32[128,32,128]{0,2,1:T(8,128)}, u32[]{:S(2)}, u32[]{:S(2)}) async-start(f32[128,32,128]{0,2,1:T(8,128)} %bitcast.281), calls=%async_computation.9 | async-start | bytes 4194304 | tf_op jit(solution)/shard_map/all_to_all | solution.py:101
  672.3 19.7 %all-to-all-done.9 = f32[128,32,128]{0,2,1:T(8,128)} async-done(((f32[128,32,128]{0,2,1:T(8,128)}), f32[128,32,128]{0,2,1:T(8,128)}, u32[]{:S(2)}, u32[]{:S(2)}) %all-to-all-start.9) | async-done | bytes 2097184 | tf_op jit(solution)/shard_map/all_to_all | solution.py:101
  708.9 17.1 %all-to-all-done.8 = f32[128,32,128]{0,2,1:T(8,128)} async-done(((f32[128,32,128]{0,2,1:T(8,128)}), f32[128,32,128]{0,2,1:T(8,128)}, u32[]{:S(2)}, u32[]{:S(2)}) %all-to-all-start.8) | async-done | bytes 2097184 | tf_op jit(solution)/shard_map/all_to_all | solution.py:100
  771.8 7.2 all-to-all-start.11
  789.4 17.3 %all-to-all-done.11 = f32[32,128,128]{2,1,0:T(8,128)} async-done(((f32[32,128,128]{2,1,0:T(8,128)}), f32[32,128,128]{2,1,0:T(8,128)}, u32[]{:S(2)}, u32[]{:S(2)}) %all-to-all-start.11) | async-done | bytes 2097184 | tf_op jit(solution)/shard_map/all_to_all | solution.py:109
  806.7 7.6 all-to-all-start.10
  825.2 16.2 %all-to-all-done.10 = f32[32,128,128]{2,1,0:T(8,128)} async-done(((f32[32,128,128]{2,1,0:T(8,128)}), f32[32,128,128]{2,1,0:T(8,128)}, u32[]{:S(2)}, u32[]{:S(2)}) %all-to-all-start.10) | async-done | bytes 2097184 | tf_op jit(solution)/shard_map/all_to_all | solution.py:108
  (202 shorter events, 346.8 us)
Async XLA Ops:
  26.1 11.4 %copy-start.22 = (s32[1,128,64,1]{1,3,2,0:T(1,128)S(1)}, s32[1,128,64,1]{1,3,2,0:T(1,128)}, u32[]{:S(2)}) copy-start(s32[1,128,64,1]{1,3,2,0:T(1,128)} %param.14) | copy-start | bytes 98308
  26.1 41.2 %all-to-all-start.3 = ((f32[128,32,128]{0,2,1:T(8,128)}), f32[128,32,128]{0,2,1:T(8,128)}, u32[]{:S(2)}, u32[]{:S(2)}) async-start(f32[128,32,128]{0,2,1:T(8,128)} %bitcast.20), calls=%async_computation.3 | async-start | bytes 4194304 | tf_op jit(solution)/shard_map/all_to_all | solution.py:101
  37.9 19.4 %copy-start.10 = (f32[128,64,64]{0,1,2:T(8,128)S(1)}, f32[128,64,64]{0,1,2:T(8,128)}, u32[]{:S(2)}) copy-start(f32[128,64,64]{0,1,2:T(8,128)} %copy-done.9) | copy-start | bytes 6291460
  67.3 52.9 %all-to-all-start.2 = ((f32[128,32,128]{0,2,1:T(8,128)}), f32[128,32,128]{0,2,1:T(8,128)}, u32[]{:S(2)}, u32[]{:S(2)}) async-start(f32[128,32,128]{0,2,1:T(8,128)} %bitcast.16), calls=%async_computation.2 | async-start | bytes 4194304 | tf_op jit(solution)/shard_map/all_to_all | solution.py:100
  120.2 54.9 %all-to-all-start = ((s32[32,1,512]{2,1,0:T(1,128)}), s32[32,1,512]{2,1,0:T(1,128)S(1)}, u32[]{:S(2)}, u32[]{:S(2)}) async-start(s32[32,1,512]{2,1,0:T(1,128)} %bitcast.5), calls=%async_computation | async-start | bytes 131072 | tf_op jit(solution)/shard_map/all_to_all | solution.py:135
  175.1 35.8 %all-to-all-start.5 = ((f32[32,128,128]{2,1,0:T(8,128)}), f32[32,128,128]{2,1,0:T(8,128)}, u32[]{:S(2)}, u32[]{:S(2)}) async-start(f32[32,128,128]{2,1,0:T(8,128)} %bitcast.279), calls=%async_computation.5 | async-start | bytes 4194304 | tf_op jit(solution)/shard_map/all_to_all | solution.py:109
  210.8 32.5 %all-to-all-start.4 = ((f32[32,128,128]{2,1,0:T(8,128)}), f32[32,128,128]{2,1,0:T(8,128)S(1)}, u32[]{:S(2)}, u32[]{:S(2)}) async-start(f32[32,128,128]{2,1,0:T(8,128)} %bitcast.280), calls=%async_computation.4 | async-start | bytes 4194304 | tf_op jit(solution)/shard_map/all_to_all | solution.py:108
  244.7 128.3 %all-to-all-start.1 = ((bf16[32,512,128]{2,1,0:T(8,128)(2,1)}), bf16[32,512,128]{2,1,0:T(8,128)(2,1)}, u32[]{:S(2)}, u32[]{:S(2)}) async-start(bf16[32,512,128]{2,1,0:T(8,128)(2,1)} %bitcast.277), calls=%async_computation.1 | async-start | bytes 8388608 | tf_op jit(solution)/shard_map/all_to_all | solution.py:134
  279.0 11.0 %copy-start = (f32[128,64,64]{0,1,2:T(8,128)}, f32[128,64,64]{0,1,2:T(8,128)S(1)}, u32[]{:S(2)}) copy-start(f32[128,64,64]{0,1,2:T(8,128)S(1)} %subtract_bitcast_fusion.4) | copy-start | bytes 6291460
  284.6 213.6 %collective-permute-start = (f32[128,4096]{1,0:T(8,128)}, f32[128,4096]{1,0:T(8,128)}, u32[]{:S(2)}, u32[]{:S(2)}) collective-permute-start(f32[128,4096]{1,0:T(8,128)} %copy.241), channel_id=1, source_target_pairs={{32,0},{64,32},{96,64},{33,1},{65,33},{97,65},{34,2},{66,34},{98,6... | collective-permute-start | bytes 6291464 | tf_op jit(solution)/shard_map/ppermute | solution.py:32
  307.2 190.2 %collective-permute-start.1 = (f32[32,4096]{1,0:T(8,128)}, f32[32,4096]{1,0:T(8,128)}, u32[]{:S(2)}, u32[]{:S(2)}) collective-permute-start(f32[32,4096]{1,0:T(8,128)} %slice.33), channel_id=1, source_target_pairs={{0,1},{1,2},{2,3},{3,4},{4,5},{5,6},{6,7},{7,8},{8,9},{9,10},{10,1... | collective-permute-start | bytes 1572872 | tf_op jit(solution)/shard_map/ppermute | solution.py:21
  312.7 184.7 %collective-permute-start.2 = (f32[32,4096]{1,0:T(8,128)}, f32[32,4096]{1,0:T(8,128)S(1)}, u32[]{:S(2)}, u32[]{:S(2)}) collective-permute-start(f32[32,4096]{1,0:T(8,128)} %slice.35), channel_id=1, source_target_pairs={{1,0},{2,1},{3,2},{4,3},{5,4},{6,5},{7,6},{8,7},{9,8},{10,9},{11,1... | collective-permute-start | bytes 1572872 | tf_op jit(solution)/shard_map/ppermute | solution.py:24
  373.0 12.4 %copy-start.24 = (s32[1,2]{1,0:T(1,128)S(1)}, s32[1,2]{1,0:T(1,128)}, u32[]{:S(2)}) copy-start(s32[1,2]{1,0:T(1,128)} %param.13) | copy-start | bytes 28
  373.0 17.6 %copy-start.21 = (f32[1,128,64]{1,2,0:T(8,128)S(1)}, f32[1,128,64]{1,2,0:T(8,128)}, u32[]{:S(2)}) copy-start(f32[1,128,64]{1,2,0:T(8,128)} %param.17) | copy-start | bytes 98308
  380.5 13.7 %all-to-all-start.6 = ((f32[32,1,512]{2,1,0:T(1,128)}), f32[32,1,512]{2,1,0:T(1,128)S(1)}, u32[]{:S(2)}, u32[]{:S(2)}) async-start(f32[32,1,512]{2,1,0:T(1,128)} %all_to_all.134), calls=%async_computation.6 | async-start | bytes 131072 | tf_op jit(solution)/shard_map/all_to_all | solution.py:116
  394.2 103.3 %copy-start.18 = (f32[128,4096]{1,0:T(8,128)S(1)}, f32[128,4096]{1,0:T(8,128)}, u32[]{:S(2)}) copy-start(f32[128,4096]{1,0:T(8,128)} %copy.241) | copy-start | bytes 6291460
  490.6 22.4 %all-to-all-start.7 = ((f32[32,1,512]{2,1,0:T(1,128)}), f32[32,1,512]{2,1,0:T(1,128)S(1)}, u32[]{:S(2)}, u32[]{:S(2)}) async-start(f32[32,1,512]{2,1,0:T(1,128)} %bitcast.36), calls=%async_computation.7 | async-start | bytes 131072 | tf_op jit(solution)/shard_map/all_to_all | solution.py:116
  500.9 125.9 %collective-permute-start.3 = (f32[128,4096]{1,0:T(8,128)S(1)}, f32[128,4096]{1,0:T(8,128)}, u32[]{:S(2)}, u32[]{:S(2)}) collective-permute-start(f32[128,4096]{1,0:T(8,128)S(1)} %fusion.9), channel_id=1, source_target_pairs={{0,32},{32,64},{64,96},{1,33},{33,65},{65,97},{2,34},{34,66},{66,9... | collective-permute-start | bytes 6291464 | tf_op jit(solution)/shard_map/ppermute | solution.py:32
  504.9 120.1 %collective-permute-start.4 = (f32[32,4096]{1,0:T(8,128)S(1)}, f32[32,4096]{1,0:T(8,128)}, u32[]{:S(2)}, u32[]{:S(2)}) collective-permute-start(f32[32,4096]{1,0:T(8,128)S(1)} %get-tuple-element.23), channel_id=1, source_target_pairs={{0,1},{1,2},{2,3},{3,4},{4,5},{5,6},{6,7},{7,8},{8,9},{9,10},{10,1... | collective-permute-start | bytes 1572872 | tf_op jit(solution)/shard_map/ppermute | solution.py:21
  506.6 118.4 %collective-permute-start.5 = (f32[32,4096]{1,0:T(8,128)S(1)}, f32[32,4096]{1,0:T(8,128)}, u32[]{:S(2)}, u32[]{:S(2)}) collective-permute-start(f32[32,4096]{1,0:T(8,128)S(1)} %get-tuple-element.22), channel_id=1, source_target_pairs={{1,0},{2,1},{3,2},{4,3},{5,4},{6,5},{7,6},{8,7},{9,8},{10,9},{11,1... | collective-permute-start | bytes 1572872 | tf_op jit(solution)/shard_map/ppermute | solution.py:24
  652.6 39.5 %all-to-all-start.9 = ((f32[128,32,128]{0,2,1:T(8,128)}), f32[128,32,128]{0,2,1:T(8,128)}, u32[]{:S(2)}, u32[]{:S(2)}) async-start(f32[128,32,128]{0,2,1:T(8,128)} %bitcast.281), calls=%async_computation.9 | async-start | bytes 4194304 | tf_op jit(solution)/shard_map/all_to_all | solution.py:101
  692.1 34.0 %all-to-all-start.8 = ((f32[128,32,128]{0,2,1:T(8,128)}), f32[128,32,128]{0,2,1:T(8,128)}, u32[]{:S(2)}, u32[]{:S(2)}) async-start(f32[128,32,128]{0,2,1:T(8,128)} %bitcast.49), calls=%async_computation.8 | async-start | bytes 4194304 | tf_op jit(solution)/shard_map/all_to_all | solution.py:100
  771.8 34.8 %all-to-all-start.11 = ((f32[32,128,128]{2,1,0:T(8,128)}), f32[32,128,128]{2,1,0:T(8,128)}, u32[]{:S(2)}, u32[]{:S(2)}) async-start(f32[32,128,128]{2,1,0:T(8,128)} %bitcast.282), calls=%async_computation.11 | async-start | bytes 4194304 | tf_op jit(solution)/shard_map/all_to_all | solution.py:109
  806.7 34.7 %all-to-all-start.10 = ((f32[32,128,128]{2,1,0:T(8,128)}), f32[32,128,128]{2,1,0:T(8,128)}, u32[]{:S(2)}, u32[]{:S(2)}) async-start(f32[32,128,128]{2,1,0:T(8,128)} %bitcast.56), calls=%async_computation.10 | async-start | bytes 4194304 | tf_op jit(solution)/shard_map/all_to_all | solution.py:108
  (21 other events, 98.2 us)
where the time goes:
time: 879 us; the launch traced here: 863 us
  local copies, waits for them, and re-layouts  286 us (33%)
  matrix products  213 us (24%)
  other arithmetic  146 us (17%)
  starting transfers between devices  119 us (14%)
  waiting for transfers between devices  91.3 us (10%)
    scatter-add x1, other arithmetic, misfit(): jnp.zeros_like(tiles).at[flat_ids]  102 us
    unnamed x62, local copies, waits for them, and re-layouts  90 us
    gather x1, local copies, waits for them, and re-layouts, misfit(): phase_own = returned[target, position].reshape(antennas, directions)  65 us
    dot_general x16, matrix products, complex_einsum(): jnp.einsum(form, left_re, right_re, precision=EXACT_MODE)  60.3 us
    dot_general x15, matrix products, complex_einsum(): jnp.einsum(form, left_im, right_im, precision=EXACT_MODE)  54.5 us
    gather x1, local copies, waits for them, and re-layouts, misfit(): tiles[flat_ids] * flat_weights  54.4 us
    dot_general x14, matrix products, complex_einsum(): jnp.einsum(form, left_re, right_im, precision=EXACT_MODE)  53.5 us
    dot_general x13, matrix products, complex_einsum(): jnp.einsum(form, left_im, right_re, precision=EXACT_MODE)  44.6 us
  transfers between devices with their start and end apart: 18, of which 7 were waited for; matrix products, arithmetic and copies ran while one was open for 61% of the time, Pallas kernels for 0%

commit v1 on v0

v1 whole, which is shorter than its diff:
```python
import math

import jax
import jax.numpy as jnp
import ml_dtypes
import numpy as np
from jax import lax
from jax.experimental import pallas as pl
from jax.experimental.pallas import tpu as pltpu
from jax.sharding import PartitionSpec as P

KZERO = 2.0
SIDE = 4096
OUTER = 32
INNER = 128
HALF = 64
PEERS = 32
SLOTS = 512
POINT_ROWS = 64
VMEM_BYTES = 56 * 1024 * 1024
F32 = jnp.float32
BF16 = jnp.bfloat16


def pieces(table, count):
    rest = np.asarray(table, np.float64)
    out = []
    for _ in range(count):
        out.append(rest.astype(np.float32).astype(ml_dtypes.bfloat16))
        rest = rest - out[-1].astype(np.float64)
    return np.stack(out)


def row_tables():
    b = np.arange(INNER)[:, None]
    j = np.arange(HALF)[None, :]
    theta = [2 * np.pi * ((b * j) % INNER) / INNER, 2 * np.pi * ((b * (INNER - 1 - j)) % INNER) / INNER]
    forward = []
    backward = []
    for t in theta:
        forward.append(np.concatenate([np.cos(t), -np.sin(t)], axis=1))
        forward.append(np.concatenate([np.sin(t), np.cos(t)], axis=1))
        backward.append(np.concatenate([np.cos(t).T, np.sin(t).T], axis=1))
        backward.append(np.concatenate([-np.sin(t).T, np.cos(t).T], axis=1))
    fwd = np.concatenate(
        [np.concatenate([forward[0], forward[1]], axis=0), np.concatenate([forward[2], forward[3]], axis=0)], axis=1
    )
    inv = np.concatenate(backward, axis=0)
    sign = np.where(np.arange(INNER) % 2 == 0, 1.0, -1.0)
    t0 = theta[0]
    first = np.concatenate([np.cos(t0), -np.sin(t0)], axis=1)
    first[:, HALF] = sign
    first_inv = np.concatenate([2 * np.cos(t0).T, -2 * np.sin(t0).T], axis=0)
    first_inv[0, :] = 1.0
    first_inv[HALF, :] = sign
    t16 = 2 * np.pi * ((b * (16 + 32 * j)) % SIDE) / SIDE
    mid = np.concatenate([np.cos(t16), -np.sin(t16)], axis=1)
    mid_inv = np.concatenate([2 * np.cos(t16).T, -2 * np.sin(t16).T], axis=0)
    k1 = np.arange(16)[:, None]
    tw = 2 * np.pi * (k1 * np.arange(INNER)[None, :]) / SIDE
    twiddle = np.stack([np.cos(tw), np.sin(tw)]).astype(np.float32)
    return fwd, inv, first, first_inv, mid, mid_inv, twiddle


def column_tables():
    k1 = np.arange(OUTER)[:, None, None]
    k2 = np.arange(INNER)[None, :, None]
    r = np.arange(INNER)[None, None, :]
    theta = 2 * np.pi * (((k1 + OUTER * k2) * r) % SIDE) / SIDE
    fwd = np.concatenate([np.cos(theta), -np.sin(theta)], axis=1)
    theta = theta.transpose(0, 2, 1)
    inv = np.concatenate([np.cos(theta), np.sin(theta)], axis=1)
    return fwd, inv


def split(value):
    high = value.astype(BF16)
    return high, (value - high.astype(F32)).astype(BF16)


def mm(left, right):
    return lax.dot_general(left, right, (((1,), (0,)), ((), ())), preferred_element_type=F32)


def mm_nt(left, right):
    return lax.dot_general(left, right, (((1,), (1,)), ((), ())), preferred_element_type=F32)


def split_into(value, count):
    parts = []
    for i in range(count):
        parts.append(value.astype(BF16))
        if i + 1 < count:
            value = value - parts[-1].astype(F32)
    return parts


def data_by_table(value, tables):
    count = len(tables)
    parts = split_into(value, count)
    total = None
    for order in reversed(range(count)):
        for i in range(order + 1):
            term = mm(parts[i], tables[order - i])
            total = term if total is None else total + term
    return total


def table_by_data(tables, value):
    parts = split_into(value, len(tables))
    left = jnp.concatenate(tables[0:2], axis=1)
    right = jnp.concatenate(parts[0:2], axis=1)
    r = mm(left, jnp.concatenate([right, right], axis=0))
    total = r[:, INNER : 2 * INNER] + r[:, 0:INNER]
    if len(tables) == 3:
        left = jnp.concatenate([tables[0], tables[2]], axis=1)
        total = total + mm(left, jnp.concatenate([parts[2], parts[0]], axis=0))
    return total


def every(ref):
    return [ref[i] for i in range(ref.shape[0])]


def c_mul(value, factor):
    re, im = value
    c, s = factor.real, factor.imag
    if im is None:
        return (re * c, re * s)
    return (re * c - im * s, re * s + im * c)


def real_forward(xs):
    n = len(xs)
    if n == 2:
        return [(xs[0] + xs[1], None), (xs[0] - xs[1], None)]
    even, odd = real_forward(xs[0::2]), real_forward(xs[1::2])
    m = n // 2
    out = [None] * (m + 1)
    for k in range(m // 2 + 1):
        if k == 0:
            out[0] = (even[0][0] + odd[0][0], None)
            out[m] = (even[0][0] - odd[0][0], None)
        elif 2 * k == m:
            out[k] = (even[k][0], -odd[k][0])
        else:
            tr, ti = c_mul(odd[k], complex(math.cos(2 * math.pi * k / n), -math.sin(2 * math.pi * k / n)))
            er, ei = even[k]
            out[k] = (er + tr, ei + ti)
            out[m - k] = (er - tr, ti - ei)
    return out


def real_backward(spec):
    n = 2 * (len(spec) - 1)
    if n == 2:
        return [spec[0][0] + spec[1][0], spec[0][0] - spec[1][0]]
    m = n // 2
    even, odd = [], []
    for k in range(m // 2 + 1):
        if k == 0:
            even.append((spec[0][0] + spec[m][0], None))
            odd.append((spec[0][0] - spec[m][0], None))
        elif 2 * k == m:
            even.append((2.0 * spec[k][0], None))
            odd.append((-2.0 * spec[k][1], None))
        else:
            ar, ai = spec[k]
            br, bi = spec[m - k]
            even.append((ar + br, ai - bi))
            odd.append(c_mul((ar - br, ai + bi), complex(math.cos(2 * math.pi * k / n), math.sin(2 * math.pi * k / n))))
    xe, xo = real_backward(even), real_backward(odd)
    out = [None] * n
    out[0::2] = xe
    out[1::2] = xo
    return out


def packed_fft(xs, sign, flip):
    n = len(xs)
    if n == 1:
        return xs
    even, odd = packed_fft(xs[0::2], sign, flip), packed_fft(xs[1::2], sign, flip)
    out = [None] * n
    for k in range(n // 2):
        t = odd[k]
        if k:
            turned = pltpu.roll(t, HALF, 1) * flip
            c, s = math.cos(2 * math.pi * k / n), sign * math.sin(2 * math.pi * k / n)
            t = (-s) * turned if 4 * k == n else c * t - s * turned
        out[k] = even[k] + t
        out[k + n // 2] = even[k] - t
    return out


def flip_lanes(rows):
    lane = lax.broadcasted_iota(jnp.int32, (rows, INNER), 1)
    return jnp.where(lane < HALF, 1.0, -1.0).astype(F32)


def row_forward_kernel(tiled, x_ref, tw_ref, f_ref, a_ref, m_ref, out_ref, y_scr, e_scr):
    def slab(g, carry):
        if tiled:
            xs = [x_ref[pl.ds(pl.multiple_of(g * 256 + a * 8, 8), 8), :] for a in range(OUTER)]
        else:
            xs = [x_ref[pl.ds(pl.multiple_of(g * 8, 8), 8), a * INNER : (a + 1) * INNER] for a in range(OUTER)]
        ys = real_forward(xs)
        rows = pl.ds(pl.multiple_of(g * 8, 8), 8)
        e_scr[0, rows, :] = ys[0][0]
        e_scr[1, rows, :] = ys[16][0]
        for k in range(1, 16):
            c = tw_ref[0, k : k + 1, :]
            s = tw_ref[1, k : k + 1, :]
            re, im = ys[k]
            base = pl.ds(pl.multiple_of((k - 1) * INNER + g * 8, 8), 8)
            y_scr[base, 0:INNER] = re * c + im * s
            y_scr[base, INNER : 2 * INNER] = im * c - re * s
        return carry

    lax.fori_loop(0, 16, slab, 0)
    out_ref[0] = data_by_table(e_scr[0], every(a_ref))
    out_ref[1] = data_by_table(e_scr[1], every(m_ref))

    def group(q, carry):
        v = data_by_table(y_scr[pl.ds(pl.multiple_of(q * 384, 8), 384), :], every(f_ref))
        for i in range(3):
            out_ref[2 + 2 * (3 * q + i)] = v[i * INNER : (i + 1) * INNER, 0:INNER]
            out_ref[3 + 2 * (3 * q + i)] = v[i * INNER : (i + 1) * INNER, INNER : 2 * INNER]
        return carry

    lax.fori_loop(0, 5, group, 0)


def row_backward_kernel(final, *refs):
    if final:
        in_ref, base_ref, tw_ref, f_ref, a_ref, m_ref, out_ref, z_scr, e_scr = refs
    else:
        in_ref, tw_ref, f_ref, a_ref, m_ref, out_ref, z_scr, e_scr = refs
    e_scr[0] = data_by_table(in_ref[0], every(a_ref))
    e_scr[1] = data_by_table(in_ref[1], every(m_ref))

    def group(q, carry):
        parts = []
        for i in range(3):
            k = 3 * q + i
            parts.append(jnp.concatenate([in_ref[2 + 2 * k], in_ref[3 + 2 * k]], axis=1))
        v = jnp.concatenate(parts, axis=0)
        z_scr[pl.ds(pl.multiple_of(q * 384, 8), 384), :] = data_by_table(v, every(f_ref))
        return carry

    lax.fori_loop(0, 5, group, 0)

    def slab(g, carry):
        rows = pl.ds(pl.multiple_of(g * 8, 8), 8)
        spec = [(e_scr[0, rows, :], None)]
        for k in range(1, 16):
            c = tw_ref[0, k : k + 1, :]
            s = tw_ref[1, k : k + 1, :]
            base = pl.ds(pl.multiple_of((k - 1) * INNER + g * 8, 8), 8)
            re = z_scr[base, 0:INNER]
            im = z_scr[base, INNER : 2 * INNER]
            spec.append((re * c - im * s, im * c + re * s))
        spec.append((e_scr[1, rows, :], None))
        xs = real_backward(spec)
        for a in range(OUTER):
            if final:
                cols = slice(a * INNER, (a + 1) * INNER)
                out_ref[rows, cols] = base_ref[rows, cols] + xs[a]
            else:
                out_ref[pl.ds(pl.multiple_of(g * 256 + a * 8, 8), 8), :] = xs[a]
        return carry

    lax.fori_loop(0, 16, slab, 0)


def column_first_step(in_ref, y_scr, sign):
    flip = flip_lanes(8)

    def slab(g, carry):
        rows = pl.ds(pl.multiple_of(g * 8, 8), 8)
        ys = packed_fft([in_ref[s, rows, :] for s in range(OUTER)], sign, flip)
        for k in range(OUTER):
            y_scr[k, rows, :] = ys[k]
        return carry

    lax.fori_loop(0, 16, slab, 0)


def apply_packed(e_ref, k1, value, flip):
    r = table_by_data([e_ref[i, k1] for i in range(e_ref.shape[0])], value)
    return r[0:INNER] - pltpu.roll(r[INNER : 2 * INNER], HALF, 1) * flip


def edge_lanes():
    lane = lax.broadcasted_iota(jnp.int32, (INNER, INNER), 1)
    return jnp.logical_or(lane == 0, lane == HALF), lane < HALF


def edge_gather(ref):
    mask, _ = edge_lanes()

    def step(k1, acc):
        return acc + pltpu.roll(jnp.where(mask, ref[k1], 0.0), k1, 1)

    return lax.fori_loop(0, OUTER, step, jnp.zeros((INNER, INNER), F32), unroll=4)


def edge_split(spec, amp):
    i = lax.broadcasted_iota(jnp.int32, (INNER, INNER), 0)
    j = lax.broadcasted_iota(jnp.int32, (INNER, INNER), 1)
    one = jnp.ones((INNER, INNER), F32)
    none = jnp.zeros((INNER, INNER), F32)
    rows = jnp.where(i + j == INNER - 1, one, none).astype(BF16)
    rows0 = jnp.where(((i + j) & (INNER - 1)) == 0, one, none).astype(BF16)
    sign = jnp.where(j < HALF, one, -one)
    col = j & (HALF - 1)
    same = (i < HALF) == (j < HALF)
    lanes = jnp.where(
        jnp.logical_and(same, jnp.logical_and(col > 0, col + (i & (HALF - 1)) == OUTER)), sign, none
    ).astype(BF16)
    lanes0 = jnp.where(jnp.logical_and(i == j, col == 0), sign, none).astype(BF16)

    def move(left, value, right):
        value = sum(mm(left, p) for p in reversed(split_into(value, 3)))
        return sum(mm(p, right) for p in reversed(split_into(value, 3)))

    rev = move(rows, spec, lanes) + move(rows0, spec, lanes0)
    swapped = pltpu.roll(amp, HALF, 1)
    _, left = edge_lanes()
    a0 = jnp.where(left, amp, swapped)
    a2 = jnp.where(left, swapped, amp)
    return 0.5 * (spec + rev), 0.5 * (spec - rev), a0, a2


def turn(c, s, value, flip):
    return c * value + s * (pltpu.roll(value, HALF, 1) * flip)


def column_first_kernel(
    scal, in_ref, amp_ref, ph_ref, edge_ref, ef, ei, out_ref, own_ref, up_ref, down_ref, y_scr, z_scr
):
    column_first_step(in_ref, y_scr, -1.0)
    flip = flip_lanes(INNER)

    def step(k1, carry):
        value = apply_packed(ef, k1, y_scr[k1], flip)
        amp = amp_ref[k1]
        once = value * amp
        twice = once * amp
        y_scr[k1] = value
        z_scr[k1] = scal[0] * once
        own_ref[k1] = scal[3] * twice
        for n, ref, gain in ((0, up_ref, scal[1]), (1, down_ref, scal[2])):
            cb = ph_ref[2 * n]
            sb = ph_ref[2 * n + 1]
            ca = scal[8 + 64 * n + k1] * gain
            sa = scal[8 + 64 * n + 32 + k1] * gain
            ref[k1] = turn(cb * ca - sb * sa, sb * ca + cb * sa, twice, flip).astype(BF16)
        return carry

    lax.fori_loop(0, OUTER, step, 0, unroll=4)

    @pl.when(scal[6] > 0.5)
    def _():
        u0, u2, a0, a2 = edge_split(edge_gather(y_scr), edge_gather(amp_ref))
        mask, _ = edge_lanes()
        e0 = a0 * u0
        e2 = a2 * u2
        fixed = [scal[0] * (e0 + e2)]
        e0 = a0 * e0
        e2 = a2 * e2
        fixed.append(scal[3] * (e0 + e2))
        fixed.append(scal[1] * turn(edge_ref[0], edge_ref[1], e0 + scal[4] * e2, flip))
        fixed.append(scal[2] * turn(edge_ref[2], edge_ref[3], e0 + scal[5] * e2, flip))

        def put(k1, carry):
            back = lax.rem(INNER - k1, INNER)
            for ref, value in zip((z_scr, own_ref, up_ref, down_ref), fixed):
                value = jnp.where(mask, pltpu.roll(value, back, 1), ref[k1].astype(F32))
                ref[k1] = value.astype(ref.dtype)
            return carry

        lax.fori_loop(0, OUTER, put, 0)

    def inverse(k1, carry):
        z_scr[k1] = apply_packed(ei, k1, z_scr[k1], flip)
        return carry

    lax.fori_loop(0, OUTER, inverse, 0, unroll=4)
    column_first_step(z_scr, out_ref, 1.0)


def column_second_kernel(scal, in_ref, amp_ref, own_ref, prev_ref, next_ref, ef, ei, out_ref, y_scr, z_scr):
    column_first_step(in_ref, y_scr, -1.0)
    flip = flip_lanes(INNER)

    def step(k1, carry):
        value = apply_packed(ef, k1, y_scr[k1], flip)
        moved = prev_ref[k1].astype(F32) + next_ref[k1].astype(F32)
        y_scr[k1] = value
        z_scr[k1] = scal[0] * (value * amp_ref[k1] - moved) + own_ref[k1]
        return carry

    lax.fori_loop(0, OUTER, step, 0, unroll=4)

    @pl.when(scal[6] > 0.5)
    def _():
        spec = edge_gather(y_scr)
        amp = edge_gather(amp_ref)
        u0, u2, a0, a2 = edge_split(spec, amp)
        mask, _ = edge_lanes()
        change = scal[0] * (a0 * u0 + a2 * u2 - amp * spec)

        def put(k1, carry):
            back = lax.rem(INNER - k1, INNER)
            z_scr[k1] = z_scr[k1] + jnp.where(mask, pltpu.roll(change, back, 1), 0.0)
            return carry

        lax.fori_loop(0, OUTER, put, 0)

    def inverse(k1, carry):
        z_scr[k1] = apply_packed(ei, k1, z_scr[k1], flip)
        return carry

    lax.fori_loop(0, OUTER, inverse, 0, unroll=4)
    column_first_step(z_scr, out_ref, 1.0)


def route_kernel(t_ref, id_ref, slot_ref, idp_ref, cnt_ref):
    row = lax.broadcasted_iota(jnp.int32, (INNER, 2 * INNER), 0)
    col = lax.broadcasted_iota(jnp.int32, (INNER, 2 * INNER), 1)
    tri = jnp.where(jnp.logical_or(row < col, col >= INNER), 1.0, 0.0).astype(BF16)
    peer = lax.broadcasted_iota(jnp.int32, (PEERS, INNER), 0)
    base = jnp.zeros((PEERS, INNER), F32)
    for i in range(0, POINT_ROWS, 8):
        hots = [jnp.where(peer == t_ref[i + j : i + j + 1, :], 1.0, 0.0) for j in range(8)]
        cum = mm(jnp.concatenate(hots, axis=0).astype(BF16), tri)
        for j in range(8):
            part = cum[j * PEERS : (j + 1) * PEERS]
            pos = jnp.sum(hots[j] * (part[:, 0:INNER] + base), axis=0, keepdims=True)
            base = base + part[:, INNER : 2 * INNER]
            slot_ref[i + j : i + j + 1, :] = t_ref[i + j : i + j + 1, :] * SLOTS + pos.astype(jnp.int32)
    cnt_ref[...] = base.astype(jnp.int32)
    ids = id_ref[...]
    r = lax.shift_right_logical(ids, 5)
    idp_ref[...] = lax.shift_right_logical(r, 3) * 256 + (ids & 31) * 8 + (r & 7)


def pack_kernel(slot_ref, idp_ref, cnt_ref, w_ref, out_ref, sid_ref, w_scr, buf):
    def clear(i, carry):
        rows = pl.ds(pl.multiple_of(i * 64, 64), 64)
        buf[rows, :] = jnp.zeros((64, INNER), F32)
        buf[pl.ds(pl.multiple_of(i * 64 + PEERS * SLOTS // 2, 64), 64), :] = jnp.zeros((64, INNER), F32)
        w_scr[rows, :] = w_ref[rows, :].astype(F32)
        return carry

    lax.fori_loop(0, PEERS * SLOTS // INNER, clear, 0)

    def some(q, carry):
        first = q * 16
        slots = [slot_ref[first + j] for j in range(16)]
        ids = [idp_ref[first + j] for j in range(16)]
        rows = [w_scr[pl.ds(first + j, 1), :] for j in range(16)]
        for j in range(16):
            buf[pl.ds(slots[j], 1), :] = rows[j]
        for j in range(16):
            sid_ref[slots[j]] = ids[j]
        return carry

    lax.fori_loop(0, POINT_ROWS * INNER // 16, some, 0)

    def tag(d, carry):
        sid_ref[d * SLOTS] = (sid_ref[d * SLOTS] & 4095) | (cnt_ref[d, 0] * 4096)
        return carry

    lax.fori_loop(0, PEERS, tag, 0)

    def narrow(i, carry):
        rows = pl.ds(pl.multiple_of(i * INNER, INNER), INNER)
        out_ref[rows, :] = buf[rows, :].astype(BF16)
        return carry

    lax.fori_loop(0, PEERS * SLOTS // INNER, narrow, 0)


def gather_kernel(sid_ref, cnt_ref, tiles_ref, w_ref, out_ref, g_scr):
    g_scr[...] = jnp.zeros_like(g_scr)
    ones = jnp.ones((8, INNER), BF16)

    def source(s, carry):
        def some(q, inner):
            first = s * SLOTS + q * 16
            ids = [sid_ref[first + j] for j in range(16)]
            rows = [tiles_ref[pl.ds(ids[j], 1), :] for j in range(16)]
            for j in range(16):
                g_scr[pl.ds(q * 16 + j, 1), :] = rows[j]
            return inner

        lax.fori_loop(0, lax.shift_right_logical(cnt_ref[s] + 15, 4), some, 0)
        w = w_ref[pl.ds(pl.multiple_of(s * SLOTS, SLOTS), SLOTS), :].astype(F32)
        high, low = split(g_scr[...] * w)
        phase = mm_nt(ones, high) + mm_nt(ones, low)
        for q in range(4):
            out_ref[pl.ds(s * 4 + q, 1), :] = phase[0:1, q * INNER : (q + 1) * INNER]
        return carry

    lax.fori_loop(0, PEERS, source, 0)


def residual_kernel(slot_ref, prec_ref, phase_ref, out_ref, p_scr):
    high, low = split(phase_ref[...])
    table = jnp.concatenate([high, low], axis=0)
    batch = 4
    index = lax.broadcasted_iota(jnp.int32, (INNER, batch * INNER), 0)

    def wide(ref, i):
        return jnp.concatenate([ref[pl.ds(i * batch + j, 1), :] for j in range(batch)], axis=1)

    def pick(i, carry):
        slot = wide(slot_ref, i)
        hot = jnp.where(index == (slot & 127), 1.0, 0.0).astype(BF16)
        v = mm(table, hot)
        v = v[0:INNER] + v[INNER : 2 * INNER]
        got = jnp.sum(jnp.where(index == lax.shift_right_logical(slot, 7), v, 0.0), axis=0, keepdims=True)
        for j in range(batch):
            p_scr[pl.ds(i * batch + j, 1), :] = got[:, j * INNER : (j + 1) * INNER]
        return carry

    lax.fori_loop(0, POINT_ROWS // batch, pick, 0, unroll=2)
    row = lax.broadcasted_iota(jnp.int32, (INNER, INNER), 0)
    lane = lax.broadcasted_iota(jnp.int32, (INNER, INNER), 1)
    same = jnp.where((row < HALF) == (lane < HALF), 1.0, 0.0).astype(BF16)
    prec = prec_ref[...]
    phase = p_scr[...]

    def total(value):
        return sum(mm(p, same) for p in reversed(split_into(value, 3)))

    p_scr[...] = prec * (phase - total(prec * phase) / total(prec))

    def put(i, acc):
        slot = wide(slot_ref, i)
        hot = jnp.where(index == (slot & 127), 1.0, 0.0).astype(BF16)
        v = jnp.where(index == lax.shift_right_logical(slot, 7), wide(p_scr, i), 0.0)
        vh, vl = split(v)
        return acc + mm_nt(jnp.concatenate([vh, vl], axis=0), hot)

    acc = lax.fori_loop(0, POINT_ROWS // batch, put, jnp.zeros((2 * INNER, INNER), F32), unroll=2)
    out_ref[...] = acc[0:INNER] + acc[INNER : 2 * INNER]


COPIES = 8


def scatter_kernel(sid_ref, cnt_ref, r_ref, w_ref, out_ref, rt_scr, u_scr, *accs):
    def clear(i, carry):
        rows = pl.ds(pl.multiple_of(i * 64, 64), 64)
        for acc in accs:
            acc[rows, :] = jnp.zeros((64, INNER), F32)
        return carry

    lax.fori_loop(0, SIDE // 64, clear, 0)
    rt_scr[...] = r_ref[...].T
    lane = lax.broadcasted_iota(jnp.int32, (INNER, INNER), 1)

    def source(s, carry):
        for q in range(4):
            col = jnp.sum(jnp.where(lane == s * 4 + q, rt_scr[...], 0.0), axis=1, keepdims=True)
            base = pl.multiple_of(s * SLOTS + q * INNER, INNER)
            u_scr[q * INNER : (q + 1) * INNER, :] = w_ref[pl.ds(base, INNER), :].astype(F32) * col

        def some(q, inner):
            first = s * SLOTS + q * 16
            ids = [sid_ref[first + j] for j in range(16)]
            us = [u_scr[pl.ds(q * 16 + j, 1), :] for j in range(16)]
            for h in range(0, 16, COPIES):
                sums = [accs[j][pl.ds(ids[h + j], 1), :] + us[h + j] for j in range(COPIES)]
                for j in range(COPIES):
                    accs[j][pl.ds(ids[h + j], 1), :] = sums[j]
            return inner

        lax.fori_loop(0, lax.shift_right_logical(cnt_ref[s] + 15, 4), some, 0)
        return carry

    lax.fori_loop(0, PEERS, source, 0)

    def add(i, carry):
        rows = pl.ds(pl.multiple_of(i * 64, 64), 64)
        total = accs[0][rows, :]
        for acc in accs[1:]:
            total = total + acc[rows, :]
        out_ref[rows, :] = total
        return carry

    lax.fori_loop(0, SIDE // 64, add, 0)


def call(kernel, name, out_shapes, args, smem=0, smem_outs=(), scratch=()):
    vmem = pl.BlockSpec(memory_space=pltpu.VMEM)
    small = pl.BlockSpec(memory_space=pltpu.SMEM)
    outs = [small if i in smem_outs else vmem for i in range(len(out_shapes))]
    result = pl.pallas_call(
        kernel,
        out_shape=out_shapes,
        in_specs=[small] * smem + [vmem] * (len(args) - smem),
        out_specs=outs,
        scratch_shapes=list(scratch),
        compiler_params=pltpu.CompilerParams(vmem_limit_bytes=VMEM_BYTES),
        cost_estimate=pl.CostEstimate(flops=1024, bytes_accessed=1024, transcendentals=0),
        name=name,
    )(*args)
    return result


def shape(dims, dtype=F32):
    return jax.ShapeDtypeStruct(dims, dtype)


PENCILS = (PEERS, INNER, INNER)


def row_forward(x, tables, tiled):
    args = [x] + tables
    return call(
        lambda *refs: row_forward_kernel(tiled, *refs),
        "row_forward",
        [shape(PENCILS)],
        args,
        scratch=[pltpu.VMEM((15 * INNER, 2 * INNER), F32), pltpu.VMEM((2, INNER, INNER), F32)],
    )[0]


def row_backward(pencils, base, tables):
    final = base is not None
    args = [pencils] + ([base] if final else []) + tables
    return call(
        lambda *refs: row_backward_kernel(final, *refs),
        "row_backward",
        [shape((INNER, SIDE) if final else (SIDE, INNER))],
        args,
        scratch=[pltpu.VMEM((15 * INNER, 2 * INNER), F32), pltpu.VMEM((2, INNER, INNER), F32)],
    )[0]


def exchange(value):
    return lax.all_to_all(value, "strip", split_axis=0, concat_axis=0, tiled=True)


def amplitude_table(strip):
    j = jnp.arange(HALF, dtype=jnp.int32)
    k1 = strip // 2
    fold = jnp.where(strip % 2 == 0, k1 + OUTER * j, OUTER - k1 + OUTER * j)
    fold = jnp.where(strip == 1, 16 + OUTER * j, fold)
    edge = jnp.where((strip == 0) & (j == 0), SIDE // 2, fold)
    cols = jnp.concatenate([fold, edge]).astype(F32)[None, None, :]
    kr = jnp.arange(OUTER, dtype=jnp.int32)[:, None] + OUTER * jnp.arange(INNER, dtype=jnp.int32)[None, :]
    rows = jnp.minimum(kr, SIDE - kr).astype(F32)[:, :, None]
    radius = (rows * rows + cols * cols) / (KZERO * KZERO)
    return SIDE / (2.0 * KZERO) * jnp.power(1.0 + radius, -11.0 / 12.0)


def signed_columns(strip):
    j = jnp.arange(HALF, dtype=jnp.int32)
    k1 = strip // 2
    cols = jnp.where(strip % 2 == 0, k1 + OUTER * j, k1 + OUTER * (INNER - 1 - j))
    cols = jnp.where(strip == 1, 16 + OUTER * j, cols)
    return jnp.concatenate([cols, cols])


def phase_tables(wind_row, wind_col, strip, sign):
    unit = 2.0 * math.pi / SIDE
    k2 = jnp.arange(INNER, dtype=jnp.int32)[:, None]
    turn = (OUTER * k2 * wind_row + signed_columns(strip)[None, :] * wind_col) % SIDE
    angle = turn.astype(F32) * unit
    small = ((jnp.arange(OUTER, dtype=jnp.int32) * wind_row) % SIDE).astype(F32) * unit
    return jnp.cos(angle), sign * jnp.sin(angle), jnp.cos(small), sign * jnp.sin(small)


def edge_tables(wind_row, sign):
    k1 = jnp.arange(INNER, dtype=jnp.int32)[None, :] % HALF
    kr = k1 + OUTER * jnp.arange(INNER, dtype=jnp.int32)[:, None]
    angle = ((kr * wind_row) % SIDE).astype(F32) * (2.0 * math.pi / SIDE)
    return [jnp.cos(angle), sign * jnp.sin(angle)]


def const(*tables):
    return [jnp.asarray(t) for t in tables]


def local(
    screen_vec,
    prior_scale,
    flow_weight,
    wind,
    pierce_point_strip,
    pierce_block,
    pierce_weights,
    noise_prec,
):
    strip = lax.axis_index("strip")
    slot = lax.axis_index("tm")
    fwd, inv, first, first_inv, mid, mid_inv, twiddle = row_tables()
    row_fwd_tables = const(twiddle, pieces(fwd, 2), pieces(first, 2), pieces(mid, 2))
    row_fine_tables = const(twiddle, pieces(fwd, 3), pieces(first, 3), pieces(mid, 3))
    row_inv_tables = const(twiddle, pieces(inv, 2), pieces(first_inv, 2), pieces(mid_inv, 2))
    col_fwd, col_inv = column_tables()
    col_fine_tables = const(pieces(col_fwd, 3), pieces(col_inv, 2))
    col_tables = const(pieces(col_fwd, 2), pieces(col_inv, 2))

    x = screen_vec[0]
    scale = prior_scale[0]
    weights = pierce_weights[0].reshape(POINT_ROWS * INNER, INNER)
    target = pierce_point_strip.reshape(POINT_ROWS, INNER)
    block = pierce_block.reshape(POINT_ROWS, INNER)
    prec = noise_prec.reshape(POINT_ROWS, INNER)

    last = lax.axis_size("tm") - 1
    rate = flow_weight[0] * (slot < last).astype(F32)
    mine = jnp.stack([rate, wind[0, 0].astype(F32), wind[0, 1].astype(F32)])
    up_pairs = [(i, i + 1) for i in range(last)]
    down_pairs = [(i + 1, i) for i in range(last)]
    prior = lax.ppermute(mine, "tm", up_pairs)
    back_row, back_col = prior[1].astype(jnp.int32), prior[2].astype(jnp.int32)
    cu, su, cua, sua = phase_tables(wind[0, 0], wind[0, 1], strip, 1.0)
    cd, sd, cda, sda = phase_tables(back_row, back_col, strip, -1.0)
    phases = jnp.stack([cu, su, cd, sd])
    edge_phases = jnp.stack(edge_tables(wind[0, 0], 1.0) + edge_tables(back_row, -1.0))
    norm = scale / (SIDE * SIDE)
    parity_up = jnp.where(wind[0, 1] % 2 == 0, 1.0, -1.0)
    parity_down = jnp.where(back_col % 2 == 0, 1.0, -1.0)
    head = jnp.stack(
        [
            norm,
            rate * scale,
            prior[0] * scale,
            (rate + prior[0]) * scale * norm,
            parity_up,
            parity_down,
            (strip == 0).astype(F32),
            jnp.zeros((), F32),
        ]
    )
    scal = jnp.concatenate([head, cua, sua, cda, sda])
    amp = amplitude_table(strip)

    slots, ids, counts = call(
        route_kernel,
        "route",
        [shape((POINT_ROWS, INNER), jnp.int32)] * 2 + [shape((PEERS, INNER), jnp.int32)],
        [target, block],
    )
    sent, sent_ids = call(
        pack_kernel,
        "pack",
        [shape((PEERS * SLOTS, INNER), BF16), shape((PEERS * SLOTS,), jnp.int32)],
        [slots.reshape(-1), ids.reshape(-1), counts, weights],
        smem=3,
        smem_outs=(1,),
        scratch=[pltpu.VMEM((POINT_ROWS * INNER, INNER), F32), pltpu.VMEM((PEERS * SLOTS, INNER), F32)],
    )
    pencils = exchange(row_forward(x, row_fine_tables, False))
    here = exchange(sent.reshape(PEERS, SLOTS, INNER)).reshape(PEERS * SLOTS, INNER)
    tagged = exchange(sent_ids.reshape(PEERS, 4, INNER))
    here_counts = lax.shift_right_logical(tagged[:, 0, 0], 12)
    here_ids = (tagged & 4095).reshape(PEERS * SLOTS)

    spectral = [pltpu.VMEM(PENCILS, F32), pltpu.VMEM(PENCILS, F32)]
    screen_pencils, own, up, down = call(
        column_first_kernel,
        "column_first",
        [shape(PENCILS), shape(PENCILS), shape(PENCILS, BF16), shape(PENCILS, BF16)],
        [scal, pencils, amp, phases, edge_phases] + col_fine_tables,
        smem=1,
        scratch=spectral,
    )
    from_prev = lax.ppermute(up, "tm", up_pairs)
    from_next = lax.ppermute(down, "tm", down_pairs)
    tiles = row_backward(exchange(screen_pencils), None, row_inv_tables)

    phase = call(
        gather_kernel,
        "gather",
        [shape((INNER, INNER))],
        [here_ids, here_counts, tiles, here],
        smem=2,
        scratch=[pltpu.VMEM((SLOTS, INNER), F32)],
    )[0]
    returned = exchange(phase.reshape(PEERS, 4, INNER)).reshape(INNER, INNER)
    resid = call(
        residual_kernel,
        "residual",
        [shape((INNER, INNER))],
        [slots, prec, returned],
        scratch=[pltpu.VMEM((POINT_ROWS, INNER), F32)],
    )[0]
    resid_here = exchange(resid.reshape(PEERS, 4, INNER)).reshape(INNER, INNER)
    gradient = call(
        scatter_kernel,
        "scatter",
        [shape((SIDE, INNER))],
        [here_ids, here_counts, resid_here, here],
        smem=2,
        scratch=[pltpu.VMEM((INNER, INNER), F32), pltpu.VMEM((SLOTS, INNER), F32)]
        + [pltpu.VMEM((SIDE, INNER), F32)] * COPIES,
    )[0]
    pencils = exchange(row_forward(gradient, row_fwd_tables, True))
    out_pencils = call(
        column_second_kernel,
        "column_second",
        [shape(PENCILS)],
        [scal, pencils, amp, own, from_prev, from_next] + col_tables,
        smem=1,
        scratch=spectral,
    )[0]
    return row_backward(exchange(out_pencils), x, row_inv_tables)[None]


def solution(mesh):
    in_specs = (
        P("tm", "strip", None),
        P("tm"),
        P("tm"),
        P("tm", None),
        P("tm", "strip", None, None),
        P("tm", "strip", None),
        P("tm", "strip", None, None),
        P("tm", "strip", None),
    )
    out_specs = P("tm", "strip", None)
    return jax.shard_map(local, mesh=mesh, in_specs=in_specs, out_specs=out_specs, check_vma=False)
```

time: 879 us -> 411 us (0.47); the launches traced: 863 us -> 410 us
  local copies, waits for them, and re-layouts: 286 us -> 7.32 us
  matrix products: 213 us -> 0 us
  Pallas kernels: 0 us -> 148 us
  other arithmetic: 146 us -> 9.31 us
  blocking collectives: 0 us -> 77.6 us
  starting transfers between devices: 119 us -> 78.4 us
  waiting for transfers between devices: 91.3 us -> 81.2 us
    dot_general x58 -> x0, matrix products: 213 us -> none  [the longest x16 60.3 us: complex_einsum(): jnp.einsum(form, left_re, right_re, precision=EXACT_MODE)]
    pallas_call x0 -> x11, Pallas kernels: none -> 148 us  [call(): pl.pallas_call(kernel, out_shape=out_shapes, in_specs=[small] * smem + [v...]
    gather x2 -> x0, local copies, waits for them, and re-layouts: 119 us -> none  [the longest x1 65 us: misfit(): phase_own = returned[target, position].reshape(antennas, directions)]
    scatter-add x1 -> x0, other arithmetic: 102 us -> none  [misfit(): jnp.zeros_like(tiles).at[flat_ids]]
    unnamed x62 -> x17, local copies, waits for them, and re-layouts: 90 us -> 2.57 us
    all_to_all x0 -> x3, blocking collectives: none -> 77.6 us  [exchange(): lax.all_to_all(value, 'strip', split_axis=0, concat_axis=0, tiled=True)]
    all_to_all x12 -> x5, waiting for transfers between devices: 91.3 us -> 53 us  [exchange(): lax.all_to_all(value, 'strip', split_axis=0, concat_axis=0, tiled=True)]
    all_to_all x12 -> x5, starting transfers between devices: 94.6 us -> 66 us  [exchange(): lax.all_to_all(value, 'strip', split_axis=0, concat_axis=0, tiled=True)]
  transfers between devices with their start and end apart: 18 -> 8, of which waited for: 7 -> 3; matrix products, arithmetic and copies ran while one was open for 61% -> 3% of each run, Pallas kernels for 0% -> 16%
where the time goes in v1:
time: 411 us; the launch traced here: 410 us
  Pallas kernels  148 us (36%)
  waiting for transfers between devices  81.2 us (20%)
  starting transfers between devices  78.4 us (19%)
  blocking collectives  77.6 us (19%)
  other arithmetic  9.31 us (2%)
  between operations  8.07 us (2%)
  local copies, waits for them, and re-layouts  7.32 us (2%)
    pallas_call x11, Pallas kernels, call(): pl.pallas_call(kernel, out_shape=out_shapes, in_specs=[small] * smem + [v...  148 us
    all_to_all x3, blocking collectives, exchange(): lax.all_to_all(value, 'strip', split_axis=0, concat_axis=0, tiled=True)  77.6 us
    all_to_all x5, starting transfers between devices, exchange(): lax.all_to_all(value, 'strip', split_axis=0, concat_axis=0, tiled=True)  66 us
    all_to_all x5, waiting for transfers between devices, exchange(): lax.all_to_all(value, 'strip', split_axis=0, concat_axis=0, tiled=True)  53 us
    ppermute x1, waiting for transfers between devices, local(): from_prev = lax.ppermute(up, 'tm', up_pairs)  28.2 us
  transfers between devices with their start and end apart: 8, of which 3 were waited for; matrix products, arithmetic and copies ran while one was open for 3% of the time, Pallas kernels for 16%

profile of v1, /device:TPU:1, one launch (start us, length us, event | category | flops | bytes accessed | tf_op | source)
XLA Modules:
  0.0 410.1 jit_solution(13366668336513491067)
XLA Ops:
  3.4 4.9 %collective-permute-start = (f32[3]{0:T(128)S(1)}, f32[3]{0:T(128)S(1)}, u32[]{:S(2)}, u32[]{:S(2)}) collective-permute-start(f32[3]{0:T(128)S(1)} %pad_maximum_fusion.2), channel_id=1, source_target_pairs={{0,32},{32,64},{64,96},{1,33},{33,65},{65,97},{2,34},{34,66},{66,9... | collective-permute-start | bytes 44 | tf_op jit(solution)/shard_map/ppermute | solution.py:722
  8.3 6.5 %row_forward.2 = f32[32,128,128]{2,1,0:T(8,128)} custom-call(f32[128,4096]{1,0:T(8,128)} %bitcast.39, f32[2,16,128]{2,1,0:T(8,128)} %constant.179.clone.refs_1_.refs_2_, bf16[3,256,256]{2,1,0:T(8,128)(2,1)} %constant.183.clone.refs_2_, bf16[3,128,128]{2,1,0:T(8,128)(2,1)} %constant.184.clone.refs_3_, bf16[3,128,128]{2,1,0:T(8,128)(2,1)} %constant.185.clone.refs_4_), custom_call_target="tpu_custom_call" | custom-call | flops 1024 | bytes 1024 | tf_op jit(solution)/shard_map/row_forward/pallas_call | solution.py:602
  14.9 10.2 %all-to-all-start.1 = ((f32[32,128,128]{2,1,0:T(8,128)}), f32[32,128,128]{2,1,0:T(8,128)S(1)}, u32[]{:S(2)}, u32[]{:S(2)}) async-start(f32[32,128,128]{2,1,0:T(8,128)} %row_forward.2), calls=%async_computation.1 | async-start | bytes 4194304 | tf_op jit(solution)/shard_map/all_to_all | solution.py:646
  29.4 20.6 %pack.1 = (bf16[16384,128]{1,0:T(8,128)(2,1)}, s32[16384]{0:T(1024)}) custom-call(s32[8192]{0:T(1024)} %bitcast.49, s32[8192]{0:T(1024)} %bitcast.50, s32[32,128]{1,0:T(8,128)} %get-tuple-element.16.cnt_ref, bf16[8192,128]{1,0:T(8,128)(2,1)} %bitcast.42), custom_call_target="tpu_custom_call" | custom-call | flops 1024 | bytes 1024 | tf_op jit(solution)/shard_map/pack/pallas_call | solution.py:602
  53.3 2.4 power_multiply_fusion.amp_ref
  63.1 9.3 %all-to-all-start = ((s32[32,4,128]{2,1,0:T(4,128)}), s32[32,4,128]{2,1,0:T(4,128)S(1)}, u32[]{:S(2)}, u32[]{:S(2)}) async-start(s32[32,4,128]{2,1,0:T(4,128)} %bitcast.20), calls=%async_computation | async-start | bytes 131072 | tf_op jit(solution)/shard_map/all_to_all | solution.py:646
  73.1 32.5 %column_first.1 = (f32[32,128,128]{2,1,0:T(8,128)}, f32[32,128,128]{2,1,0:T(8,128)}, bf16[32,128,128]{2,1,0:T(8,128)(2,1)}, bf16[32,128,128]{2,1,0:T(8,128)(2,1)}) custom-call(f32[136]{0:T(256)} %concatenate.22.scal, f32[32,128,128]{2,1,0:T(8,128)} %copy-done.1, f32[32,128,128]{2,1,0:T(8,128)} %power_multiply_fusion.amp_ref, ...), custom_call_target="tpu_custom_call" | custom-call | flops 1024 | bytes 1024 | tf_op jit(solution)/shard_map/column_first/pallas_call | solution.py:602
  105.6 34.3 %all_to_all.40.refs_0_ = f32[32,128,128]{2,1,0:T(8,128)} all-to-all(f32[32,128,128]{2,1,0:T(8,128)} %get-tuple-element.18), channel_id=1, replica_groups=mesh['tm'=4,'strip'=32] {'strip'}, dimensions={0} | all-to-all | bytes 4194304 | tf_op jit(solution)/shard_map/all_to_all | solution.py:646
  139.9 6.5 %all-to-all-start.3 = ((bf16[32,512,128]{2,1,0:T(8,128)(2,1)}), bf16[32,512,128]{2,1,0:T(8,128)(2,1)}, u32[]{:S(2)}, u32[]{:S(2)}) async-start(bf16[32,512,128]{2,1,0:T(8,128)(2,1)} %bitcast.41), calls=%async_computation.3 | async-start | bytes 8388608 | tf_op jit(solution)/shard_map/all_to_all | solution.py:646
  148.2 5.7 %row_backward.2.tiles_ref = f32[4096,128]{1,0:T(8,128)} custom-call(f32[32,128,128]{2,1,0:T(8,128)} %all_to_all.40.refs_0_, f32[2,16,128]{2,1,0:T(8,128)} %constant.179.clone.refs_1_.refs_2_, bf16[2,256,256]{2,1,0:T(8,128)(2,1)} %constant.186.clone.refs_2_.refs_3_, bf16[2,128,128]{2,1,0:T(8,128)(2,1)} %constant.187.clone.refs_3_.refs_4_, ...), custom_call_target="tpu_custom_call" | custom-call | flops 1024 | bytes 1024 | tf_op jit(solution)/shard_map/row_backward/pallas_call | solution.py:602
  153.9 44.9 %all-to-all-done.3 = bf16[32,512,128]{2,1,0:T(8,128)(2,1)} async-done(((bf16[32,512,128]{2,1,0:T(8,128)(2,1)}), bf16[32,512,128]{2,1,0:T(8,128)(2,1)}, u32[]{:S(2)}, u32[]{:S(2)}) %all-to-all-start.3) | async-done | bytes 4194336 | tf_op jit(solution)/shard_map/all_to_all | solution.py:646
  198.9 15.6 %gather.1 = f32[128,128]{1,0:T(8,128)} custom-call(s32[16384]{0:T(1024)} %bitcast.43, s32[32]{0:T(128)} %fusion.22.cnt_ref, f32[4096,128]{1,0:T(8,128)} %row_backward.2.tiles_ref, bf16[16384,128]{1,0:T(8,128)(2,1)} %bitcast.24.w_ref), custom_call_target="tpu_custom_call" | custom-call | flops 1024 | bytes 1024 | tf_op jit(solution)/shard_map/gather/pallas_call | solution.py:602
  214.4 22.9 %all-to-all-start.4 = ((f32[32,4,128]{2,1,0:T(4,128)}), f32[32,4,128]{2,1,0:T(4,128)S(1)}, u32[]{:S(2)}, u32[]{:S(2)}) async-start(f32[32,4,128]{2,1,0:T(4,128)} %bitcast.45), calls=%async_computation.4 | async-start | bytes 131072 | tf_op jit(solution)/shard_map/all_to_all | solution.py:646
  238.1 8.1 %all-to-all-done.4 = f32[32,4,128]{2,1,0:T(4,128)S(1)} async-done(((f32[32,4,128]{2,1,0:T(4,128)}), f32[32,4,128]{2,1,0:T(4,128)S(1)}, u32[]{:S(2)}, u32[]{:S(2)}) %all-to-all-start.4) | async-done | bytes 65568 | tf_op jit(solution)/shard_map/all_to_all | solution.py:646
  246.8 6.9 %residual.1 = f32[128,128]{1,0:T(8,128)} custom-call(s32[64,128]{1,0:T(8,128)} %get-tuple-element.14.slot_ref, f32[64,128]{1,0:T(8,128)} %reshape.670.prec_ref, f32[128,128]{1,0:T(8,128)} %bitcast.47), custom_call_target="tpu_custom_call" | custom-call | flops 1024 | bytes 1024 | tf_op jit(solution)/shard_map/residual/pallas_call | solution.py:602
  253.7 13.2 %all_to_all.41 = f32[32,4,128]{2,1,0:T(4,128)} all-to-all(f32[32,4,128]{2,1,0:T(4,128)} %bitcast.48), channel_id=1, replica_groups=mesh['tm'=4,'strip'=32] {'strip'}, dimensions={0} | all-to-all | bytes 131072 | tf_op jit(solution)/shard_map/all_to_all | solution.py:646
  266.9 17.7 %scatter.1.refs_0_ = f32[4096,128]{1,0:T(8,128)} custom-call(s32[16384]{0:T(1024)} %bitcast.44, s32[32]{0:T(128)} %fusion.22.cnt_ref, f32[128,128]{1,0:T(8,128)} %bitcast.46, bf16[16384,128]{1,0:T(8,128)(2,1)} %bitcast.24.w_ref), custom_call_target="tpu_custom_call" | custom-call | flops 1024 | bytes 1024 | tf_op jit(solution)/shard_map/scatter/pallas_call | solution.py:602
  284.6 5.7 %row_forward.3 = f32[32,128,128]{2,1,0:T(8,128)} custom-call(f32[4096,128]{1,0:T(8,128)} %scatter.1.refs_0_, f32[2,16,128]{2,1,0:T(8,128)} %constant.179.clone.refs_1_.refs_2_, bf16[2,256,256]{2,1,0:T(8,128)(2,1)} %constant.180.clone.refs_2_, bf16[2,128,128]{2,1,0:T(8,128)(2,1)} %constant.181.clone.refs_3_, bf16[2,128,128]{2,1,0:T(8,128)(2,1)} %constant.182.clone.refs_4_), custom_call_target="tpu_custom_call" | custom-call | flops 1024 | bytes 1024 | tf_op jit(solution)/shard_map/row_forward/pallas_call | solution.py:602
  290.2 17.1 %all-to-all-start.6 = ((f32[32,128,128]{2,1,0:T(8,128)}), f32[32,128,128]{2,1,0:T(8,128)S(1)}, u32[]{:S(2)}, u32[]{:S(2)}) async-start(f32[32,128,128]{2,1,0:T(8,128)} %row_forward.3), calls=%async_computation.6 | async-start | bytes 4194304 | tf_op jit(solution)/shard_map/all_to_all | solution.py:646
  309.3 5.6 %collective-permute-start.2 = (bf16[32,128,128]{2,1,0:T(8,128)(2,1)}, bf16[32,128,128]{2,1,0:T(8,128)(2,1)}, u32[]{:S(2)}, u32[]{:S(2)}) collective-permute-start(bf16[32,128,128]{2,1,0:T(8,128)(2,1)} %get-tuple-element.22), channel_id=1, source_target_pairs={{32,0},{64,32},{96,64},{33,1},{65,33},{97,65},{34,2},{66,34},{98,6... | collective-permute-start | bytes 3145736 | tf_op jit(solution)/shard_map/ppermute | solution.py:777
  314.9 28.2 %collective-permute-done.1.prev_ref = bf16[32,128,128]{2,1,0:T(8,128)(2,1)S(1)} collective-permute-done((bf16[32,128,128]{2,1,0:T(8,128)(2,1)}, bf16[32,128,128]{2,1,0:T(8,128)(2,1)S(1)}, u32[]{:S(2)}, u32[]{:S(2)}) %collective-permute-start.1) | collective-permute-done | bytes 1048608 | tf_op jit(solution)/shard_map/ppermute | solution.py:776
  344.7 28.8 %column_second.1 = f32[32,128,128]{2,1,0:T(8,128)} custom-call(f32[136]{0:T(256)} %concatenate.22.scal, f32[32,128,128]{2,1,0:T(8,128)} %copy-done, f32[32,128,128]{2,1,0:T(8,128)} %power_multiply_fusion.amp_ref, f32[32,128,128]{2,1,0:T(8,128)} %get-tuple-element.20.own_ref, bf16[32,128,128]{2,1,0:T(8,128)(2,1)} %copy-done.2, ...), custom_call_target="tpu_custom_call" | custom-call | flops 1024 | bytes 1024 | tf_op jit(solution)/shard_map/column_second/pallas_call | solution.py:602
  373.5 30.1 %all_to_all.42.refs_0_ = f32[32,128,128]{2,1,0:T(8,128)} all-to-all(f32[32,128,128]{2,1,0:T(8,128)} %column_second.1), channel_id=1, replica_groups=mesh['tm'=4,'strip'=32] {'strip'}, dimensions={0} | all-to-all | bytes 4194304 | tf_op jit(solution)/shard_map/all_to_all | solution.py:646
  403.7 6.4 %row_backward.3 = f32[128,4096]{1,0:T(8,128)} custom-call(f32[32,128,128]{2,1,0:T(8,128)} %all_to_all.42.refs_0_, f32[128,4096]{1,0:T(8,128)} %bitcast.40, f32[2,16,128]{2,1,0:T(8,128)} %constant.179.clone.refs_1_.refs_2_, bf16[2,256,256]{2,1,0:T(8,128)(2,1)} %constant.186.clone.refs_2_.refs_3_, bf16[2,128,128]{2,1,0:T(8,128)(2,1)} %constant.187.clone.refs_3_.refs_4_, ...), custom_call_target="tpu_custom_call" | custom-call | flops 1024 | bytes 1024 | tf_op jit(solution)/shard_map/row_backward/pallas_call | solution.py:602
  (47 shorter events, 18.1 us)
Async XLA Ops:
  3.4 52.3 %collective-permute-start = (f32[3]{0:T(128)S(1)}, f32[3]{0:T(128)S(1)}, u32[]{:S(2)}, u32[]{:S(2)}) collective-permute-start(f32[3]{0:T(128)S(1)} %pad_maximum_fusion.2), channel_id=1, source_target_pairs={{0,32},{32,64},{64,96},{1,33},{33,65},{65,97},{2,34},{34,66},{66,9... | collective-permute-start | bytes 44 | tf_op jit(solution)/shard_map/ppermute | solution.py:722
  14.9 10.9 %copy-start.4 = (s32[1,128,64,1]{1,3,2,0:T(1,128)S(1)}, s32[1,128,64,1]{1,3,2,0:T(1,128)}, u32[]{:S(2)}) copy-start(s32[1,128,64,1]{1,3,2,0:T(1,128)} %param.26) | copy-start | bytes 98308
  14.9 11.7 %copy-start.5 = (s32[1,128,64]{1,2,0:T(8,128)S(1)}, s32[1,128,64]{1,2,0:T(8,128)}, u32[]{:S(2)}) copy-start(s32[1,128,64]{1,2,0:T(8,128)} %param.27) | copy-start | bytes 98308
  14.9 48.2 %all-to-all-start.1 = ((f32[32,128,128]{2,1,0:T(8,128)}), f32[32,128,128]{2,1,0:T(8,128)S(1)}, u32[]{:S(2)}, u32[]{:S(2)}) async-start(f32[32,128,128]{2,1,0:T(8,128)} %row_forward.2), calls=%async_computation.1 | async-start | bytes 4194304 | tf_op jit(solution)/shard_map/all_to_all | solution.py:646
  63.1 10.0 %copy-start.1 = (f32[32,128,128]{2,1,0:T(8,128)}, f32[32,128,128]{2,1,0:T(8,128)S(1)}, u32[]{:S(2)}) copy-start(f32[32,128,128]{2,1,0:T(8,128)S(1)} %all-to-all-done.1.in_ref) | copy-start | bytes 6291460
  63.1 42.5 %all-to-all-start = ((s32[32,4,128]{2,1,0:T(4,128)}), s32[32,4,128]{2,1,0:T(4,128)S(1)}, u32[]{:S(2)}, u32[]{:S(2)}) async-start(s32[32,4,128]{2,1,0:T(4,128)} %bitcast.20), calls=%async_computation | async-start | bytes 131072 | tf_op jit(solution)/shard_map/all_to_all | solution.py:646
  139.9 59.0 %all-to-all-start.3 = ((bf16[32,512,128]{2,1,0:T(8,128)(2,1)}), bf16[32,512,128]{2,1,0:T(8,128)(2,1)}, u32[]{:S(2)}, u32[]{:S(2)}) async-start(bf16[32,512,128]{2,1,0:T(8,128)(2,1)} %bitcast.41), calls=%async_computation.3 | async-start | bytes 8388608 | tf_op jit(solution)/shard_map/all_to_all | solution.py:646
  198.9 38.5 %copy-start.6 = (f32[1,128,64]{1,2,0:T(8,128)S(1)}, f32[1,128,64]{1,2,0:T(8,128)}, u32[]{:S(2)}) copy-start(f32[1,128,64]{1,2,0:T(8,128)} %param.29) | copy-start | bytes 98308
  214.4 31.8 %all-to-all-start.4 = ((f32[32,4,128]{2,1,0:T(4,128)}), f32[32,4,128]{2,1,0:T(4,128)S(1)}, u32[]{:S(2)}, u32[]{:S(2)}) async-start(f32[32,4,128]{2,1,0:T(4,128)} %bitcast.45), calls=%async_computation.4 | async-start | bytes 131072 | tf_op jit(solution)/shard_map/all_to_all | solution.py:646
  246.2 0.6 copy-start.3
  290.2 52.8 %all-to-all-start.6 = ((f32[32,128,128]{2,1,0:T(8,128)}), f32[32,128,128]{2,1,0:T(8,128)S(1)}, u32[]{:S(2)}, u32[]{:S(2)}) async-start(f32[32,128,128]{2,1,0:T(8,128)} %row_forward.3), calls=%async_computation.6 | async-start | bytes 4194304 | tf_op jit(solution)/shard_map/all_to_all | solution.py:646
  307.3 35.7 %collective-permute-start.1 = (bf16[32,128,128]{2,1,0:T(8,128)(2,1)}, bf16[32,128,128]{2,1,0:T(8,128)(2,1)S(1)}, u32[]{:S(2)}, u32[]{:S(2)}) collective-permute-start(bf16[32,128,128]{2,1,0:T(8,128)(2,1)} %get-tuple-element.21), channel_id=1, source_target_pairs={{0,32},{32,64},{64,96},{1,33},{33,65},{65,97},{2,34},{34,66},{66,9... | collective-permute-start | bytes 3145736 | tf_op jit(solution)/shard_map/ppermute | solution.py:776
  309.3 33.8 %collective-permute-start.2 = (bf16[32,128,128]{2,1,0:T(8,128)(2,1)}, bf16[32,128,128]{2,1,0:T(8,128)(2,1)}, u32[]{:S(2)}, u32[]{:S(2)}) collective-permute-start(bf16[32,128,128]{2,1,0:T(8,128)(2,1)} %get-tuple-element.22), channel_id=1, source_target_pairs={{32,0},{64,32},{96,64},{33,1},{65,33},{97,65},{34,2},{66,34},{98,6... | collective-permute-start | bytes 3145736 | tf_op jit(solution)/shard_map/ppermute | solution.py:777
  343.1 1.0 copy-start.2
  343.1 1.7 copy-start

commit v2 on v1

--- a/solution.py
+++ b/solution.py
@@ -17,6 +17,8 @@
 PEERS = 32
 SLOTS = 512
 POINT_ROWS = 64
+TAIL = 16
+GROUP = SLOTS + TAIL
 VMEM_BYTES = 56 * 1024 * 1024
 F32 = jnp.float32
 BF16 = jnp.bfloat16
@@ -198,7 +200,37 @@
     return jnp.where(lane < HALF, 1.0, -1.0).astype(F32)
 
 
-def row_forward_kernel(tiled, x_ref, tw_ref, f_ref, a_ref, m_ref, out_ref, y_scr, e_scr):
+def put_message(ref, d, value, fine):
+    lane = lax.broadcasted_iota(jnp.int32, (INNER, INNER), 1)
+    high = value.astype(BF16)
+    ref[d, 0:INNER, :] = high
+    rest = value - high.astype(F32)
+    if fine:
+        third = rest - rest.astype(BF16).astype(F32)
+        rest = jnp.where((lane & (HALF - 1)) == 7, pltpu.roll(third, 7, 1), rest)
+    rest = jnp.where(lane < 8, rest, pltpu.roll(rest, 72, 1))
+    rest = jnp.where(lane < 16, rest, 0.0)
+    total = rest[0:16]
+    for g in range(1, 8):
+        total = total + pltpu.roll(rest[16 * g : 16 * g + 16], 16 * g, 1)
+    ref[d, INNER : INNER + TAIL, :] = total.astype(BF16)
+
+
+def get_message(ref, d, fine):
+    lane = lax.broadcasted_iota(jnp.int32, (INNER, INNER), 1)
+    packed = ref[d, INNER : INNER + TAIL, :].astype(F32)
+    rest = jnp.concatenate([packed] + [pltpu.roll(packed, INNER - 16 * g, 1) for g in range(1, 8)], axis=0)
+    rest = jnp.where(lane < 8, rest, pltpu.roll(rest, 56, 1))
+    column = lane & (HALF - 1)
+    if fine:
+        third = jnp.where(column == 0, pltpu.roll(rest, INNER - 7, 1), 0.0)
+        rest = jnp.where(column < 7, rest, 0.0) + third
+    else:
+        rest = jnp.where(column < 8, rest, 0.0)
+    return ref[d, 0:INNER, :].astype(F32) + rest
+
+
+def row_forward_kernel(tiled, fine, x_ref, tw_ref, f_ref, a_ref, m_ref, out_ref, y_scr, e_scr):
     def slab(g, carry):
         if tiled:
             xs = [x_ref[pl.ds(pl.multiple_of(g * 256 + a * 8, 8), 8), :] for a in range(OUTER)]
@@ -217,15 +249,16 @@
             y_scr[base, INNER : 2 * INNER] = im * c - re * s
         return carry
 
-    lax.fori_loop(0, 16, slab, 0)
-    out_ref[0] = data_by_table(e_scr[0], every(a_ref))
-    out_ref[1] = data_by_table(e_scr[1], every(m_ref))
+    lax.fori_loop(0, 16, slab, 0, unroll=2)
+    put_message(out_ref, 0, data_by_table(e_scr[0], every(a_ref)), fine)
+    put_message(out_ref, 1, data_by_table(e_scr[1], every(m_ref)), fine)
 
     def group(q, carry):
         v = data_by_table(y_scr[pl.ds(pl.multiple_of(q * 384, 8), 384), :], every(f_ref))
         for i in range(3):
-            out_ref[2 + 2 * (3 * q + i)] = v[i * INNER : (i + 1) * INNER, 0:INNER]
-            out_ref[3 + 2 * (3 * q + i)] = v[i * INNER : (i + 1) * INNER, INNER : 2 * INNER]
+            rows = v[i * INNER : (i + 1) * INNER]
+            put_message(out_ref, 2 + 2 * (3 * q + i), rows[:, 0:INNER], fine)
+            put_message(out_ref, 3 + 2 * (3 * q + i), rows[:, INNER : 2 * INNER], fine)
         return carry
 
     lax.fori_loop(0, 5, group, 0)
@@ -236,14 +269,14 @@
         in_ref, base_ref, tw_ref, f_ref, a_ref, m_ref, out_ref, z_scr, e_scr = refs
     else:
         in_ref, tw_ref, f_ref, a_ref, m_ref, out_ref, z_scr, e_scr = refs
-    e_scr[0] = data_by_table(in_ref[0], every(a_ref))
-    e_scr[1] = data_by_table(in_ref[1], every(m_ref))
+    e_scr[0] = data_by_table(get_message(in_ref, 0, False), every(a_ref))
+    e_scr[1] = data_by_table(get_message(in_ref, 1, False), every(m_ref))
 
     def group(q, carry):
         parts = []
         for i in range(3):
             k = 3 * q + i
-            parts.append(jnp.concatenate([in_ref[2 + 2 * k], in_ref[3 + 2 * k]], axis=1))
+            parts.append(jnp.concatenate([get_message(in_ref, 2 + 2 * k + h, False) for h in range(2)], axis=1))
         v = jnp.concatenate(parts, axis=0)
         z_scr[pl.ds(pl.multiple_of(q * 384, 8), 384), :] = data_by_table(v, every(f_ref))
         return carry
@@ -270,7 +303,23 @@
                 out_ref[pl.ds(pl.multiple_of(g * 256 + a * 8, 8), 8), :] = xs[a]
         return carry
 
-    lax.fori_loop(0, 16, slab, 0)
+    lax.fori_loop(0, 16, slab, 0, unroll=2)
+
+
+def take_all(in_ref, scr, fine):
+    def step(s, carry):
+        scr[s] = get_message(in_ref, s, fine)
+        return carry
+
+    lax.fori_loop(0, OUTER, step, 0, unroll=4)
+
+
+def give_all(scr, out_ref):
+    def step(s, carry):
+        put_message(out_ref, s, scr[s], False)
+        return carry
+
+    lax.fori_loop(0, OUTER, step, 0, unroll=4)
 
 
 def column_first_step(in_ref, y_scr, sign):
@@ -283,7 +332,7 @@
             y_scr[k, rows, :] = ys[k]
         return carry
 
-    lax.fori_loop(0, 16, slab, 0)
+    lax.fori_loop(0, 16, slab, 0, unroll=2)
 
 
 def apply_packed(e_ref, k1, value, flip):
@@ -339,7 +388,8 @@
 def column_first_kernel(
     scal, in_ref, amp_ref, ph_ref, edge_ref, ef, ei, out_ref, own_ref, up_ref, down_ref, y_scr, z_scr
 ):
-    column_first_step(in_ref, y_scr, -1.0)
+    take_all(in_ref, z_scr, True)
+    column_first_step(z_scr, y_scr, -1.0)
     flip = flip_lanes(INNER)
 
     def step(k1, carry):
@@ -358,7 +408,7 @@
             ref[k1] = turn(cb * ca - sb * sa, sb * ca + cb * sa, twice, flip).astype(BF16)
         return carry
 
-    lax.fori_loop(0, OUTER, step, 0, unroll=4)
+    lax.fori_loop(0, OUTER, step, 0, unroll=8)
 
     @pl.when(scal[6] > 0.5)
     def _():
@@ -380,18 +430,20 @@
                 ref[k1] = value.astype(ref.dtype)
             return carry
 
-        lax.fori_loop(0, OUTER, put, 0)
+        lax.fori_loop(0, OUTER, put, 0, unroll=4)
 
     def inverse(k1, carry):
         z_scr[k1] = apply_packed(ei, k1, z_scr[k1], flip)
         return carry
 
-    lax.fori_loop(0, OUTER, inverse, 0, unroll=4)
-    column_first_step(z_scr, out_ref, 1.0)
+    lax.fori_loop(0, OUTER, inverse, 0, unroll=8)
+    column_first_step(z_scr, y_scr, 1.0)
+    give_all(y_scr, out_ref)
 
 
 def column_second_kernel(scal, in_ref, amp_ref, own_ref, prev_ref, next_ref, ef, ei, out_ref, y_scr, z_scr):
-    column_first_step(in_ref, y_scr, -1.0)
+    take_all(in_ref, z_scr, False)
+    column_first_step(z_scr, y_scr, -1.0)
     flip = flip_lanes(INNER)
 
     def step(k1, carry):
@@ -401,7 +453,7 @@
         z_scr[k1] = scal[0] * (value * amp_ref[k1] - moved) + own_ref[k1]
         return carry
 
-    lax.fori_loop(0, OUTER, step, 0, unroll=4)
+    lax.fori_loop(0, OUTER, step, 0, unroll=8)
 
     @pl.when(scal[6] > 0.5)
     def _():
@@ -416,17 +468,18 @@
             z_scr[k1] = z_scr[k1] + jnp.where(mask, pltpu.roll(change, back, 1), 0.0)
             return carry
 
-        lax.fori_loop(0, OUTER, put, 0)
+        lax.fori_loop(0, OUTER, put, 0, unroll=4)
 
     def inverse(k1, carry):
         z_scr[k1] = apply_packed(ei, k1, z_scr[k1], flip)
         return carry
 
-    lax.fori_loop(0, OUTER, inverse, 0, unroll=4)
-    column_first_step(z_scr, out_ref, 1.0)
-
-
-def route_kernel(t_ref, id_ref, slot_ref, idp_ref, cnt_ref):
+    lax.fori_loop(0, OUTER, inverse, 0, unroll=8)
+    column_first_step(z_scr, y_scr, 1.0)
+    give_all(y_scr, out_ref)
+
+
+def route_kernel(t_ref, id_ref, slot_ref, tail_ref, tail_scr):
     row = lax.broadcasted_iota(jnp.int32, (INNER, 2 * INNER), 0)
     col = lax.broadcasted_iota(jnp.int32, (INNER, 2 * INNER), 1)
     tri = jnp.where(jnp.logical_or(row < col, col >= INNER), 1.0, 0.0).astype(BF16)
@@ -440,13 +493,38 @@
             pos = jnp.sum(hots[j] * (part[:, 0:INNER] + base), axis=0, keepdims=True)
             base = base + part[:, INNER : 2 * INNER]
             slot_ref[i + j : i + j + 1, :] = t_ref[i + j : i + j + 1, :] * SLOTS + pos.astype(jnp.int32)
-    cnt_ref[...] = base.astype(jnp.int32)
-    ids = id_ref[...]
-    r = lax.shift_right_logical(ids, 5)
-    idp_ref[...] = lax.shift_right_logical(r, 3) * 256 + (ids & 31) * 8 + (r & 7)
-
-
-def pack_kernel(slot_ref, idp_ref, cnt_ref, w_ref, out_ref, sid_ref, w_scr, buf):
+    batch = 4
+    index = lax.broadcasted_iota(jnp.int32, (INNER, batch * INNER), 0)
+
+    def wide(ref, i):
+        return jnp.concatenate([ref[pl.ds(i * batch + j, 1), :] for j in range(batch)], axis=1)
+
+    def put(i, acc):
+        slot = wide(slot_ref, i)
+        ids = wide(id_ref, i)
+        r = lax.shift_right_logical(ids, 5)
+        ids = lax.shift_right_logical(r, 3) * 256 + (ids & 31) * 8 + (r & 7)
+        hot = jnp.where(index == (slot & 127), 1.0, 0.0).astype(BF16)
+        line = index == lax.shift_right_logical(slot, 7)
+        v = [
+            jnp.where(line, d.astype(F32), 0.0).astype(BF16) for d in (lax.shift_right_logical(ids, 6), ids & 63)
+        ]
+        return acc + mm_nt(jnp.concatenate(v, axis=0), hot)
+
+    acc = lax.fori_loop(0, POINT_ROWS // batch, put, jnp.zeros((2 * INNER, INNER), F32), unroll=2)
+    count = base.astype(jnp.int32)
+    count_high = lax.shift_right_logical(count, 6).astype(F32)
+    count_low = (count & 63).astype(F32)
+    tail_scr[...] = jnp.zeros_like(tail_scr)
+    for s in range(PEERS):
+        tail_scr[s * TAIL : s * TAIL + 4, :] = acc[4 * s : 4 * s + 4]
+        tail_scr[s * TAIL + 4 : s * TAIL + 8, :] = acc[INNER + 4 * s : INNER + 4 * s + 4]
+        tail_scr[s * TAIL + 8 : s * TAIL + 9, :] = count_high[s : s + 1]
+        tail_scr[s * TAIL + 9 : s * TAIL + 10, :] = count_low[s : s + 1]
+    tail_ref[...] = tail_scr[...].astype(BF16)
+
+
+def pack_kernel(slot_ref, w_ref, tail_ref, out_ref, w_scr, buf):
     def clear(i, carry):
         rows = pl.ds(pl.multiple_of(i * 64, 64), 64)
         buf[rows, :] = jnp.zeros((64, INNER), F32)
@@ -459,52 +537,53 @@
     def some(q, carry):
         first = q * 16
         slots = [slot_ref[first + j] for j in range(16)]
-        ids = [idp_ref[first + j] for j in range(16)]
         rows = [w_scr[pl.ds(first + j, 1), :] for j in range(16)]
         for j in range(16):
             buf[pl.ds(slots[j], 1), :] = rows[j]
-        for j in range(16):
-            sid_ref[slots[j]] = ids[j]
         return carry
 
     lax.fori_loop(0, POINT_ROWS * INNER // 16, some, 0)
 
-    def tag(d, carry):
-        sid_ref[d * SLOTS] = (sid_ref[d * SLOTS] & 4095) | (cnt_ref[d, 0] * 4096)
-        return carry
-
-    lax.fori_loop(0, PEERS, tag, 0)
-
-    def narrow(i, carry):
-        rows = pl.ds(pl.multiple_of(i * INNER, INNER), INNER)
-        out_ref[rows, :] = buf[rows, :].astype(BF16)
-        return carry
-
-    lax.fori_loop(0, PEERS * SLOTS // INNER, narrow, 0)
+    def narrow(d, carry):
+        for i in range(4):
+            rows = pl.ds(pl.multiple_of(d * SLOTS + i * INNER, INNER), INNER)
+            out_ref[pl.ds(pl.multiple_of(d * GROUP + i * INNER, TAIL), INNER), :] = buf[rows, :].astype(BF16)
+        tail = tail_ref[pl.ds(pl.multiple_of(d * TAIL, TAIL), TAIL), :]
+        out_ref[pl.ds(pl.multiple_of(d * GROUP + SLOTS, TAIL), TAIL), :] = tail
+        return carry
+
+    lax.fori_loop(0, PEERS, narrow, 0)
 
 
 def gather_kernel(sid_ref, cnt_ref, tiles_ref, w_ref, out_ref, g_scr):
-    g_scr[...] = jnp.zeros_like(g_scr)
-    ones = jnp.ones((8, INNER), BF16)
-
     def source(s, carry):
         def some(q, inner):
             first = s * SLOTS + q * 16
             ids = [sid_ref[first + j] for j in range(16)]
             rows = [tiles_ref[pl.ds(ids[j], 1), :] for j in range(16)]
             for j in range(16):
-                g_scr[pl.ds(q * 16 + j, 1), :] = rows[j]
+                g_scr[pl.ds(first + j, 1), :] = rows[j]
             return inner
 
-        lax.fori_loop(0, lax.shift_right_logical(cnt_ref[s] + 15, 4), some, 0)
-        w = w_ref[pl.ds(pl.multiple_of(s * SLOTS, SLOTS), SLOTS), :].astype(F32)
-        high, low = split(g_scr[...] * w)
-        phase = mm_nt(ones, high) + mm_nt(ones, low)
+        return lax.fori_loop(0, lax.shift_right_logical(cnt_ref[s] + 15, 4), some, carry)
+
+    lax.fori_loop(0, PEERS, source, 0)
+    ones = jnp.ones((2 * INNER, INNER), BF16)
+    lane = lax.broadcasted_iota(jnp.int32, (INNER, INNER), 1)
+    diagonal = lane == lax.broadcasted_iota(jnp.int32, (INNER, INNER), 0)
+    place = lax.broadcasted_iota(jnp.int32, (1, INNER), 1)
+
+    def total(s, carry):
+        w = w_ref[pl.ds(pl.multiple_of(s * GROUP, TAIL), SLOTS), :].astype(F32)
+        g = g_scr[pl.ds(pl.multiple_of(s * SLOTS, SLOTS), SLOTS), :]
+        sums = mm(jnp.concatenate(split(g * w), axis=1), ones)
         for q in range(4):
-            out_ref[pl.ds(s * 4 + q, 1), :] = phase[0:1, q * INNER : (q + 1) * INNER]
-        return carry
-
-    lax.fori_loop(0, PEERS, source, 0)
+            got = jnp.where(diagonal, sums[q * INNER : (q + 1) * INNER], 0.0)
+            got = jnp.sum(got, axis=0, keepdims=True)
+            out_ref[s, q : q + 1, :] = jnp.where(place + q * INNER < cnt_ref[s], got, 0.0)
+        return carry
+
+    lax.fori_loop(0, PEERS, total, 0, unroll=2)
 
 
 def residual_kernel(slot_ref, prec_ref, phase_ref, out_ref, p_scr):
@@ -563,24 +642,28 @@
     rt_scr[...] = r_ref[...].T
     lane = lax.broadcasted_iota(jnp.int32, (INNER, INNER), 1)
 
-    def source(s, carry):
+    def scaled(s, carry):
         for q in range(4):
             col = jnp.sum(jnp.where(lane == s * 4 + q, rt_scr[...], 0.0), axis=1, keepdims=True)
-            base = pl.multiple_of(s * SLOTS + q * INNER, INNER)
-            u_scr[q * INNER : (q + 1) * INNER, :] = w_ref[pl.ds(base, INNER), :].astype(F32) * col
-
+            base = pl.multiple_of(s * GROUP + q * INNER, TAIL)
+            rows = pl.ds(pl.multiple_of(s * SLOTS + q * INNER, INNER), INNER)
+            u_scr[rows, :] = w_ref[pl.ds(base, INNER), :].astype(F32) * col
+        return carry
+
+    lax.fori_loop(0, PEERS, scaled, 0, unroll=2)
+
+    def source(s, carry):
         def some(q, inner):
             first = s * SLOTS + q * 16
             ids = [sid_ref[first + j] for j in range(16)]
-            us = [u_scr[pl.ds(q * 16 + j, 1), :] for j in range(16)]
+            us = [u_scr[pl.ds(first + j, 1), :] for j in range(16)]
             for h in range(0, 16, COPIES):
                 sums = [accs[j][pl.ds(ids[h + j], 1), :] + us[h + j] for j in range(COPIES)]
                 for j in range(COPIES):
                     accs[j][pl.ds(ids[h + j], 1), :] = sums[j]
             return inner
 
-        lax.fori_loop(0, lax.shift_right_logical(cnt_ref[s] + 15, 4), some, 0)
-        return carry
+        return lax.fori_loop(0, lax.shift_right_logical(cnt_ref[s] + 15, 4), some, carry)
 
     lax.fori_loop(0, PEERS, source, 0)
 
@@ -617,14 +700,15 @@
 
 
 PENCILS = (PEERS, INNER, INNER)
+MESSAGES = (PEERS, INNER + TAIL, INNER)
 
 
 def row_forward(x, tables, tiled):
     args = [x] + tables
     return call(
-        lambda *refs: row_forward_kernel(tiled, *refs),
+        lambda *refs: row_forward_kernel(tiled, not tiled, *refs),
         "row_forward",
-        [shape(PENCILS)],
+        [shape(MESSAGES, BF16)],
         args,
         scratch=[pltpu.VMEM((15 * INNER, 2 * INNER), F32), pltpu.VMEM((2, INNER, INNER), F32)],
     )[0]
@@ -640,6 +724,64 @@
         args,
         scratch=[pltpu.VMEM((15 * INNER, 2 * INNER), F32), pltpu.VMEM((2, INNER, INNER), F32)],
     )[0]
+
+
+def swap_kernel(in_ref, out_ref, send_sem, recv_sem, own_sem):
+    me = lax.axis_index("strip")
+    barrier = pltpu.get_barrier_semaphore()
+
+    def greet(i, carry):
+        peer = lax.rem(me + i, PEERS)
+        pl.semaphore_signal(barrier, inc=1, device_id={"strip": peer}, device_id_type=pl.DeviceIdType.MESH)
+        return carry
+
+    lax.fori_loop(1, PEERS, greet, 0)
+    pl.semaphore_wait(barrier, PEERS - 1)
+
+    def remote(i, row):
+        peer = lax.rem(me + i, PEERS)
+        return pltpu.make_async_remote_copy(
+            src_ref=in_ref.at[peer],
+            dst_ref=out_ref.at[row],
+            send_sem=send_sem.at[i],
+            recv_sem=recv_sem.at[i],
+            device_id={"strip": peer},
+            device_id_type=pl.DeviceIdType.MESH,
+        )
+
+    def start(i, carry):
+        remote(i, me).start()
+        return carry
+
+    lax.fori_loop(1, PEERS, start, 0)
+    own = pltpu.make_async_copy(in_ref.at[me], out_ref.at[me], own_sem)
+    own.start()
+    own.wait()
+
+    def finish(i, carry):
+        copy = remote(i, lax.rem(me + PEERS - i, PEERS))
+        copy.wait_send()
+        copy.wait_recv()
+        return carry
+
+    lax.fori_loop(1, PEERS, finish, 0)
+
+
+def swap(value, collective_id):
+    anywhere = pl.BlockSpec(memory_space=pl.ANY)
+    return pl.pallas_call(
+        swap_kernel,
+        out_shape=shape(value.shape, value.dtype),
+        in_specs=[anywhere],
+        out_specs=anywhere,
+        scratch_shapes=[
+            pltpu.SemaphoreType.DMA((PEERS,)),
+            pltpu.SemaphoreType.DMA((PEERS,)),
+            pltpu.SemaphoreType.DMA,
+        ],
+        compiler_params=pltpu.CompilerParams(collective_id=collective_id, has_side_effects=True),
+        name="swap",
+    )(value)
 
 
 def exchange(value):
@@ -743,49 +885,53 @@
     scal = jnp.concatenate([head, cua, sua, cda, sda])
     amp = amplitude_table(strip)
 
-    slots, ids, counts = call(
+    slots, tail = call(
         route_kernel,
         "route",
-        [shape((POINT_ROWS, INNER), jnp.int32)] * 2 + [shape((PEERS, INNER), jnp.int32)],
+        [shape((POINT_ROWS, INNER), jnp.int32), shape((PEERS * TAIL, INNER), BF16)],
         [target, block],
+        scratch=[pltpu.VMEM((PEERS * TAIL, INNER), F32)],
     )
-    sent, sent_ids = call(
+    sent = call(
         pack_kernel,
         "pack",
-        [shape((PEERS * SLOTS, INNER), BF16), shape((PEERS * SLOTS,), jnp.int32)],
-        [slots.reshape(-1), ids.reshape(-1), counts, weights],
-        smem=3,
-        smem_outs=(1,),
+        [shape((PEERS * GROUP, INNER), BF16)],
+        [slots.reshape(-1), weights, tail],
+        smem=1,
         scratch=[pltpu.VMEM((POINT_ROWS * INNER, INNER), F32), pltpu.VMEM((PEERS * SLOTS, INNER), F32)],
-    )
+    )[0]
     pencils = exchange(row_forward(x, row_fine_tables, False))
-    here = exchange(sent.reshape(PEERS, SLOTS, INNER)).reshape(PEERS * SLOTS, INNER)
-    tagged = exchange(sent_ids.reshape(PEERS, 4, INNER))
-    here_counts = lax.shift_right_logical(tagged[:, 0, 0], 12)
-    here_ids = (tagged & 4095).reshape(PEERS * SLOTS)
+    pencils, sent = lax.optimization_barrier((pencils, sent))
+    arrived = exchange(sent.reshape(PEERS, GROUP, INNER))
 
     spectral = [pltpu.VMEM(PENCILS, F32), pltpu.VMEM(PENCILS, F32)]
     screen_pencils, own, up, down = call(
         column_first_kernel,
         "column_first",
-        [shape(PENCILS), shape(PENCILS), shape(PENCILS, BF16), shape(PENCILS, BF16)],
+        [shape(MESSAGES, BF16), shape(PENCILS), shape(PENCILS, BF16), shape(PENCILS, BF16)],
         [scal, pencils, amp, phases, edge_phases] + col_fine_tables,
         smem=1,
         scratch=spectral,
     )
     from_prev = lax.ppermute(up, "tm", up_pairs)
     from_next = lax.ppermute(down, "tm", down_pairs)
-    tiles = row_backward(exchange(screen_pencils), None, row_inv_tables)
+    screen_pencils, arrived = lax.optimization_barrier((screen_pencils, arrived))
+    tiles = row_backward(swap(screen_pencils, 1), None, row_inv_tables)
+    here = arrived.reshape(PEERS * GROUP, INNER)
+    digits = arrived[:, SLOTS:, :].astype(F32)
+    here_ids = (digits[:, 0:4] * 64.0 + digits[:, 4:8]).astype(jnp.int32).reshape(PEERS * SLOTS)
+    here_counts = (digits[:, 8, 0] * 64.0 + digits[:, 9, 0]).astype(jnp.int32)
 
     phase = call(
         gather_kernel,
         "gather",
-        [shape((INNER, INNER))],
+        [shape((PEERS, 4, INNER))],
         [here_ids, here_counts, tiles, here],
         smem=2,
-        scratch=[pltpu.VMEM((SLOTS, INNER), F32)],
+        scratch=[pltpu.VMEM((PEERS * SLOTS, INNER), F32)],
     )[0]
-    returned = exchange(phase.reshape(PEERS, 4, INNER)).reshape(INNER, INNER)
+    returned = swap(phase, 2).reshape(INNER, INNER)
+    from_prev, from_next, returned = lax.optimization_barrier((from_prev, from_next, returned))
     resid = call(
         residual_kernel,
         "residual",
@@ -793,26 +939,26 @@
         [slots, prec, returned],
         scratch=[pltpu.VMEM((POINT_ROWS, INNER), F32)],
     )[0]
-    resid_here = exchange(resid.reshape(PEERS, 4, INNER)).reshape(INNER, INNER)
+    resid_here = swap(resid.reshape(PEERS, 4, INNER), 2).reshape(INNER, INNER)
     gradient = call(
         scatter_kernel,
         "scatter",
         [shape((SIDE, INNER))],
         [here_ids, here_counts, resid_here, here],
         smem=2,
-        scratch=[pltpu.VMEM((INNER, INNER), F32), pltpu.VMEM((SLOTS, INNER), F32)]
+        scratch=[pltpu.VMEM((INNER, INNER), F32), pltpu.VMEM((PEERS * SLOTS, INNER), F32)]
         + [pltpu.VMEM((SIDE, INNER), F32)] * COPIES,
     )[0]
-    pencils = exchange(row_forward(gradient, row_fwd_tables, True))
+    pencils = swap(row_forward(gradient, row_fwd_tables, True), 1)
     out_pencils = call(
         column_second_kernel,
         "column_second",
-        [shape(PENCILS)],
+        [shape(MESSAGES, BF16)],
         [scal, pencils, amp, own, from_prev, from_next] + col_tables,
         smem=1,
         scratch=spectral,
     )[0]
-    return row_backward(exchange(out_pencils), x, row_inv_tables)[None]
+    return row_backward(swap(out_pencils, 1), x, row_inv_tables)[None]
 
 
 def solution(mesh):

time: 411 us -> 324 us (0.79)
  Pallas kernels: 148 us -> 263 us
  waiting for transfers between devices: 81.2 us -> 0.01 us
  blocking collectives: 77.6 us -> 0 us
  starting transfers between devices: 78.4 us -> 36.7 us
    pallas_call x0 -> x5, Pallas kernels: none -> 125 us  [swap(): pl.pallas_call(swap_kernel, out_shape=shape(value.shape, value.dtype), in...]
    all_to_all x3 -> x0, blocking collectives: 77.6 us -> none  [exchange(): lax.all_to_all(value, 'strip', split_axis=0, concat_axis=0, tiled=True)]
    all_to_all x5 -> x2, waiting for transfers between devices: 53 us -> 0.01 us  [exchange(): lax.all_to_all(value, 'strip', split_axis=0, concat_axis=0, tiled=True)]
    all_to_all x5 -> x2, starting transfers between devices: 66 us -> 20.7 us  [exchange(): lax.all_to_all(value, 'strip', split_axis=0, concat_axis=0, tiled=True)]
    ppermute x1, waiting for transfers between devices: 28.2 us -> 0.01 us  [local(): from_prev = lax.ppermute(up, 'tm', up_pairs)]
    pallas_call x11, Pallas kernels: 148 us -> 138 us  [call(): pl.pallas_call(kernel, out_shape=out_shapes, in_specs=[small] * smem + [v...]
    ppermute x1, starting transfers between devices: 1.92 us -> 9.86 us  [local(): from_prev = lax.ppermute(up, 'tm', up_pairs)]
  transfers between devices with their start and end apart: 8 -> 5, of which waited for: 3 -> 0; matrix products, arithmetic and copies ran while one was open for 3% -> 4% of each run, Pallas kernels for 16% -> 40%
where the time goes in v2:
time: 324 us; the launch traced here: 323 us
  Pallas kernels  263 us (81%)
  starting transfers between devices  36.7 us (11%)
  other arithmetic  10.1 us (3%)
  between operations  7.75 us (2%)
  local copies, waits for them, and re-layouts  5.32 us (2%)
    pallas_call x11, Pallas kernels, call(): pl.pallas_call(kernel, out_shape=out_shapes, in_specs=[small] * smem + [v...  138 us
    pallas_call x5, Pallas kernels, swap(): pl.pallas_call(swap_kernel, out_shape=shape(value.shape, value.dtype), in...  125 us
    all_to_all x2, starting transfers between devices, exchange(): lax.all_to_all(value, 'strip', split_axis=0, concat_axis=0, tiled=True)  20.7 us
    ppermute x1, starting transfers between devices, local(): from_prev = lax.ppermute(up, 'tm', up_pairs)  9.86 us
  transfers between devices with their start and end apart: 5, of which 0 were waited for; matrix products, arithmetic and copies ran while one was open for 4% of the time, Pallas kernels for 40%

profile of v2, /device:TPU:1, one launch (start us, length us, event | category | flops | bytes accessed | tf_op | source)
XLA Modules:
  0.0 322.7 jit_solution(13071505145572685095)
XLA Ops:
  0.0 7.8 %row_forward.2 = bf16[32,144,128]{2,1,0:T(8,128)(2,1)} custom-call(f32[128,4096]{1,0:T(8,128)} %bitcast.37, f32[2,16,128]{2,1,0:T(8,128)} %constant.179.clone.refs_1_.refs_2_, bf16[3,256,256]{2,1,0:T(8,128)(2,1)} %constant.183.clone.refs_2_, bf16[3,128,128]{2,1,0:T(8,128)(2,1)} %constant.184.clone.refs_3_, bf16[3,128,128]{2,1,0:T(8,128)(2,1)} %constant.185.clone.refs_4_), custom_call_target="tpu_custom_call" | custom-call | flops 1024 | bytes 1024 | tf_op jit(solution)/shard_map/row_forward/pallas_call | solution.py:685
  7.8 11.3 %all-to-all-start = ((bf16[32,144,128]{2,1,0:T(8,128)(2,1)}), bf16[32,144,128]{2,1,0:T(8,128)(2,1)S(1)}, u32[]{:S(2)}, u32[]{:S(2)}) async-start(bf16[32,144,128]{2,1,0:T(8,128)(2,1)} %row_forward.2), calls=%async_computation | async-start | bytes 2359296 | tf_op jit(solution)/shard_map/all_to_all | solution.py:788
  20.7 4.6 %route.1 = (s32[64,128]{1,0:T(8,128)}, bf16[512,128]{1,0:T(8,128)(2,1)}) custom-call(s32[64,128]{1,0:T(8,128)} %reshape.657.t_ref, s32[64,128]{1,0:T(8,128)} %reshape.658.id_ref), custom_call_target="tpu_custom_call" | custom-call | flops 1024 | bytes 1024 | tf_op jit(solution)/shard_map/route/pallas_call | solution.py:685
  25.3 14.1 %pack.1 = bf16[16896,128]{1,0:T(8,128)(2,1)} custom-call(s32[8192]{0:T(1024)} %bitcast.45, bf16[8192,128]{1,0:T(8,128)(2,1)} %bitcast.39, bf16[512,128]{1,0:T(8,128)(2,1)} %get-tuple-element.19.tail_ref), custom_call_target="tpu_custom_call" | custom-call | flops 1024 | bytes 1024 | tf_op jit(solution)/shard_map/pack/pallas_call | solution.py:685
  40.4 9.4 %all-to-all-start.1 = ((bf16[32,528,128]{2,1,0:T(8,128)(2,1)}), bf16[32,528,128]{2,1,0:T(8,128)(2,1)}, u32[]{:S(2)}, u32[]{:S(2)}) async-start(bf16[32,528,128]{2,1,0:T(8,128)(2,1)} %bitcast.36), calls=%async_computation.1 | async-start | bytes 8650752 | tf_op jit(solution)/shard_map/all_to_all | solution.py:788
  52.4 4.0 %collective-permute-start = (f32[3]{0:T(128)S(1)}, f32[3]{0:T(128)S(1)}, u32[]{:S(2)}, u32[]{:S(2)}) collective-permute-start(f32[3]{0:T(128)S(1)} %pad_maximum_fusion.2), channel_id=1, source_target_pairs={{0,32},{32,64},{64,96},{1,33},{33,65},{65,97},{2,34},{34,66},{66,9... | collective-permute-start | bytes 44 | tf_op jit(solution)/shard_map/ppermute | solution.py:864
  60.5 2.4 power_multiply_fusion.amp_ref
  68.8 1.2 fusion.17
  70.8 26.9 %column_first.1 = (bf16[32,144,128]{2,1,0:T(8,128)(2,1)}, f32[32,128,128]{2,1,0:T(8,128)}, bf16[32,128,128]{2,1,0:T(8,128)(2,1)}, bf16[32,128,128]{2,1,0:T(8,128)(2,1)}) custom-call(f32[136]{0:T(256)} %concatenate.22.scal, bf16[32,144,128]{2,1,0:T(8,128)(2,1)} %copy-done, f32[32,128,128]{2,1,0:T(8,128)} %power_multiply_fusion.amp_ref, ...), custom_call_target="tpu_custom_call" | custom-call | flops 1024 | bytes 1024 | tf_op jit(solution)/shard_map/column_first/pallas_call | solution.py:685
  97.7 9.9 %collective-permute-start.1 = (bf16[32,128,128]{2,1,0:T(8,128)(2,1)}, bf16[32,128,128]{2,1,0:T(8,128)(2,1)S(1)}, u32[]{:S(2)}, u32[]{:S(2)}) collective-permute-start(bf16[32,128,128]{2,1,0:T(8,128)(2,1)} %get-tuple-element.24), channel_id=1, source_target_pairs={{0,32},{32,64},{64,96},{1,33},{33,65},{65,97},{2,34},{34,66},{66,9... | collective-permute-start | bytes 3145736 | tf_op jit(solution)/shard_map/ppermute | solution.py:916
  107.5 2.1 collective-permute-start.2
  110.4 35.8 %swap.5.refs_0_ = bf16[32,144,128]{2,1,0:T(8,128)(2,1)} custom-call(bf16[32,144,128]{2,1,0:T(8,128)(2,1)} %get-tuple-element.26.in_ref), custom_call_target="tpu_custom_call" | custom-call | tf_op jit(solution)/shard_map/swap/pallas_call | solution.py:772
  146.2 6.2 %row_backward.2.tiles_ref = f32[4096,128]{1,0:T(8,128)} custom-call(bf16[32,144,128]{2,1,0:T(8,128)(2,1)} %swap.5.refs_0_, f32[2,16,128]{2,1,0:T(8,128)} %constant.179.clone.refs_1_.refs_2_, bf16[2,256,256]{2,1,0:T(8,128)(2,1)} %constant.186.clone.refs_2_.refs_3_, bf16[2,128,128]{2,1,0:T(8,128)(2,1)} %constant.187.clone.refs_3_.refs_4_, ...), custom_call_target="tpu_custom_call" | custom-call | flops 1024 | bytes 1024 | tf_op jit(solution)/shard_map/row_backward/pallas_call | solution.py:685
  153.3 1.2 fusion.24.cnt_ref
  155.2 16.2 %gather.1.in_ref = f32[32,4,128]{2,1,0:T(4,128)} custom-call(s32[16384]{0:T(1024)} %bitcast.40, s32[32]{0:T(128)} %fusion.24.cnt_ref, f32[4096,128]{1,0:T(8,128)} %row_backward.2.tiles_ref, bf16[16896,128]{1,0:T(8,128)(2,1)} %bitcast.22.w_ref), custom_call_target="tpu_custom_call" | custom-call | flops 1024 | bytes 1024 | tf_op jit(solution)/shard_map/gather/pallas_call | solution.py:685
  171.4 25.9 %swap.6 = f32[32,4,128]{2,1,0:T(4,128)} custom-call(f32[32,4,128]{2,1,0:T(4,128)} %gather.1.in_ref), custom_call_target="tpu_custom_call" | custom-call | tf_op jit(solution)/shard_map/swap/pallas_call | solution.py:772
  197.4 7.0 %residual.1 = f32[128,128]{1,0:T(8,128)} custom-call(s32[64,128]{1,0:T(8,128)} %get-tuple-element.18.slot_ref, f32[64,128]{1,0:T(8,128)} %reshape.662.prec_ref, f32[128,128]{1,0:T(8,128)} %bitcast.42), custom_call_target="tpu_custom_call" | custom-call | flops 1024 | bytes 1024 | tf_op jit(solution)/shard_map/residual/pallas_call | solution.py:685
  204.4 10.5 %swap.7 = f32[32,4,128]{2,1,0:T(4,128)} custom-call(f32[32,4,128]{2,1,0:T(4,128)} %bitcast.43), custom_call_target="tpu_custom_call" | custom-call | tf_op jit(solution)/shard_map/swap/pallas_call | solution.py:772
  214.9 18.8 %scatter.1.refs_0_ = f32[4096,128]{1,0:T(8,128)} custom-call(s32[16384]{0:T(1024)} %bitcast.41, s32[32]{0:T(128)} %fusion.24.cnt_ref, f32[128,128]{1,0:T(8,128)} %bitcast.44, bf16[16896,128]{1,0:T(8,128)(2,1)} %bitcast.22.w_ref), custom_call_target="tpu_custom_call" | custom-call | flops 1024 | bytes 1024 | tf_op jit(solution)/shard_map/scatter/pallas_call | solution.py:685
  233.8 6.2 %row_forward.3.in_ref = bf16[32,144,128]{2,1,0:T(8,128)(2,1)} custom-call(f32[4096,128]{1,0:T(8,128)} %scatter.1.refs_0_, f32[2,16,128]{2,1,0:T(8,128)} %constant.179.clone.refs_1_.refs_2_, bf16[2,256,256]{2,1,0:T(8,128)(2,1)} %constant.180.clone.refs_2_, bf16[2,128,128]{2,1,0:T(8,128)(2,1)} %constant.181.clone.refs_3_, ...), custom_call_target="tpu_custom_call" | custom-call | flops 1024 | bytes 1024 | tf_op jit(solution)/shard_map/row_forward/pallas_call | solution.py:685
  240.0 31.8 %swap.8.in_ref = bf16[32,144,128]{2,1,0:T(8,128)(2,1)} custom-call(bf16[32,144,128]{2,1,0:T(8,128)(2,1)} %row_forward.3.in_ref), custom_call_target="tpu_custom_call" | custom-call | tf_op jit(solution)/shard_map/swap/pallas_call | solution.py:772
  271.8 23.0 %column_second.1.in_ref = bf16[32,144,128]{2,1,0:T(8,128)(2,1)} custom-call(f32[136]{0:T(256)} %concatenate.22.scal, bf16[32,144,128]{2,1,0:T(8,128)(2,1)} %swap.8.in_ref, f32[32,128,128]{2,1,0:T(8,128)} %power_multiply_fusion.amp_ref, f32[32,128,128]{2,1,0:T(8,128)} %get-tuple-element.28.own_ref, bf16[32,128,128]{2,1,0:T(8,128)(2,1)} %copy-done.1, ...), custom_call_target="tpu_custom_call" | custom-call | flops 1024 | bytes 1024 | tf_op jit(solution)/shard_map/column_second/pallas_call | solution.py:685
  294.8 21.0 %swap.9.refs_0_ = bf16[32,144,128]{2,1,0:T(8,128)(2,1)} custom-call(bf16[32,144,128]{2,1,0:T(8,128)(2,1)} %column_second.1.in_ref), custom_call_target="tpu_custom_call" | custom-call | tf_op jit(solution)/shard_map/swap/pallas_call | solution.py:772
  315.9 6.8 %row_backward.3 = f32[128,4096]{1,0:T(8,128)} custom-call(bf16[32,144,128]{2,1,0:T(8,128)(2,1)} %swap.9.refs_0_, f32[128,4096]{1,0:T(8,128)} %bitcast.38, f32[2,16,128]{2,1,0:T(8,128)} %constant.179.clone.refs_1_.refs_2_, bf16[2,256,256]{2,1,0:T(8,128)(2,1)} %constant.186.clone.refs_2_.refs_3_, bf16[2,128,128]{2,1,0:T(8,128)(2,1)} %constant.187.clone.refs_3_.refs_4_, ...), custom_call_target="tpu_custom_call" | custom-call | flops 1024 | bytes 1024 | tf_op jit(solution)/shard_map/row_backward/pallas_call | solution.py:685
  (44 shorter events, 10.7 us)
Async XLA Ops:
  7.8 11.3 %copy-start.3 = (s32[1,128,64,1]{1,3,2,0:T(1,128)S(1)}, s32[1,128,64,1]{1,3,2,0:T(1,128)}, u32[]{:S(2)}) copy-start(s32[1,128,64,1]{1,3,2,0:T(1,128)} %param.26) | copy-start | bytes 98308
  7.8 12.1 %copy-start.4 = (s32[1,128,64]{1,2,0:T(8,128)S(1)}, s32[1,128,64]{1,2,0:T(8,128)}, u32[]{:S(2)}) copy-start(s32[1,128,64]{1,2,0:T(8,128)} %param.27) | copy-start | bytes 98308
  7.8 31.7 %all-to-all-start = ((bf16[32,144,128]{2,1,0:T(8,128)(2,1)}), bf16[32,144,128]{2,1,0:T(8,128)(2,1)S(1)}, u32[]{:S(2)}, u32[]{:S(2)}) async-start(bf16[32,144,128]{2,1,0:T(8,128)(2,1)} %row_forward.2), calls=%async_computation | async-start | bytes 2359296 | tf_op jit(solution)/shard_map/all_to_all | solution.py:788
  39.4 1.0 copy-start
  39.4 11.0 %copy-start.6 = (s32[1,2]{1,0:T(1,128)S(1)}, s32[1,2]{1,0:T(1,128)}, u32[]{:S(2)}) copy-start(s32[1,2]{1,0:T(1,128)} %param.25) | copy-start | bytes 28
  40.4 70.0 %all-to-all-start.1 = ((bf16[32,528,128]{2,1,0:T(8,128)(2,1)}), bf16[32,528,128]{2,1,0:T(8,128)(2,1)}, u32[]{:S(2)}, u32[]{:S(2)}) async-start(bf16[32,528,128]{2,1,0:T(8,128)(2,1)} %bitcast.36), calls=%async_computation.1 | async-start | bytes 8650752 | tf_op jit(solution)/shard_map/all_to_all | solution.py:788
  52.4 10.5 %collective-permute-start = (f32[3]{0:T(128)S(1)}, f32[3]{0:T(128)S(1)}, u32[]{:S(2)}, u32[]{:S(2)}) collective-permute-start(f32[3]{0:T(128)S(1)} %pad_maximum_fusion.2), channel_id=1, source_target_pairs={{0,32},{32,64},{64,96},{1,33},{33,65},{65,97},{2,34},{34,66},{66,9... | collective-permute-start | bytes 44 | tf_op jit(solution)/shard_map/ppermute | solution.py:864
  70.8 38.9 %copy-start.5 = (f32[1,128,64]{1,2,0:T(8,128)S(1)}, f32[1,128,64]{1,2,0:T(8,128)}, u32[]{:S(2)}) copy-start(f32[1,128,64]{1,2,0:T(8,128)} %param.29) | copy-start | bytes 98308
  97.7 99.6 %collective-permute-start.1 = (bf16[32,128,128]{2,1,0:T(8,128)(2,1)}, bf16[32,128,128]{2,1,0:T(8,128)(2,1)S(1)}, u32[]{:S(2)}, u32[]{:S(2)}) collective-permute-start(bf16[32,128,128]{2,1,0:T(8,128)(2,1)} %get-tuple-element.24), channel_id=1, source_target_pairs={{0,32},{32,64},{64,96},{1,33},{33,65},{65,97},{2,34},{34,66},{66,9... | collective-permute-start | bytes 3145736 | tf_op jit(solution)/shard_map/ppermute | solution.py:916
  107.5 89.8 %collective-permute-start.2 = (bf16[32,128,128]{2,1,0:T(8,128)(2,1)}, bf16[32,128,128]{2,1,0:T(8,128)(2,1)S(1)}, u32[]{:S(2)}, u32[]{:S(2)}) collective-permute-start(bf16[32,128,128]{2,1,0:T(8,128)(2,1)} %get-tuple-element.25), channel_id=1, source_target_pairs={{32,0},{64,32},{96,64},{33,1},{65,33},{97,65},{34,2},{66,34},{98,6... | collective-permute-start | bytes 3145736 | tf_op jit(solution)/shard_map/ppermute | solution.py:917
  197.3 36.4 %copy-start.1 = (bf16[32,128,128]{2,1,0:T(8,128)(2,1)}, bf16[32,128,128]{2,1,0:T(8,128)(2,1)S(1)}, u32[]{:S(2)}) copy-start(bf16[32,128,128]{2,1,0:T(8,128)(2,1)S(1)} %collective-permute-done.1.prev_ref) | copy-start | bytes 3145732
  197.3 36.4 %copy-start.2 = (bf16[32,128,128]{2,1,0:T(8,128)(2,1)}, bf16[32,128,128]{2,1,0:T(8,128)(2,1)S(1)}, u32[]{:S(2)}) copy-start(bf16[32,128,128]{2,1,0:T(8,128)(2,1)S(1)} %collective-permute-done.2.next_ref) | copy-start | bytes 3145732

commit v3 on v2

--- a/solution.py
+++ b/solution.py
@@ -340,6 +340,63 @@
     return r[0:INNER] - pltpu.roll(r[INNER : 2 * INNER], HALF, 1) * flip
 
 
+MESH = pl.DeviceIdType.MESH
+
+
+def greet_peers(me, barrier, extra=()):
+    def greet(i, carry):
+        pl.semaphore_signal(barrier, inc=1, device_id={"strip": lax.rem(me + i, PEERS)}, device_id_type=MESH)
+        return carry
+
+    lax.fori_loop(1, PEERS, greet, 0)
+    for device in extra:
+        pl.semaphore_signal(barrier, inc=1, device_id=device, device_id_type=MESH)
+    pl.semaphore_wait(barrier, PEERS - 1 + len(extra))
+
+
+class Exchange:
+    def __init__(self, me, in_ref, out_ref, send_sem, recv_sem, own_sem):
+        self.me, self.in_ref, self.out_ref = me, in_ref, out_ref
+        self.send_sem, self.recv_sem = send_sem, recv_sem
+        self.own = pltpu.make_async_copy(in_ref.at[me], out_ref.at[me], own_sem)
+
+    def copy(self, peer, send, source):
+        return pltpu.make_async_remote_copy(
+            src_ref=self.in_ref.at[peer],
+            dst_ref=self.out_ref.at[source],
+            send_sem=self.send_sem.at[send],
+            recv_sem=self.recv_sem.at[source],
+            device_id={"strip": peer},
+            device_id_type=MESH,
+        )
+
+    def peer(self, i):
+        return lax.rem(self.me + 1 + lax.rem(i + 2 * self.me, PEERS - 1), PEERS)
+
+    def start(self):
+        def step(i, carry):
+            self.copy(self.peer(i), i, self.me).start()
+            return carry
+
+        lax.fori_loop(0, PEERS - 1, step, 0)
+        self.own.start()
+
+    def wait(self):
+        def step(i, carry):
+            peer = self.peer(i)
+            copy = self.copy(peer, i, peer)
+            copy.wait_send()
+            copy.wait_recv()
+            return carry
+
+        self.own.wait()
+        lax.fori_loop(0, PEERS - 1, step, 0)
+
+
+def exchange_sems():
+    return [pltpu.SemaphoreType.DMA((PEERS,)), pltpu.SemaphoreType.DMA((PEERS,)), pltpu.SemaphoreType.DMA]
+
+
 def edge_lanes():
     lane = lax.broadcasted_iota(jnp.int32, (INNER, INNER), 1)
     return jnp.logical_or(lane == 0, lane == HALF), lane < HALF
@@ -386,8 +443,15 @@
 
 
 def column_first_kernel(
-    scal, in_ref, amp_ref, ph_ref, edge_ref, ef, ei, out_ref, own_ref, up_ref, down_ref, y_scr, z_scr
+    scale, rate, wind, prior, in_ref, ef, ei, sent_ref,
+    back_ref, own_ref, up_ref, down_ref, here_ref, amp_ref, par, *scratch,
 ):
+    y_scr, z_scr, msg_scr, tab_ref = scratch[0:4]
+    me = lax.axis_index("strip")
+    greet_peers(me, pltpu.get_barrier_semaphore())
+    weights = Exchange(me, sent_ref, here_ref, *scratch[4:7])
+    weights.start()
+    tables_kernel(scale, rate, wind, prior, tab_ref, amp_ref, par)
     take_all(in_ref, z_scr, True)
     column_first_step(z_scr, y_scr, -1.0)
     flip = flip_lanes(INNER)
@@ -398,30 +462,30 @@
         once = value * amp
         twice = once * amp
         y_scr[k1] = value
-        z_scr[k1] = scal[0] * once
-        own_ref[k1] = scal[3] * twice
-        for n, ref, gain in ((0, up_ref, scal[1]), (1, down_ref, scal[2])):
-            cb = ph_ref[2 * n]
-            sb = ph_ref[2 * n + 1]
-            ca = scal[8 + 64 * n + k1] * gain
-            sa = scal[8 + 64 * n + 32 + k1] * gain
+        z_scr[k1] = par[0] * once
+        own_ref[k1] = par[3] * twice
+        for n, ref, gain in ((0, up_ref, par[1]), (1, down_ref, par[2])):
+            cb = tab_ref[2 * n]
+            sb = tab_ref[2 * n + 1]
+            ca = tab_ref[8, pl.ds(64 * n + k1, 1), :] * gain
+            sa = tab_ref[8, pl.ds(64 * n + 32 + k1, 1), :] * gain
             ref[k1] = turn(cb * ca - sb * sa, sb * ca + cb * sa, twice, flip).astype(BF16)
         return carry
 
     lax.fori_loop(0, OUTER, step, 0, unroll=8)
 
-    @pl.when(scal[6] > 0.5)
+    @pl.when(me == 0)
     def _():
         u0, u2, a0, a2 = edge_split(edge_gather(y_scr), edge_gather(amp_ref))
         mask, _ = edge_lanes()
         e0 = a0 * u0
         e2 = a2 * u2
-        fixed = [scal[0] * (e0 + e2)]
+        fixed = [par[0] * (e0 + e2)]
         e0 = a0 * e0
         e2 = a2 * e2
-        fixed.append(scal[3] * (e0 + e2))
-        fixed.append(scal[1] * turn(edge_ref[0], edge_ref[1], e0 + scal[4] * e2, flip))
-        fixed.append(scal[2] * turn(edge_ref[2], edge_ref[3], e0 + scal[5] * e2, flip))
+        fixed.append(par[3] * (e0 + e2))
+        fixed.append(par[1] * turn(tab_ref[4], tab_ref[5], e0 + par[4] * e2, flip))
+        fixed.append(par[2] * turn(tab_ref[6], tab_ref[7], e0 + par[5] * e2, flip))
 
         def put(k1, carry):
             back = lax.rem(INNER - k1, INNER)
@@ -438,30 +502,60 @@
 
     lax.fori_loop(0, OUTER, inverse, 0, unroll=8)
     column_first_step(z_scr, y_scr, 1.0)
-    give_all(y_scr, out_ref)
-
-
-def column_second_kernel(scal, in_ref, amp_ref, own_ref, prev_ref, next_ref, ef, ei, out_ref, y_scr, z_scr):
-    take_all(in_ref, z_scr, False)
+    give_all(y_scr, msg_scr)
+    back = Exchange(me, msg_scr, back_ref, *scratch[7:10])
+    back.start()
+    back.wait()
+    weights.wait()
+
+
+SIDE_PARTS = 4
+
+
+def column_second_kernel(par, in_ref, amp_ref, own_ref, up_ref, down_ref, ef, ei, back_ref, *scratch):
+    y_scr, z_scr, msg_scr, prev_ref, next_ref, side_sems = scratch[0:6]
+    me = lax.axis_index("strip")
+    slot_at = lax.axis_index("tm")
+    above, below = lax.rem(slot_at + 1, 4), lax.rem(slot_at + 3, 4)
+    greet_peers(me, pltpu.get_barrier_semaphore(), ({"tm": above}, {"tm": below}))
+    pencils = Exchange(me, in_ref, msg_scr, *scratch[6:9])
+    pencils.start()
+    sides = []
+    for p in range(SIDE_PARTS):
+        rows = pl.ds(p * (OUTER // SIDE_PARTS), OUTER // SIDE_PARTS)
+        for n, (src, dst, device) in enumerate(((up_ref, prev_ref, above), (down_ref, next_ref, below))):
+            sides.append(
+                pltpu.make_async_remote_copy(
+                    src_ref=src.at[rows],
+                    dst_ref=dst.at[rows],
+                    send_sem=side_sems.at[0, n, p],
+                    recv_sem=side_sems.at[1, n, p],
+                    device_id={"tm": device},
+                    device_id_type=MESH,
+                )
+            )
+    for side in sides:
+        side.start()
+    pencils.wait()
+    take_all(msg_scr, z_scr, False)
     column_first_step(z_scr, y_scr, -1.0)
     flip = flip_lanes(INNER)
 
     def step(k1, carry):
         value = apply_packed(ef, k1, y_scr[k1], flip)
-        moved = prev_ref[k1].astype(F32) + next_ref[k1].astype(F32)
         y_scr[k1] = value
-        z_scr[k1] = scal[0] * (value * amp_ref[k1] - moved) + own_ref[k1]
+        z_scr[k1] = par[0] * (value * amp_ref[k1]) + own_ref[k1]
         return carry
 
     lax.fori_loop(0, OUTER, step, 0, unroll=8)
 
-    @pl.when(scal[6] > 0.5)
+    @pl.when(me == 0)
     def _():
         spec = edge_gather(y_scr)
         amp = edge_gather(amp_ref)
         u0, u2, a0, a2 = edge_split(spec, amp)
         mask, _ = edge_lanes()
-        change = scal[0] * (a0 * u0 + a2 * u2 - amp * spec)
+        change = par[0] * (a0 * u0 + a2 * u2 - amp * spec)
 
         def put(k1, carry):
             back = lax.rem(INNER - k1, INNER)
@@ -470,13 +564,20 @@
 
         lax.fori_loop(0, OUTER, put, 0, unroll=4)
 
+    for side in sides:
+        side.wait()
+
     def inverse(k1, carry):
-        z_scr[k1] = apply_packed(ei, k1, z_scr[k1], flip)
+        moved = prev_ref[k1].astype(F32) + next_ref[k1].astype(F32)
+        z_scr[k1] = apply_packed(ei, k1, z_scr[k1] - par[0] * moved, flip)
         return carry
 
     lax.fori_loop(0, OUTER, inverse, 0, unroll=8)
     column_first_step(z_scr, y_scr, 1.0)
-    give_all(y_scr, out_ref)
+    give_all(y_scr, msg_scr)
+    back = Exchange(me, msg_scr, back_ref, *scratch[9:12])
+    back.start()
+    back.wait()
 
 
 def route_kernel(t_ref, id_ref, slot_ref, tail_ref, tail_scr):
@@ -555,7 +656,9 @@
     lax.fori_loop(0, PEERS, narrow, 0)
 
 
-def gather_kernel(sid_ref, cnt_ref, tiles_ref, w_ref, out_ref, g_scr):
+def gather_kernel(sid_ref, cnt_ref, in_ref, w_ref, tw, f_ref, a_ref, m_ref, out_ref, g_scr, tiles_ref, z_scr, e_scr):
+    row_backward_kernel(False, in_ref, tw, f_ref, a_ref, m_ref, tiles_ref, z_scr, e_scr)
+
     def source(s, carry):
         def some(q, inner):
             first = s * SLOTS + q * 16
@@ -586,8 +689,16 @@
     lax.fori_loop(0, PEERS, total, 0, unroll=2)
 
 
-def residual_kernel(slot_ref, prec_ref, phase_ref, out_ref, p_scr):
-    high, low = split(phase_ref[...])
+def residual_kernel(slot_ref, prec_ref, phase_ref, out_ref, *scratch):
+    p_scr, landed, table_scr, res_scr = scratch[0:4]
+    me = lax.axis_index("strip")
+    greet_peers(me, pltpu.get_barrier_semaphore())
+    phases = Exchange(me, phase_ref, landed, *scratch[4:7])
+    phases.start()
+    phases.wait()
+    for s in range(PEERS):
+        table_scr[4 * s : 4 * s + 4, :] = landed[s]
+    high, low = split(table_scr[...])
     table = jnp.concatenate([high, low], axis=0)
     batch = 4
     index = lax.broadcasted_iota(jnp.int32, (INNER, batch * INNER), 0)
@@ -625,13 +736,20 @@
         return acc + mm_nt(jnp.concatenate([vh, vl], axis=0), hot)
 
     acc = lax.fori_loop(0, POINT_ROWS // batch, put, jnp.zeros((2 * INNER, INNER), F32), unroll=2)
-    out_ref[...] = acc[0:INNER] + acc[INNER : 2 * INNER]
+    acc = acc[0:INNER] + acc[INNER : 2 * INNER]
+    for s in range(PEERS):
+        res_scr[s] = acc[4 * s : 4 * s + 4]
+    residuals = Exchange(me, res_scr, out_ref, *scratch[7:10])
+    residuals.start()
+    residuals.wait()
 
 
 COPIES = 8
 
 
-def scatter_kernel(sid_ref, cnt_ref, r_ref, w_ref, out_ref, rt_scr, u_scr, *accs):
+def scatter_kernel(
+    sid_ref, cnt_ref, r_ref, w_ref, tw, f_ref, a_ref, m_ref, out_ref, rt_scr, u_scr, y_scr, e_scr, *accs
+):
     def clear(i, carry):
         rows = pl.ds(pl.multiple_of(i * 64, 64), 64)
         for acc in accs:
@@ -672,27 +790,27 @@
         total = accs[0][rows, :]
         for acc in accs[1:]:
             total = total + acc[rows, :]
-        out_ref[rows, :] = total
+        accs[0][rows, :] = total
         return carry
 
     lax.fori_loop(0, SIDE // 64, add, 0)
-
-
-def call(kernel, name, out_shapes, args, smem=0, smem_outs=(), scratch=()):
-    vmem = pl.BlockSpec(memory_space=pltpu.VMEM)
-    small = pl.BlockSpec(memory_space=pltpu.SMEM)
-    outs = [small if i in smem_outs else vmem for i in range(len(out_shapes))]
-    result = pl.pallas_call(
+    row_forward_kernel(True, False, accs[0], tw, f_ref, a_ref, m_ref, out_ref, y_scr, e_scr)
+
+
+def call(kernel, name, out_shapes, args, smem=0, scratch=(), any_args=(), any_outs=(), smem_outs=(), collective_id=None):
+    spaces = [pltpu.SMEM if i < smem else pl.ANY if i in any_args else pltpu.VMEM for i in range(len(args))]
+    outs = [pl.ANY if i in any_outs else pltpu.SMEM if i in smem_outs else pltpu.VMEM for i in range(len(out_shapes))]
+    remote = dict(collective_id=collective_id, has_side_effects=True) if collective_id is not None else {}
+    return pl.pallas_call(
         kernel,
         out_shape=out_shapes,
-        in_specs=[small] * smem + [vmem] * (len(args) - smem),
-        out_specs=outs,
+        in_specs=[pl.BlockSpec(memory_space=space) for space in spaces],
+        out_specs=[pl.BlockSpec(memory_space=space) for space in outs],
         scratch_shapes=list(scratch),
-        compiler_params=pltpu.CompilerParams(vmem_limit_bytes=VMEM_BYTES),
+        compiler_params=pltpu.CompilerParams(vmem_limit_bytes=VMEM_BYTES, **remote),
         cost_estimate=pl.CostEstimate(flops=1024, bytes_accessed=1024, transcendentals=0),
         name=name,
     )(*args)
-    return result
 
 
 def shape(dims, dtype=F32):
@@ -726,103 +844,61 @@
     )[0]
 
 
-def swap_kernel(in_ref, out_ref, send_sem, recv_sem, own_sem):
-    me = lax.axis_index("strip")
-    barrier = pltpu.get_barrier_semaphore()
-
-    def greet(i, carry):
-        peer = lax.rem(me + i, PEERS)
-        pl.semaphore_signal(barrier, inc=1, device_id={"strip": peer}, device_id_type=pl.DeviceIdType.MESH)
-        return carry
-
-    lax.fori_loop(1, PEERS, greet, 0)
-    pl.semaphore_wait(barrier, PEERS - 1)
-
-    def remote(i, row):
-        peer = lax.rem(me + i, PEERS)
-        return pltpu.make_async_remote_copy(
-            src_ref=in_ref.at[peer],
-            dst_ref=out_ref.at[row],
-            send_sem=send_sem.at[i],
-            recv_sem=recv_sem.at[i],
-            device_id={"strip": peer},
-            device_id_type=pl.DeviceIdType.MESH,
-        )
-
-    def start(i, carry):
-        remote(i, me).start()
-        return carry
-
-    lax.fori_loop(1, PEERS, start, 0)
-    own = pltpu.make_async_copy(in_ref.at[me], out_ref.at[me], own_sem)
-    own.start()
-    own.wait()
-
-    def finish(i, carry):
-        copy = remote(i, lax.rem(me + PEERS - i, PEERS))
-        copy.wait_send()
-        copy.wait_recv()
-        return carry
-
-    lax.fori_loop(1, PEERS, finish, 0)
-
-
-def swap(value, collective_id):
-    anywhere = pl.BlockSpec(memory_space=pl.ANY)
-    return pl.pallas_call(
-        swap_kernel,
-        out_shape=shape(value.shape, value.dtype),
-        in_specs=[anywhere],
-        out_specs=anywhere,
-        scratch_shapes=[
-            pltpu.SemaphoreType.DMA((PEERS,)),
-            pltpu.SemaphoreType.DMA((PEERS,)),
-            pltpu.SemaphoreType.DMA,
-        ],
-        compiler_params=pltpu.CompilerParams(collective_id=collective_id, has_side_effects=True),
-        name="swap",
-    )(value)
-
-
 def exchange(value):
     return lax.all_to_all(value, "strip", split_axis=0, concat_axis=0, tiled=True)
 
 
-def amplitude_table(strip):
-    j = jnp.arange(HALF, dtype=jnp.int32)
-    k1 = strip // 2
-    fold = jnp.where(strip % 2 == 0, k1 + OUTER * j, OUTER - k1 + OUTER * j)
-    fold = jnp.where(strip == 1, 16 + OUTER * j, fold)
-    edge = jnp.where((strip == 0) & (j == 0), SIDE // 2, fold)
-    cols = jnp.concatenate([fold, edge]).astype(F32)[None, None, :]
-    kr = jnp.arange(OUTER, dtype=jnp.int32)[:, None] + OUTER * jnp.arange(INNER, dtype=jnp.int32)[None, :]
-    rows = jnp.minimum(kr, SIDE - kr).astype(F32)[:, :, None]
-    radius = (rows * rows + cols * cols) / (KZERO * KZERO)
-    return SIDE / (2.0 * KZERO) * jnp.power(1.0 + radius, -11.0 / 12.0)
-
-
-def signed_columns(strip):
-    j = jnp.arange(HALF, dtype=jnp.int32)
-    k1 = strip // 2
-    cols = jnp.where(strip % 2 == 0, k1 + OUTER * j, k1 + OUTER * (INNER - 1 - j))
-    cols = jnp.where(strip == 1, 16 + OUTER * j, cols)
-    return jnp.concatenate([cols, cols])
-
-
-def phase_tables(wind_row, wind_col, strip, sign):
-    unit = 2.0 * math.pi / SIDE
-    k2 = jnp.arange(INNER, dtype=jnp.int32)[:, None]
-    turn = (OUTER * k2 * wind_row + signed_columns(strip)[None, :] * wind_col) % SIDE
-    angle = turn.astype(F32) * unit
-    small = ((jnp.arange(OUTER, dtype=jnp.int32) * wind_row) % SIDE).astype(F32) * unit
-    return jnp.cos(angle), sign * jnp.sin(angle), jnp.cos(small), sign * jnp.sin(small)
-
-
-def edge_tables(wind_row, sign):
-    k1 = jnp.arange(INNER, dtype=jnp.int32)[None, :] % HALF
-    kr = k1 + OUTER * jnp.arange(INNER, dtype=jnp.int32)[:, None]
-    angle = ((kr * wind_row) % SIDE).astype(F32) * (2.0 * math.pi / SIDE)
-    return [jnp.cos(angle), sign * jnp.sin(angle)]
+def tables_kernel(scale, rate, wind, prior, tab_ref, amp_ref, par_ref):
+    strip = lax.axis_index("strip")
+    live = (lax.axis_index("tm") < 3).astype(F32)
+    k1 = (strip // 2).astype(F32)
+    even = strip % 2 == 0
+    row = lax.broadcasted_iota(jnp.int32, (INNER, INNER), 0)
+    lane = lax.broadcasted_iota(jnp.int32, (INNER, INNER), 1)
+    line = row.astype(F32)
+    j = (lane & (HALF - 1)).astype(F32)
+    cols = jnp.where(even, k1 + OUTER * j, k1 + OUTER * (INNER - 1.0 - j))
+    cols = jnp.where(strip == 1, 16.0 + OUTER * j, cols)
+    winds = ((wind[0, 0].astype(F32), wind[0, 1].astype(F32)), (prior[1], prior[2]))
+
+    def cosine(turns):
+        turns = turns - SIDE * jnp.floor(turns * (1.0 / SIDE))
+        return jnp.cos(turns * (2.0 * math.pi / SIDE))
+
+    small = jnp.zeros((INNER, INNER), F32)
+    for kind in range(4):
+        wind_row, wind_col = winds[kind // 2]
+        quarter = (0.0, 3.0 * SIDE / 4, 0.0, SIDE / 4.0)[kind]
+        base = OUTER * line * wind_row + quarter
+        tab_ref[kind] = cosine(base + cols * wind_col)
+        tab_ref[4 + kind] = cosine(base + j * wind_row)
+        turns = (row & (OUTER - 1)).astype(F32) * wind_row + quarter
+        small = jnp.where(lax.shift_right_logical(row, 5) == kind, turns, small)
+    tab_ref[8] = cosine(small)
+
+    fold = jnp.where(even, k1 + OUTER * j, OUTER - k1 + OUTER * j)
+    fold = jnp.where(strip == 1, 16.0 + OUTER * j, fold)
+    fold = jnp.where(jnp.logical_and(strip == 0, lane == HALF), SIDE / 2.0, fold)
+    fold = fold * fold
+
+    def step(k, carry):
+        kr = line * OUTER + k.astype(F32)
+        kr = jnp.minimum(kr, SIDE - kr)
+        radius = (kr * kr + fold) / (KZERO * KZERO)
+        amp_ref[k] = SIDE / (2.0 * KZERO) * jnp.exp((-11.0 / 12.0) * jnp.log(1.0 + radius))
+        return carry
+
+    lax.fori_loop(0, OUTER, step, 0, unroll=2)
+    norm = scale[0] / (SIDE * SIDE)
+    mine = rate[0] * live
+    par_ref[0] = norm
+    par_ref[1] = mine * scale[0]
+    par_ref[2] = prior[0] * scale[0]
+    par_ref[3] = (mine + prior[0]) * scale[0] * norm
+    par_ref[4] = 1.0 - 2.0 * (wind[0, 1] & 1).astype(F32)
+    par_ref[5] = 1.0 - 2.0 * (prior[2].astype(jnp.int32) & 1).astype(F32)
+    par_ref[6] = 0.0
+    par_ref[7] = 0.0
 
 
 def const(*tables):
@@ -839,8 +915,6 @@
     pierce_weights,
     noise_prec,
 ):
-    strip = lax.axis_index("strip")
-    slot = lax.axis_index("tm")
     fwd, inv, first, first_inv, mid, mid_inv, twiddle = row_tables()
     row_fwd_tables = const(twiddle, pieces(fwd, 2), pieces(first, 2), pieces(mid, 2))
     row_fine_tables = const(twiddle, pieces(fwd, 3), pieces(first, 3), pieces(mid, 3))
@@ -850,41 +924,13 @@
     col_tables = const(pieces(col_fwd, 2), pieces(col_inv, 2))
 
     x = screen_vec[0]
-    scale = prior_scale[0]
     weights = pierce_weights[0].reshape(POINT_ROWS * INNER, INNER)
     target = pierce_point_strip.reshape(POINT_ROWS, INNER)
     block = pierce_block.reshape(POINT_ROWS, INNER)
     prec = noise_prec.reshape(POINT_ROWS, INNER)
 
-    last = lax.axis_size("tm") - 1
-    rate = flow_weight[0] * (slot < last).astype(F32)
-    mine = jnp.stack([rate, wind[0, 0].astype(F32), wind[0, 1].astype(F32)])
-    up_pairs = [(i, i + 1) for i in range(last)]
-    down_pairs = [(i + 1, i) for i in range(last)]
-    prior = lax.ppermute(mine, "tm", up_pairs)
-    back_row, back_col = prior[1].astype(jnp.int32), prior[2].astype(jnp.int32)
-    cu, su, cua, sua = phase_tables(wind[0, 0], wind[0, 1], strip, 1.0)
-    cd, sd, cda, sda = phase_tables(back_row, back_col, strip, -1.0)
-    phases = jnp.stack([cu, su, cd, sd])
-    edge_phases = jnp.stack(edge_tables(wind[0, 0], 1.0) + edge_tables(back_row, -1.0))
-    norm = scale / (SIDE * SIDE)
-    parity_up = jnp.where(wind[0, 1] % 2 == 0, 1.0, -1.0)
-    parity_down = jnp.where(back_col % 2 == 0, 1.0, -1.0)
-    head = jnp.stack(
-        [
-            norm,
-            rate * scale,
-            prior[0] * scale,
-            (rate + prior[0]) * scale * norm,
-            parity_up,
-            parity_down,
-            (strip == 0).astype(F32),
-            jnp.zeros((), F32),
-        ]
-    )
-    scal = jnp.concatenate([head, cua, sua, cda, sda])
-    amp = amplitude_table(strip)
-
+    mine = jnp.concatenate([flow_weight, wind[0].astype(F32)])
+    prior = lax.ppermute(mine, "tm", [(i, i + 1) for i in range(lax.axis_size("tm") - 1)])
     slots, tail = call(
         route_kernel,
         "route",
@@ -892,6 +938,7 @@
         [target, block],
         scratch=[pltpu.VMEM((PEERS * TAIL, INNER), F32)],
     )
+    tail, prior, prec = lax.optimization_barrier((tail, prior, prec))
     sent = call(
         pack_kernel,
         "pack",
@@ -901,64 +948,88 @@
         scratch=[pltpu.VMEM((POINT_ROWS * INNER, INNER), F32), pltpu.VMEM((PEERS * SLOTS, INNER), F32)],
     )[0]
     pencils = exchange(row_forward(x, row_fine_tables, False))
-    pencils, sent = lax.optimization_barrier((pencils, sent))
-    arrived = exchange(sent.reshape(PEERS, GROUP, INNER))
 
     spectral = [pltpu.VMEM(PENCILS, F32), pltpu.VMEM(PENCILS, F32)]
-    screen_pencils, own, up, down = call(
+    message = shape(MESSAGES, BF16)
+    back, own, up, down, arrived, amp, par = call(
         column_first_kernel,
         "column_first",
-        [shape(MESSAGES, BF16), shape(PENCILS), shape(PENCILS, BF16), shape(PENCILS, BF16)],
-        [scal, pencils, amp, phases, edge_phases] + col_fine_tables,
-        smem=1,
-        scratch=spectral,
+        [
+            message,
+            shape(PENCILS),
+            shape(PENCILS, BF16),
+            shape(PENCILS, BF16),
+            shape((PEERS, GROUP, INNER), BF16),
+            shape(PENCILS),
+            shape((8,)),
+        ],
+        [prior_scale, flow_weight, wind, prior, pencils] + col_fine_tables + [sent.reshape(PEERS, GROUP, INNER)],
+        smem=4,
+        any_args=(7,),
+        any_outs=(0, 4),
+        smem_outs=(6,),
+        collective_id=3,
+        scratch=spectral
+        + [pltpu.VMEM(MESSAGES, BF16), pltpu.VMEM((9, INNER, INNER), F32)]
+        + exchange_sems()
+        + exchange_sems(),
     )
-    from_prev = lax.ppermute(up, "tm", up_pairs)
-    from_next = lax.ppermute(down, "tm", down_pairs)
-    screen_pencils, arrived = lax.optimization_barrier((screen_pencils, arrived))
-    tiles = row_backward(swap(screen_pencils, 1), None, row_inv_tables)
     here = arrived.reshape(PEERS * GROUP, INNER)
     digits = arrived[:, SLOTS:, :].astype(F32)
     here_ids = (digits[:, 0:4] * 64.0 + digits[:, 4:8]).astype(jnp.int32).reshape(PEERS * SLOTS)
     here_counts = (digits[:, 8, 0] * 64.0 + digits[:, 9, 0]).astype(jnp.int32)
 
+    rows = [pltpu.VMEM((15 * INNER, 2 * INNER), F32), pltpu.VMEM((2, INNER, INNER), F32)]
+    points = pltpu.VMEM((PEERS * SLOTS, INNER), F32)
+    screen = pltpu.VMEM((SIDE, INNER), F32)
+    small = (PEERS, 4, INNER)
     phase = call(
         gather_kernel,
         "gather",
-        [shape((PEERS, 4, INNER))],
-        [here_ids, here_counts, tiles, here],
+        [shape(small)],
+        [here_ids, here_counts, back, here] + row_inv_tables,
         smem=2,
-        scratch=[pltpu.VMEM((PEERS * SLOTS, INNER), F32)],
+        scratch=[points, screen] + rows,
     )[0]
-    returned = swap(phase, 2).reshape(INNER, INNER)
-    from_prev, from_next, returned = lax.optimization_barrier((from_prev, from_next, returned))
     resid = call(
         residual_kernel,
         "residual",
-        [shape((INNER, INNER))],
-        [slots, prec, returned],
-        scratch=[pltpu.VMEM((POINT_ROWS, INNER), F32)],
+        [shape(small)],
+        [slots, prec, phase],
+        collective_id=2,
+        scratch=[
+            pltpu.VMEM((POINT_ROWS, INNER), F32),
+            pltpu.VMEM(small, F32),
+            pltpu.VMEM((INNER, INNER), F32),
+            pltpu.VMEM(small, F32),
+        ]
+        + exchange_sems()
+        + exchange_sems(),
     )[0]
-    resid_here = swap(resid.reshape(PEERS, 4, INNER), 2).reshape(INNER, INNER)
-    gradient = call(
+    pencils = call(
         scatter_kernel,
         "scatter",
-        [shape((SIDE, INNER))],
-        [here_ids, here_counts, resid_here, here],
+        [message],
+        [here_ids, here_counts, resid.reshape(INNER, INNER), here] + row_fwd_tables,
         smem=2,
-        scratch=[pltpu.VMEM((INNER, INNER), F32), pltpu.VMEM((PEERS * SLOTS, INNER), F32)]
-        + [pltpu.VMEM((SIDE, INNER), F32)] * COPIES,
+        scratch=[pltpu.VMEM((INNER, INNER), F32), points] + rows + [screen] * COPIES,
     )[0]
-    pencils = swap(row_forward(gradient, row_fwd_tables, True), 1)
     out_pencils = call(
         column_second_kernel,
         "column_second",
-        [shape(MESSAGES, BF16)],
-        [scal, pencils, amp, own, from_prev, from_next] + col_tables,
+        [message],
+        [par, pencils, amp, own, up, down] + col_tables,
         smem=1,
-        scratch=spectral,
+        any_args=(1, 4, 5),
+        any_outs=(0,),
+        collective_id=1,
+        scratch=spectral
+        + [pltpu.VMEM(MESSAGES, BF16), pltpu.VMEM(PENCILS, BF16), pltpu.VMEM(PENCILS, BF16)]
+        + [pltpu.SemaphoreType.DMA((2, 2, SIDE_PARTS))]
+        + exchange_sems()
+        + exchange_sems(),
     )[0]
-    return row_backward(swap(out_pencils, 1), x, row_inv_tables)[None]
+    return row_backward(out_pencils, x, row_inv_tables)[None]
 
 
 def solution(mesh):

time: 324 us -> 313 us (0.966)
  Pallas kernels: 263 us -> 290 us
  starting transfers between devices: 36.7 us -> 14.8 us
  other arithmetic: 10.1 us -> 2.91 us
  between operations: 7.75 us -> 1.4 us
    pallas_call x16 -> x9, Pallas kernels: 263 us -> 290 us  [call(): pl.pallas_call(kernel, out_shape=out_shapes, in_specs=[pl.BlockSpec(memor...]
    ppermute x3 -> x1, starting transfers between devices: 16 us -> 3.48 us  [local(): lax.ppermute(mine, 'tm', [(i, i + 1) for i in range(lax.axis_size('tm') -...]
    all_to_all x2 -> x1, starting transfers between devices: 20.7 us -> 11.3 us  [exchange(): lax.all_to_all(value, 'strip', split_axis=0, concat_axis=0, tiled=True)]
  transfers between devices with their start and end apart: 5 -> 2, of which waited for: 0 -> 0; matrix products, arithmetic and copies ran while one was open for 4% -> 1% of each run, Pallas kernels for 40% -> 6%
where the time goes in v3:
time: 313 us; the launch traced here: 312 us
  Pallas kernels  290 us (93%)
  starting transfers between devices  14.8 us (5%)
  local copies, waits for them, and re-layouts  3.36 us (1%)
    pallas_call x9, Pallas kernels, call(): pl.pallas_call(kernel, out_shape=out_shapes, in_specs=[pl.BlockSpec(memor...  290 us
    all_to_all x1, starting transfers between devices, exchange(): lax.all_to_all(value, 'strip', split_axis=0, concat_axis=0, tiled=True)  11.3 us
  transfers between devices with their start and end apart: 2, of which 0 were waited for; matrix products, arithmetic and copies ran while one was open for 1% of the time, Pallas kernels for 6%

profile of v3, /device:TPU:1, one launch (start us, length us, event | category | flops | bytes accessed | tf_op | source)
XLA Modules:
  0.0 312.2 jit_solution(1909311968843925318)
XLA Ops:
  0.0 7.8 %row_forward.1 = bf16[32,144,128]{2,1,0:T(8,128)(2,1)} custom-call(f32[128,4096]{1,0:T(8,128)} %bitcast.17, f32[2,16,128]{2,1,0:T(8,128)} %constant.13.clone.refs_1_.tw.refs_2_, bf16[3,256,256]{2,1,0:T(8,128)(2,1)} %constant.33.clone.refs_2_, bf16[3,128,128]{2,1,0:T(8,128)(2,1)} %constant.34.clone.refs_3_, bf16[3,128,128]{2,1,0:T(8,128)(2,1)} %constant.35.clone.refs_4_), custom_call_target="tpu_custom_call" | custom-call | flops 1024 | bytes 1024 | tf_op jit(solution)/shard_map/row_forward/pallas_call | solution.py:804
  7.8 11.3 %all-to-all-start = ((bf16[32,144,128]{2,1,0:T(8,128)(2,1)}), bf16[32,144,128]{2,1,0:T(8,128)(2,1)S(1)}, u32[]{:S(2)}, u32[]{:S(2)}) async-start(bf16[32,144,128]{2,1,0:T(8,128)(2,1)} %row_forward.1), calls=%async_computation | async-start | bytes 2359296 | tf_op jit(solution)/shard_map/all_to_all | solution.py:848
  19.8 0.1 copy.26
  19.9 0.7 reshape.29.t_ref
  20.5 0.1 copy.27
  20.6 0.7 reshape.30.id_ref
  21.3 0.1 pad_maximum_fusion
  21.4 3.5 %collective-permute-start = (f32[3]{0:T(128)S(1)}, f32[3]{0:T(128)S(1)}, u32[]{:S(2)}, u32[]{:S(2)}) collective-permute-start(f32[3]{0:T(128)S(1)} %pad_maximum_fusion), channel_id=1, source_target_pairs={{0,32},{32,64},{64,96},{1,33},{33,65},{65,97},{2,34},{34,66},{66,9... | collective-permute-start | bytes 44 | tf_op jit(solution)/shard_map/ppermute | solution.py:933
  24.9 4.6 %route.1 = (s32[64,128]{1,0:T(8,128)}, bf16[512,128]{1,0:T(8,128)(2,1)}) custom-call(s32[64,128]{1,0:T(8,128)} %reshape.29.t_ref, s32[64,128]{1,0:T(8,128)} %reshape.30.id_ref), custom_call_target="tpu_custom_call" | custom-call | flops 1024 | bytes 1024 | tf_op jit(solution)/shard_map/route/pallas_call | solution.py:804
  30.2 0.1 copy.28
  30.3 0.7 reshape.31.prec_ref
  31.0 0.0 collective-permute-done.prior
  31.0 14.1 %pack.1 = bf16[16896,128]{1,0:T(8,128)(2,1)} custom-call(s32[8192]{0:T(1024)} %bitcast.23, bf16[8192,128]{1,0:T(8,128)(2,1)} %bitcast.19, bf16[512,128]{1,0:T(8,128)(2,1)} %get-tuple-element.20.tail_ref), custom_call_target="tpu_custom_call" | custom-call | flops 1024 | bytes 1024 | tf_op jit(solution)/shard_map/pack/pallas_call | solution.py:804
  45.1 0.0 all-to-all-done.in_ref
  45.1 1.0 copy-done
  46.1 97.3 %column_first.1 = (bf16[32,144,128]{2,1,0:T(8,128)(2,1)}, f32[32,128,128]{2,1,0:T(8,128)}, bf16[32,128,128]{2,1,0:T(8,128)(2,1)}, bf16[32,128,128]{2,1,0:T(8,128...) custom-call(f32[1]{0:T(128)S(6)} %copy.29.scale, f32[1]{0:T(128)S(6)} %copy.30.rate, ...), custom_call_target="tpu_custom_call" | custom-call | flops 1024 | bytes 1024 | tf_op jit(solution)/shard_map/column_first/pallas_call | solution.py:804
  143.4 0.9 slice_convert_fusion
  144.3 1.2 fusion.2.cnt_ref
  145.6 0.7 fusion
  146.2 18.7 %gather.1.phase_ref = f32[32,4,128]{2,1,0:T(4,128)} custom-call(s32[16384]{0:T(1024)} %bitcast.20, s32[32]{0:T(128)} %fusion.2.cnt_ref, bf16[32,144,128]{2,1,0:T(8,128)(2,1)} %get-tuple-element.24.in_ref, bf16[16896,128]{1,0:T(8,128)(2,1)} %bitcast.14, f32[2,16,128]{2,1,0:T(8,128)} %constant.13.clone.refs_1_.tw.refs_2_, ...), custom_call_target="tpu_custom_call" | custom-call | flops 1024 | bytes 1024 | tf_op jit(solution)/shard_map/gather/pallas_call | solution.py:804
  165.0 35.4 %residual.1 = f32[32,4,128]{2,1,0:T(4,128)} custom-call(s32[64,128]{1,0:T(8,128)} %get-tuple-element.19.slot_ref, f32[64,128]{1,0:T(8,128)} %reshape.31.prec_ref, f32[32,4,128]{2,1,0:T(4,128)} %gather.1.phase_ref), custom_call_target="tpu_custom_call" | custom-call | flops 1024 | bytes 1024 | tf_op jit(solution)/shard_map/residual/pallas_call | solution.py:804
  200.3 21.1 %scatter.1.in_ref = bf16[32,144,128]{2,1,0:T(8,128)(2,1)} custom-call(s32[16384]{0:T(1024)} %bitcast.21, s32[32]{0:T(128)} %fusion.2.cnt_ref, f32[128,128]{1,0:T(8,128)} %bitcast.22, bf16[16896,128]{1,0:T(8,128)(2,1)} %bitcast.15, f32[2,16,128]{2,1,0:T(8,128)} %constant.13.clone.refs_1_.tw.refs_2_, bf16[2,256,256]{2,1,0:T(8,128)(2,1)} %constant.30.clone.f_ref, ...), custom_call_target="tpu_custom_call" | custom-call | flops 1024 | bytes 1024 | tf_op jit(solution)/shard_map/scatter/pallas_call | solution.py:804
  221.5 83.8 %column_second.1.refs_0_ = bf16[32,144,128]{2,1,0:T(8,128)(2,1)} custom-call(f32[8]{0:T(128)} %get-tuple-element.21.par, bf16[32,144,128]{2,1,0:T(8,128)(2,1)} %scatter.1.in_ref, f32[32,128,128]{2,1,0:T(8,128)} %get-tuple-element.25.amp_ref, f32[32,128,128]{2,1,0:T(8,128)} %get-tuple-element.26.own_ref, bf16[32,128,128]{2,1,0:T(8,128)(2,1)} %get-tuple-element.27.up_ref, ...), custom_call_target="tpu_custom_call" | custom-call | flops 1024 | bytes 1024 | tf_op jit(solution)/shard_map/column_second/pallas_call | solution.py:804
  305.3 6.8 %row_backward.1 = f32[128,4096]{1,0:T(8,128)} custom-call(bf16[32,144,128]{2,1,0:T(8,128)(2,1)} %column_second.1.refs_0_, f32[128,4096]{1,0:T(8,128)} %bitcast.18, f32[2,16,128]{2,1,0:T(8,128)} %constant.13.clone.refs_1_.tw.refs_2_, bf16[2,256,256]{2,1,0:T(8,128)(2,1)} %constant.36.clone.f_ref.refs_3_, bf16[2,128,128]{2,1,0:T(8,128)(2,1)} %constant.37.clone.a_ref.refs_4_, ...), custom_call_target="tpu_custom_call" | custom-call | flops 1024 | bytes 1024 | tf_op jit(solution)/shard_map/row_backward/pallas_call | solution.py:804
  (12 shorter events, 0.0 us)
Async XLA Ops:
  7.8 12.0 %copy-start.1 = (s32[1,128,64,1]{1,3,2,0:T(1,128)S(1)}, s32[1,128,64,1]{1,3,2,0:T(1,128)}, u32[]{:S(2)}) copy-start(s32[1,128,64,1]{1,3,2,0:T(1,128)} %param.26) | copy-start | bytes 98308
  7.8 12.8 %copy-start.2 = (s32[1,128,64]{1,2,0:T(8,128)S(1)}, s32[1,128,64]{1,2,0:T(8,128)}, u32[]{:S(2)}) copy-start(s32[1,128,64]{1,2,0:T(8,128)} %param.27) | copy-start | bytes 98308
  7.8 13.6 %copy-start.4 = (s32[1,2]{1,0:T(1,128)S(1)}, s32[1,2]{1,0:T(1,128)}, u32[]{:S(2)}) copy-start(s32[1,2]{1,0:T(1,128)} %wind.1) | copy-start | bytes 28
  7.8 22.4 %copy-start.3 = (f32[1,128,64]{1,2,0:T(8,128)S(1)}, f32[1,128,64]{1,2,0:T(8,128)}, u32[]{:S(2)}) copy-start(f32[1,128,64]{1,2,0:T(8,128)} %param.29) | copy-start | bytes 98308
  7.8 37.3 %all-to-all-start = ((bf16[32,144,128]{2,1,0:T(8,128)(2,1)}), bf16[32,144,128]{2,1,0:T(8,128)(2,1)S(1)}, u32[]{:S(2)}, u32[]{:S(2)}) async-start(bf16[32,144,128]{2,1,0:T(8,128)(2,1)} %row_forward.1), calls=%async_computation | async-start | bytes 2359296 | tf_op jit(solution)/shard_map/all_to_all | solution.py:848
  21.4 9.6 %collective-permute-start = (f32[3]{0:T(128)S(1)}, f32[3]{0:T(128)S(1)}, u32[]{:S(2)}, u32[]{:S(2)}) collective-permute-start(f32[3]{0:T(128)S(1)} %pad_maximum_fusion), channel_id=1, source_target_pairs={{0,32},{32,64},{64,96},{1,33},{33,65},{65,97},{2,34},{34,66},{66,9... | collective-permute-start | bytes 44 | tf_op jit(solution)/shard_map/ppermute | solution.py:933
  31.0 14.1 %copy-start.5 = (f32[3]{0:T(128)}, f32[3]{0:T(128)S(1)}, u32[]{:S(2)}) copy-start(f32[3]{0:T(128)S(1)} %collective-permute-done.prior) | copy-start | bytes 40
  45.1 1.0 copy-start

commit v4 on v3

--- a/solution.py
+++ b/solution.py
@@ -18,7 +18,8 @@
 SLOTS = 512
 POINT_ROWS = 64
 TAIL = 16
-GROUP = SLOTS + TAIL
+ID_ROWS = 8
+ID_STRIDE = ID_ROWS * 128
 VMEM_BYTES = 56 * 1024 * 1024
 F32 = jnp.float32
 BF16 = jnp.bfloat16
@@ -373,13 +374,14 @@
     def peer(self, i):
         return lax.rem(self.me + 1 + lax.rem(i + 2 * self.me, PEERS - 1), PEERS)
 
-    def start(self):
+    def start(self, first=0, last=PEERS - 1):
         def step(i, carry):
             self.copy(self.peer(i), i, self.me).start()
             return carry
 
-        lax.fori_loop(0, PEERS - 1, step, 0)
-        self.own.start()
+        lax.fori_loop(first, last, step, 0)
+        if first == 0:
+            self.own.start()
 
     def wait(self):
         def step(i, carry):
@@ -442,17 +444,27 @@
     return c * value + s * (pltpu.roll(value, HALF, 1) * flip)
 
 
+EARLY = 8
+
+
 def column_first_kernel(
-    scale, rate, wind, prior, in_ref, ef, ei, sent_ref,
-    back_ref, own_ref, up_ref, down_ref, here_ref, amp_ref, par, *scratch,
+    scale, rate, wind, prior, x_ref, tw, f_ref, a_ref, m_ref, ef, ei, sent_ref, ids_ref,
+    back_ref, own_ref, up_ref, down_ref, here_ref, here_ids_ref, amp_ref, par, *scratch,
 ):
-    y_scr, z_scr, msg_scr, tab_ref = scratch[0:4]
+    y_scr, z_scr, msg_scr, land_scr, tab_ref, row_scr, row_edge = scratch[0:7]
     me = lax.axis_index("strip")
     greet_peers(me, pltpu.get_barrier_semaphore())
-    weights = Exchange(me, sent_ref, here_ref, *scratch[4:7])
-    weights.start()
+    ids = Exchange(me, ids_ref, here_ids_ref, *scratch[7:10])
+    weights = Exchange(me, sent_ref, here_ref, *scratch[10:13])
+    pencils = Exchange(me, msg_scr, land_scr, *scratch[13:16])
+    ids.start()
+    weights.start(0, EARLY)
+    row_forward_kernel(False, True, x_ref, tw, f_ref, a_ref, m_ref, msg_scr, row_scr, row_edge)
+    pencils.start()
+    weights.start(EARLY)
     tables_kernel(scale, rate, wind, prior, tab_ref, amp_ref, par)
-    take_all(in_ref, z_scr, True)
+    pencils.wait()
+    take_all(land_scr, z_scr, True)
     column_first_step(z_scr, y_scr, -1.0)
     flip = flip_lanes(INNER)
 
@@ -503,39 +515,20 @@
     lax.fori_loop(0, OUTER, inverse, 0, unroll=8)
     column_first_step(z_scr, y_scr, 1.0)
     give_all(y_scr, msg_scr)
-    back = Exchange(me, msg_scr, back_ref, *scratch[7:10])
+    back = Exchange(me, msg_scr, back_ref, *scratch[16:19])
     back.start()
+    ids.wait()
     back.wait()
     weights.wait()
 
 
-SIDE_PARTS = 4
-
-
-def column_second_kernel(par, in_ref, amp_ref, own_ref, up_ref, down_ref, ef, ei, back_ref, *scratch):
-    y_scr, z_scr, msg_scr, prev_ref, next_ref, side_sems = scratch[0:6]
+def column_second_kernel(par, in_ref, amp_ref, own_ref, prev_ref, next_ref, ef, ei, back_ref, *scratch):
+    y_scr, z_scr, msg_scr = scratch[0:3]
     me = lax.axis_index("strip")
     slot_at = lax.axis_index("tm")
-    above, below = lax.rem(slot_at + 1, 4), lax.rem(slot_at + 3, 4)
-    greet_peers(me, pltpu.get_barrier_semaphore(), ({"tm": above}, {"tm": below}))
-    pencils = Exchange(me, in_ref, msg_scr, *scratch[6:9])
+    greet_peers(me, pltpu.get_barrier_semaphore())
+    pencils = Exchange(me, in_ref, msg_scr, *scratch[3:6])
     pencils.start()
-    sides = []
-    for p in range(SIDE_PARTS):
-        rows = pl.ds(p * (OUTER // SIDE_PARTS), OUTER // SIDE_PARTS)
-        for n, (src, dst, device) in enumerate(((up_ref, prev_ref, above), (down_ref, next_ref, below))):
-            sides.append(
-                pltpu.make_async_remote_copy(
-                    src_ref=src.at[rows],
-                    dst_ref=dst.at[rows],
-                    send_sem=side_sems.at[0, n, p],
-                    recv_sem=side_sems.at[1, n, p],
-                    device_id={"tm": device},
-                    device_id_type=MESH,
-                )
-            )
-    for side in sides:
-        side.start()
     pencils.wait()
     take_all(msg_scr, z_scr, False)
     column_first_step(z_scr, y_scr, -1.0)
@@ -564,23 +557,21 @@
 
         lax.fori_loop(0, OUTER, put, 0, unroll=4)
 
-    for side in sides:
-        side.wait()
-
     def inverse(k1, carry):
-        moved = prev_ref[k1].astype(F32) + next_ref[k1].astype(F32)
+        moved = jnp.where(slot_at > 0, prev_ref[k1].astype(F32), 0.0)
+        moved = moved + jnp.where(slot_at < 3, next_ref[k1].astype(F32), 0.0)
         z_scr[k1] = apply_packed(ei, k1, z_scr[k1] - par[0] * moved, flip)
         return carry
 
     lax.fori_loop(0, OUTER, inverse, 0, unroll=8)
     column_first_step(z_scr, y_scr, 1.0)
     give_all(y_scr, msg_scr)
-    back = Exchange(me, msg_scr, back_ref, *scratch[9:12])
+    back = Exchange(me, msg_scr, back_ref, *scratch[6:9])
     back.start()
     back.wait()
 
 
-def route_kernel(t_ref, id_ref, slot_ref, tail_ref, tail_scr):
+def route_kernel(t_ref, id_ref, slot_ref, tail_ref):
     row = lax.broadcasted_iota(jnp.int32, (INNER, 2 * INNER), 0)
     col = lax.broadcasted_iota(jnp.int32, (INNER, 2 * INNER), 1)
     tri = jnp.where(jnp.logical_or(row < col, col >= INNER), 1.0, 0.0).astype(BF16)
@@ -613,62 +604,54 @@
         return acc + mm_nt(jnp.concatenate(v, axis=0), hot)
 
     acc = lax.fori_loop(0, POINT_ROWS // batch, put, jnp.zeros((2 * INNER, INNER), F32), unroll=2)
+    ids = (acc[0:INNER] * 64.0 + acc[INNER : 2 * INNER]).astype(jnp.int32)
     count = base.astype(jnp.int32)
-    count_high = lax.shift_right_logical(count, 6).astype(F32)
-    count_low = (count & 63).astype(F32)
-    tail_scr[...] = jnp.zeros_like(tail_scr)
+    tail_ref[...] = jnp.zeros_like(tail_ref)
     for s in range(PEERS):
-        tail_scr[s * TAIL : s * TAIL + 4, :] = acc[4 * s : 4 * s + 4]
-        tail_scr[s * TAIL + 4 : s * TAIL + 8, :] = acc[INNER + 4 * s : INNER + 4 * s + 4]
-        tail_scr[s * TAIL + 8 : s * TAIL + 9, :] = count_high[s : s + 1]
-        tail_scr[s * TAIL + 9 : s * TAIL + 10, :] = count_low[s : s + 1]
-    tail_ref[...] = tail_scr[...].astype(BF16)
-
-
-def pack_kernel(slot_ref, w_ref, tail_ref, out_ref, w_scr, buf):
-    def clear(i, carry):
+        tail_ref[s, 0:4, :] = ids[4 * s : 4 * s + 4]
+        tail_ref[s, 4:5, :] = count[s : s + 1]
+
+
+def pack_kernel(slot_ref, w_ref, out_ref, w_scr, buf):
+    def widen(i, carry):
         rows = pl.ds(pl.multiple_of(i * 64, 64), 64)
-        buf[rows, :] = jnp.zeros((64, INNER), F32)
-        buf[pl.ds(pl.multiple_of(i * 64 + PEERS * SLOTS // 2, 64), 64), :] = jnp.zeros((64, INNER), F32)
         w_scr[rows, :] = w_ref[rows, :].astype(F32)
         return carry
 
-    lax.fori_loop(0, PEERS * SLOTS // INNER, clear, 0)
+    lax.fori_loop(0, POINT_ROWS * INNER // 64, widen, 0, unroll=2)
 
     def some(q, carry):
-        first = q * 16
-        slots = [slot_ref[first + j] for j in range(16)]
-        rows = [w_scr[pl.ds(first + j, 1), :] for j in range(16)]
-        for j in range(16):
+        first = q * 32
+        slots = [slot_ref[first + j] for j in range(32)]
+        rows = [w_scr[pl.ds(first + j, 1), :] for j in range(32)]
+        for j in range(32):
             buf[pl.ds(slots[j], 1), :] = rows[j]
         return carry
 
-    lax.fori_loop(0, POINT_ROWS * INNER // 16, some, 0)
-
-    def narrow(d, carry):
-        for i in range(4):
-            rows = pl.ds(pl.multiple_of(d * SLOTS + i * INNER, INNER), INNER)
-            out_ref[pl.ds(pl.multiple_of(d * GROUP + i * INNER, TAIL), INNER), :] = buf[rows, :].astype(BF16)
-        tail = tail_ref[pl.ds(pl.multiple_of(d * TAIL, TAIL), TAIL), :]
-        out_ref[pl.ds(pl.multiple_of(d * GROUP + SLOTS, TAIL), TAIL), :] = tail
-        return carry
-
-    lax.fori_loop(0, PEERS, narrow, 0)
-
-
-def gather_kernel(sid_ref, cnt_ref, in_ref, w_ref, tw, f_ref, a_ref, m_ref, out_ref, g_scr, tiles_ref, z_scr, e_scr):
+    lax.fori_loop(0, POINT_ROWS * INNER // 32, some, 0)
+
+    def narrow(i, carry):
+        rows = pl.ds(pl.multiple_of(i * INNER, INNER), INNER)
+        out_ref[rows, :] = buf[rows, :].astype(BF16)
+        return carry
+
+    lax.fori_loop(0, PEERS * SLOTS // INNER, narrow, 0, unroll=2)
+
+
+def gather_kernel(sid_ref, in_ref, w_ref, tw, f_ref, a_ref, m_ref, out_ref, g_scr, tiles_ref, z_scr, e_scr):
     row_backward_kernel(False, in_ref, tw, f_ref, a_ref, m_ref, tiles_ref, z_scr, e_scr)
 
     def source(s, carry):
         def some(q, inner):
             first = s * SLOTS + q * 16
-            ids = [sid_ref[first + j] for j in range(16)]
+            line = s * ID_STRIDE + q * 16
+            ids = [sid_ref[line + j] for j in range(16)]
             rows = [tiles_ref[pl.ds(ids[j], 1), :] for j in range(16)]
             for j in range(16):
                 g_scr[pl.ds(first + j, 1), :] = rows[j]
             return inner
 
-        return lax.fori_loop(0, lax.shift_right_logical(cnt_ref[s] + 15, 4), some, carry)
+        return lax.fori_loop(0, lax.shift_right_logical(sid_ref[s * ID_STRIDE + SLOTS] + 15, 4), some, carry)
 
     lax.fori_loop(0, PEERS, source, 0)
     ones = jnp.ones((2 * INNER, INNER), BF16)
@@ -677,25 +660,57 @@
     place = lax.broadcasted_iota(jnp.int32, (1, INNER), 1)
 
     def total(s, carry):
-        w = w_ref[pl.ds(pl.multiple_of(s * GROUP, TAIL), SLOTS), :].astype(F32)
+        count = sid_ref[s * ID_STRIDE + SLOTS]
+        w = w_ref[pl.ds(pl.multiple_of(s * SLOTS, SLOTS), SLOTS), :].astype(F32)
         g = g_scr[pl.ds(pl.multiple_of(s * SLOTS, SLOTS), SLOTS), :]
         sums = mm(jnp.concatenate(split(g * w), axis=1), ones)
         for q in range(4):
             got = jnp.where(diagonal, sums[q * INNER : (q + 1) * INNER], 0.0)
             got = jnp.sum(got, axis=0, keepdims=True)
-            out_ref[s, q : q + 1, :] = jnp.where(place + q * INNER < cnt_ref[s], got, 0.0)
+            out_ref[s, q : q + 1, :] = jnp.where(place + q * INNER < count, got, 0.0)
         return carry
 
     lax.fori_loop(0, PEERS, total, 0, unroll=2)
 
 
-def residual_kernel(slot_ref, prec_ref, phase_ref, out_ref, *scratch):
+SIDE_PARTS = 4
+
+
+def residual_kernel(slot_ref, prec_ref, phase_ref, up_ref, down_ref, out_ref, prev_ref, next_ref, *scratch):
     p_scr, landed, table_scr, res_scr = scratch[0:4]
     me = lax.axis_index("strip")
-    greet_peers(me, pltpu.get_barrier_semaphore())
+    side_sems = scratch[10]
+    slot_at = lax.axis_index("tm")
+    above, below = lax.rem(slot_at + 1, 4), lax.rem(slot_at + 3, 4)
+    greet_peers(me, pltpu.get_barrier_semaphore(), ({"tm": above}, {"tm": below}))
+
+    def sides(n):
+        src, dst, device = ((up_ref, prev_ref, above), (down_ref, next_ref, below))[n]
+        for p in range(SIDE_PARTS):
+            rows = pl.ds(p * (OUTER // SIDE_PARTS), OUTER // SIDE_PARTS)
+            yield pltpu.make_async_remote_copy(
+                src_ref=src.at[rows],
+                dst_ref=dst.at[rows],
+                send_sem=side_sems.at[0, n, p],
+                recv_sem=side_sems.at[1, n, p],
+                device_id={"tm": device},
+                device_id_type=MESH,
+            )
+
     phases = Exchange(me, phase_ref, landed, *scratch[4:7])
     phases.start()
     phases.wait()
+
+    @pl.when(slot_at < 3)
+    def _():
+        for side in sides(0):
+            side.start()
+
+    @pl.when(slot_at > 0)
+    def _():
+        for side in sides(1):
+            side.start()
+
     for s in range(PEERS):
         table_scr[4 * s : 4 * s + 4, :] = landed[s]
     high, low = split(table_scr[...])
@@ -743,12 +758,24 @@
     residuals.start()
     residuals.wait()
 
+    @pl.when(slot_at < 3)
+    def _():
+        for up, down in zip(sides(0), sides(1)):
+            up.wait_send()
+            down.wait_recv()
+
+    @pl.when(slot_at > 0)
+    def _():
+        for up, down in zip(sides(0), sides(1)):
+            up.wait_recv()
+            down.wait_send()
+
 
 COPIES = 8
 
 
 def scatter_kernel(
-    sid_ref, cnt_ref, r_ref, w_ref, tw, f_ref, a_ref, m_ref, out_ref, rt_scr, u_scr, y_scr, e_scr, *accs
+    sid_ref, r_ref, w_ref, tw, f_ref, a_ref, m_ref, out_ref, rt_scr, u_scr, y_scr, e_scr, *accs
 ):
     def clear(i, carry):
         rows = pl.ds(pl.multiple_of(i * 64, 64), 64)
@@ -759,13 +786,14 @@
     lax.fori_loop(0, SIDE // 64, clear, 0)
     rt_scr[...] = r_ref[...].T
     lane = lax.broadcasted_iota(jnp.int32, (INNER, INNER), 1)
+    row = lax.broadcasted_iota(jnp.int32, (INNER, INNER), 0)
 
     def scaled(s, carry):
         for q in range(4):
             col = jnp.sum(jnp.where(lane == s * 4 + q, rt_scr[...], 0.0), axis=1, keepdims=True)
-            base = pl.multiple_of(s * GROUP + q * INNER, TAIL)
             rows = pl.ds(pl.multiple_of(s * SLOTS + q * INNER, INNER), INNER)
-            u_scr[rows, :] = w_ref[pl.ds(base, INNER), :].astype(F32) * col
+            used = row + q * INNER < sid_ref[s * ID_STRIDE + SLOTS]
+            u_scr[rows, :] = jnp.where(used, w_ref[rows, :].astype(F32) * col, 0.0)
         return carry
 
     lax.fori_loop(0, PEERS, scaled, 0, unroll=2)
@@ -773,7 +801,8 @@
     def source(s, carry):
         def some(q, inner):
             first = s * SLOTS + q * 16
-            ids = [sid_ref[first + j] for j in range(16)]
+            line = s * ID_STRIDE + q * 16
+            ids = [sid_ref[line + j] for j in range(16)]
             us = [u_scr[pl.ds(first + j, 1), :] for j in range(16)]
             for h in range(0, 16, COPIES):
                 sums = [accs[j][pl.ds(ids[h + j], 1), :] + us[h + j] for j in range(COPIES)]
@@ -781,7 +810,7 @@
                     accs[j][pl.ds(ids[h + j], 1), :] = sums[j]
             return inner
 
-        return lax.fori_loop(0, lax.shift_right_logical(cnt_ref[s] + 15, 4), some, carry)
+        return lax.fori_loop(0, lax.shift_right_logical(sid_ref[s * ID_STRIDE + SLOTS] + 15, 4), some, carry)
 
     lax.fori_loop(0, PEERS, source, 0)
 
@@ -821,17 +850,6 @@
 MESSAGES = (PEERS, INNER + TAIL, INNER)
 
 
-def row_forward(x, tables, tiled):
-    args = [x] + tables
-    return call(
-        lambda *refs: row_forward_kernel(tiled, not tiled, *refs),
-        "row_forward",
-        [shape(MESSAGES, BF16)],
-        args,
-        scratch=[pltpu.VMEM((15 * INNER, 2 * INNER), F32), pltpu.VMEM((2, INNER, INNER), F32)],
-    )[0]
-
-
 def row_backward(pencils, base, tables):
     final = base is not None
     args = [pencils] + ([base] if final else []) + tables
@@ -842,10 +860,6 @@
         args,
         scratch=[pltpu.VMEM((15 * INNER, 2 * INNER), F32), pltpu.VMEM((2, INNER, INNER), F32)],
     )[0]
-
-
-def exchange(value):
-    return lax.all_to_all(value, "strip", split_axis=0, concat_axis=0, tiled=True)
 
 
 def tables_kernel(scale, rate, wind, prior, tab_ref, amp_ref, par_ref):
@@ -931,27 +945,26 @@
 
     mine = jnp.concatenate([flow_weight, wind[0].astype(F32)])
     prior = lax.ppermute(mine, "tm", [(i, i + 1) for i in range(lax.axis_size("tm") - 1)])
-    slots, tail = call(
+    slots, ids = call(
         route_kernel,
         "route",
-        [shape((POINT_ROWS, INNER), jnp.int32), shape((PEERS * TAIL, INNER), BF16)],
+        [shape((POINT_ROWS, INNER), jnp.int32), shape((PEERS, ID_ROWS, INNER), jnp.int32)],
         [target, block],
-        scratch=[pltpu.VMEM((PEERS * TAIL, INNER), F32)],
     )
-    tail, prior, prec = lax.optimization_barrier((tail, prior, prec))
+    ids, prior, prec = lax.optimization_barrier((ids, prior, prec))
     sent = call(
         pack_kernel,
         "pack",
-        [shape((PEERS * GROUP, INNER), BF16)],
-        [slots.reshape(-1), weights, tail],
+        [shape((PEERS * SLOTS, INNER), BF16)],
+        [slots.reshape(-1), weights],
         smem=1,
         scratch=[pltpu.VMEM((POINT_ROWS * INNER, INNER), F32), pltpu.VMEM((PEERS * SLOTS, INNER), F32)],
     )[0]
-    pencils = exchange(row_forward(x, row_fine_tables, False))
 
     spectral = [pltpu.VMEM(PENCILS, F32), pltpu.VMEM(PENCILS, F32)]
+    rows = [pltpu.VMEM((15 * INNER, 2 * INNER), F32), pltpu.VMEM((2, INNER, INNER), F32)]
     message = shape(MESSAGES, BF16)
-    back, own, up, down, arrived, amp, par = call(
+    back, own, up, down, arrived, here_ids, amp, par = call(
         column_first_kernel,
         "column_first",
         [
@@ -959,27 +972,28 @@
             shape(PENCILS),
             shape(PENCILS, BF16),
             shape(PENCILS, BF16),
-            shape((PEERS, GROUP, INNER), BF16),
+            shape((PEERS, SLOTS, INNER), BF16),
+            shape((PEERS, ID_ROWS, INNER), jnp.int32),
             shape(PENCILS),
             shape((8,)),
         ],
-        [prior_scale, flow_weight, wind, prior, pencils] + col_fine_tables + [sent.reshape(PEERS, GROUP, INNER)],
+        [prior_scale, flow_weight, wind, prior, x]
+        + row_fine_tables
+        + col_fine_tables
+        + [sent.reshape(PEERS, SLOTS, INNER), ids],
         smem=4,
-        any_args=(7,),
-        any_outs=(0, 4),
-        smem_outs=(6,),
+        any_args=(11, 12),
+        any_outs=(0, 4, 5),
+        smem_outs=(7,),
         collective_id=3,
         scratch=spectral
-        + [pltpu.VMEM(MESSAGES, BF16), pltpu.VMEM((9, INNER, INNER), F32)]
-        + exchange_sems()
-        + exchange_sems(),
+        + [pltpu.VMEM(MESSAGES, BF16), pltpu.VMEM(MESSAGES, BF16), pltpu.VMEM((9, INNER, INNER), F32)]
+        + rows
+        + exchange_sems() * 4,
     )
-    here = arrived.reshape(PEERS * GROUP, INNER)
-    digits = arrived[:, SLOTS:, :].astype(F32)
-    here_ids = (digits[:, 0:4] * 64.0 + digits[:, 4:8]).astype(jnp.int32).reshape(PEERS * SLOTS)
-    here_counts = (digits[:, 8, 0] * 64.0 + digits[:, 9, 0]).astype(jnp.int32)
-
-    rows = [pltpu.VMEM((15 * INNER, 2 * INNER), F32), pltpu.VMEM((2, INNER, INNER), F32)]
+    here = arrived.reshape(PEERS * SLOTS, INNER)
+    here_ids = here_ids.reshape(PEERS * ID_STRIDE)
+
     points = pltpu.VMEM((PEERS * SLOTS, INNER), F32)
     screen = pltpu.VMEM((SIDE, INNER), F32)
     small = (PEERS, 4, INNER)
@@ -987,15 +1001,17 @@
         gather_kernel,
         "gather",
         [shape(small)],
-        [here_ids, here_counts, back, here] + row_inv_tables,
-        smem=2,
+        [here_ids, back, here] + row_inv_tables,
+        smem=1,
         scratch=[points, screen] + rows,
     )[0]
-    resid = call(
+    resid, from_prev, from_next = call(
         residual_kernel,
         "residual",
-        [shape(small)],
-        [slots, prec, phase],
+        [shape(small), shape(PENCILS, BF16), shape(PENCILS, BF16)],
+        [slots, prec, phase, up, down],
+        any_args=(3, 4),
+        any_outs=(1, 2),
         collective_id=2,
         scratch=[
             pltpu.VMEM((POINT_ROWS, INNER), F32),
@@ -1004,30 +1020,27 @@
             pltpu.VMEM(small, F32),
         ]
         + exchange_sems()
-        + exchange_sems(),
-    )[0]
+        + exchange_sems()
+        + [pltpu.SemaphoreType.DMA((2, 2, SIDE_PARTS))],
+    )
     pencils = call(
         scatter_kernel,
         "scatter",
         [message],
-        [here_ids, here_counts, resid.reshape(INNER, INNER), here] + row_fwd_tables,
-        smem=2,
+        [here_ids, resid.reshape(INNER, INNER), here] + row_fwd_tables,
+        smem=1,
         scratch=[pltpu.VMEM((INNER, INNER), F32), points] + rows + [screen] * COPIES,
     )[0]
     out_pencils = call(
         column_second_kernel,
         "column_second",
         [message],
-        [par, pencils, amp, own, up, down] + col_tables,
+        [par, pencils, amp, own, from_prev, from_next] + col_tables,
         smem=1,
-        any_args=(1, 4, 5),
+        any_args=(1,),
         any_outs=(0,),
         collective_id=1,
-        scratch=spectral
-        + [pltpu.VMEM(MESSAGES, BF16), pltpu.VMEM(PENCILS, BF16), pltpu.VMEM(PENCILS, BF16)]
-        + [pltpu.SemaphoreType.DMA((2, 2, SIDE_PARTS))]
-        + exchange_sems()
-        + exchange_sems(),
+        scratch=spectral + [pltpu.VMEM(MESSAGES, BF16)] + exchange_sems() + exchange_sems(),
     )[0]
     return row_backward(out_pencils, x, row_inv_tables)[None]
 

time: 313 us -> 303 us (0.968)
  starting transfers between devices: 14.8 us -> 4.92 us
    all_to_all x1 -> x0, starting transfers between devices: 11.3 us -> none  [exchange(): lax.all_to_all(value, 'strip', split_axis=0, concat_axis=0, tiled=True)]
    pallas_call x9 -> x8, Pallas kernels: 290 us -> 290 us  [call(): pl.pallas_call(kernel, out_shape=out_shapes, in_specs=[pl.BlockSpec(memor...]
  transfers between devices with their start and end apart: 2 -> 1, of which waited for: 0 -> 0; matrix products, arithmetic and copies ran while one was open for 1% -> 2% of each run, Pallas kernels for 6% -> 6%
where the time goes in v4:
time: 303 us; the launch traced here: 302 us
  Pallas kernels  290 us (96%)
  local copies, waits for them, and re-layouts  5.21 us (2%)
  starting transfers between devices  4.92 us (2%)
    pallas_call x8, Pallas kernels, call(): pl.pallas_call(kernel, out_shape=out_shapes, in_specs=[pl.BlockSpec(memor...  290 us
  transfers between devices with their start and end apart: 1, of which 0 were waited for; matrix products, arithmetic and copies ran while one was open for 2% of the time, Pallas kernels for 6%

profile of v4, /device:TPU:1, one launch (start us, length us, event | category | flops | bytes accessed | tf_op | source)
XLA Modules:
  0.0 302.4 jit_solution(9318109077666292949)
XLA Ops:
  0.7 0.7 convert_bitcast_fusion
  1.3 0.1 pad_maximum_fusion
  1.4 4.9 %collective-permute-start = (f32[3]{0:T(128)S(1)}, f32[3]{0:T(128)S(1)}, u32[]{:S(2)}, u32[]{:S(2)}) collective-permute-start(f32[3]{0:T(128)S(1)} %pad_maximum_fusion), channel_id=1, source_target_pairs={{0,32},{32,64},{64,96},{1,33},{33,65},{65,97},{2,34},{34,66},{66,9... | collective-permute-start | bytes 44 | tf_op jit(solution)/shard_map/ppermute | solution.py:947
  7.0 0.8 copy.26
  7.8 0.7 reshape.25.t_ref
  8.5 0.8 copy.27
  9.4 0.7 reshape.26.id_ref
  10.1 0.8 copy.28
  10.9 0.7 reshape.27.prec_ref
  11.6 4.6 %route.1 = (s32[64,128]{1,0:T(8,128)}, s32[32,8,128]{2,1,0:T(8,128)}) custom-call(s32[64,128]{1,0:T(8,128)} %reshape.25.t_ref, s32[64,128]{1,0:T(8,128)} %reshape.26.id_ref), custom_call_target="tpu_custom_call" | custom-call | flops 1024 | bytes 1024 | tf_op jit(solution)/shard_map/route/pallas_call | solution.py:833
  16.2 12.5 %pack.1 = bf16[16384,128]{1,0:T(8,128)(2,1)} custom-call(s32[8192]{0:T(1024)} %bitcast.22, bf16[8192,128]{1,0:T(8,128)(2,1)} %bitcast.19), custom_call_target="tpu_custom_call" | custom-call | flops 1024 | bytes 1024 | tf_op jit(solution)/shard_map/pack/pallas_call | solution.py:833
  28.7 0.0 collective-permute-done.prior
  28.7 0.0 copy-start
  28.7 0.6 copy-done
  29.3 117.0 %column_first.1 = (bf16[32,144,128]{2,1,0:T(8,128)(2,1)}, f32[32,128,128]{2,1,0:T(8,128)}, bf16[32,128,128]{2,1,0:T(8,128)(2,1)}, bf16[32,128,128]{2,1,0:T(8,128...) custom-call(f32[1]{0:T(128)S(6)} %copy.29.scale, ...), custom_call_target="tpu_custom_call" | custom-call | flops 1024 | bytes 1024 | tf_op jit(solution)/shard_map/column_first/pallas_call | solution.py:833
  146.2 22.0 %gather.1.phase_ref = f32[32,4,128]{2,1,0:T(4,128)} custom-call(s32[32768]{0:T(1024)} %bitcast.20, bf16[32,144,128]{2,1,0:T(8,128)(2,1)} %get-tuple-element.28.in_ref, bf16[16384,128]{1,0:T(8,128)(2,1)} %bitcast.14, f32[2,16,128]{2,1,0:T(8,128)} %constant.26.clone.tw.refs_2_, bf16[2,256,256]{2,1,0:T(8,128)(2,1)} %constant.33.clone.f_ref.refs_3_, ...), custom_call_target="tpu_custom_call" | custom-call | flops 1024 | bytes 1024 | tf_op jit(solution)/shard_map/gather/pallas_call | solution.py:833
  168.3 36.1 %residual.1 = (f32[32,4,128]{2,1,0:T(4,128)}, bf16[32,128,128]{2,1,0:T(8,128)(2,1)}, bf16[32,128,128]{2,1,0:T(8,128)(2,1)}) custom-call(s32[64,128]{1,0:T(8,128)} %get-tuple-element.23.slot_ref, f32[64,128]{1,0:T(8,128)} %reshape.27.prec_ref, f32[32,4,128]{2,1,0:T(4,128)} %gather.1.phase_ref, bf16[32,128,128]{2,1,0:T(8,128)(2,1)} %get-tuple-element.30.up_ref, ...), custom_call_target="tpu_custom_call" | custom-call | flops 1024 | bytes 1024 | tf_op jit(solution)/shard_map/residual/pallas_call | solution.py:833
  204.3 25.3 %scatter.1.in_ref = bf16[32,144,128]{2,1,0:T(8,128)(2,1)} custom-call(s32[32768]{0:T(1024)} %bitcast.21, f32[128,128]{1,0:T(8,128)} %bitcast.23, bf16[16384,128]{1,0:T(8,128)(2,1)} %bitcast.15, f32[2,16,128]{2,1,0:T(8,128)} %constant.26.clone.tw.refs_2_, bf16[2,256,256]{2,1,0:T(8,128)(2,1)} %constant.27.clone.f_ref, ...), custom_call_target="tpu_custom_call" | custom-call | flops 1024 | bytes 1024 | tf_op jit(solution)/shard_map/scatter/pallas_call | solution.py:833
  229.6 66.0 %column_second.1.refs_0_ = bf16[32,144,128]{2,1,0:T(8,128)(2,1)} custom-call(f32[8]{0:T(128)} %get-tuple-element.25.par, bf16[32,144,128]{2,1,0:T(8,128)(2,1)} %scatter.1.in_ref, f32[32,128,128]{2,1,0:T(8,128)} %get-tuple-element.33.amp_ref, f32[32,128,128]{2,1,0:T(8,128)} %get-tuple-element.34.own_ref, bf16[32,128,128]{2,1,0:T(8,128)(2,1)} %get-tuple-element.35.prev_ref, ...), custom_call_target="tpu_custom_call" | custom-call | flops 1024 | bytes 1024 | tf_op jit(solution)/shard_map/column_second/pallas_call | solution.py:833
  295.6 6.8 %row_backward.1 = f32[128,4096]{1,0:T(8,128)} custom-call(bf16[32,144,128]{2,1,0:T(8,128)(2,1)} %column_second.1.refs_0_, f32[128,4096]{1,0:T(8,128)} %bitcast.18, f32[2,16,128]{2,1,0:T(8,128)} %constant.26.clone.tw.refs_2_, bf16[2,256,256]{2,1,0:T(8,128)(2,1)} %constant.33.clone.f_ref.refs_3_, bf16[2,128,128]{2,1,0:T(8,128)(2,1)} %constant.34.clone.a_ref.refs_4_, ...), custom_call_target="tpu_custom_call" | custom-call | flops 1024 | bytes 1024 | tf_op jit(solution)/shard_map/row_backward/pallas_call | solution.py:833
Async XLA Ops:
  1.4 27.3 %collective-permute-start = (f32[3]{0:T(128)S(1)}, f32[3]{0:T(128)S(1)}, u32[]{:S(2)}, u32[]{:S(2)}) collective-permute-start(f32[3]{0:T(128)S(1)} %pad_maximum_fusion), channel_id=1, source_target_pairs={{0,32},{32,64},{64,96},{1,33},{33,65},{65,97},{2,34},{34,66},{66,9... | collective-permute-start | bytes 44 | tf_op jit(solution)/shard_map/ppermute | solution.py:947
  28.7 0.6 copy-start

commit v5 on v4

--- a/solution.py
+++ b/solution.py
@@ -372,7 +372,23 @@
         )
 
     def peer(self, i):
-        return lax.rem(self.me + 1 + lax.rem(i + 2 * self.me, PEERS - 1), PEERS)
+        return lax.rem(self.me + 1 + i, PEERS)
+
+    def source(self, i):
+        return lax.rem(self.me + PEERS - 1 - i, PEERS)
+
+    def send(self, i):
+        self.copy(self.peer(i), i, self.me).start()
+
+    def wait_source(self, i):
+        self.copy(self.peer(i), i, self.source(i)).wait_recv()
+
+    def wait_sends(self):
+        def step(i, carry):
+            self.copy(self.peer(i), i, self.me).wait_send()
+            return carry
+
+        lax.fori_loop(0, PEERS - 1, step, 0)
 
     def start(self, first=0, last=PEERS - 1):
         def step(i, carry):
@@ -385,14 +401,12 @@
 
     def wait(self):
         def step(i, carry):
-            peer = self.peer(i)
-            copy = self.copy(peer, i, peer)
-            copy.wait_send()
-            copy.wait_recv()
+            self.wait_source(i)
             return carry
 
         self.own.wait()
         lax.fori_loop(0, PEERS - 1, step, 0)
+        self.wait_sends()
 
 
 def exchange_sems():
@@ -445,23 +459,33 @@
 
 
 EARLY = 8
-
-
-def column_first_kernel(
-    scale, rate, wind, prior, x_ref, tw, f_ref, a_ref, m_ref, ef, ei, sent_ref, ids_ref,
-    back_ref, own_ref, up_ref, down_ref, here_ref, here_ids_ref, amp_ref, par, *scratch,
+MIDDLE = 18
+
+
+def first_kernel(
+    scale, rate, wind, prior, x_ref, tw, f_ref, a_ref, m_ref, fi_ref, ai_ref, mi_ref, ef, ei, slot_ref, prec_ref,
+    sent_ref, ids_ref,
+    own_ref, here_ref, amp_ref, resid_ref, par, here_ids_ref, prev_ref, next_ref, *scratch,
 ):
-    y_scr, z_scr, msg_scr, land_scr, tab_ref, row_scr, row_edge = scratch[0:7]
+    y_scr, z_scr, msg_scr, land_scr, back_scr, tab_ref, row_scr, row_edge = scratch[0:8]
+    up_ref, down_ref, tiles_scr, g_scr, phase_scr, landed, p_scr, table_scr, res_scr = scratch[8:17]
+    sid_scr, sid_sem, side_sems = scratch[17:20]
+    sems = scratch[20:]
     me = lax.axis_index("strip")
-    greet_peers(me, pltpu.get_barrier_semaphore())
-    ids = Exchange(me, ids_ref, here_ids_ref, *scratch[7:10])
-    weights = Exchange(me, sent_ref, here_ref, *scratch[10:13])
-    pencils = Exchange(me, msg_scr, land_scr, *scratch[13:16])
+    slot_at = lax.axis_index("tm")
+    above, below = lax.rem(slot_at + 1, 4), lax.rem(slot_at + 3, 4)
+    greet_peers(me, pltpu.get_barrier_semaphore(), ({"tm": above}, {"tm": below}))
+    ids = Exchange(me, ids_ref, here_ids_ref, *sems[0:3])
+    weights = Exchange(me, sent_ref, here_ref, *sems[3:6])
+    pencils = Exchange(me, msg_scr, land_scr, *sems[6:9])
+    back = Exchange(me, msg_scr, back_scr, *sems[9:12])
+    phases = Exchange(me, phase_scr, landed, *sems[12:15])
+    residuals = Exchange(me, res_scr, resid_ref, *sems[15:18])
     ids.start()
     weights.start(0, EARLY)
     row_forward_kernel(False, True, x_ref, tw, f_ref, a_ref, m_ref, msg_scr, row_scr, row_edge)
     pencils.start()
-    weights.start(EARLY)
+    weights.start(EARLY, MIDDLE)
     tables_kernel(scale, rate, wind, prior, tab_ref, amp_ref, par)
     pencils.wait()
     take_all(land_scr, z_scr, True)
@@ -515,11 +539,103 @@
     lax.fori_loop(0, OUTER, inverse, 0, unroll=8)
     column_first_step(z_scr, y_scr, 1.0)
     give_all(y_scr, msg_scr)
-    back = Exchange(me, msg_scr, back_ref, *scratch[16:19])
     back.start()
+    weights.start(MIDDLE, PEERS - 1)
     ids.wait()
+    fetch = pltpu.make_async_copy(here_ids_ref, sid_scr, sid_sem)
+    fetch.start()
     back.wait()
-    weights.wait()
+    row_backward_kernel(False, back_scr, tw, fi_ref, ai_ref, mi_ref, tiles_scr, row_scr, row_edge)
+    fetch.wait()
+    ones = jnp.ones((2 * INNER, INNER), BF16)
+    row = lax.broadcasted_iota(jnp.int32, (INNER, INNER), 0)
+    lane = lax.broadcasted_iota(jnp.int32, (INNER, INNER), 1)
+    place = lax.broadcasted_iota(jnp.int32, (1, INNER), 1)
+
+    def gather_source(s):
+        def some(q, carry):
+            line = q // 8
+            first = (q % 8) * 16
+            picks = [sid_scr[s, line, first + j] for j in range(16)]
+            rows = [tiles_scr[pl.ds(picks[j], 1), :] for j in range(16)]
+            for j in range(16):
+                g_scr[pl.ds(q * 16 + j, 1), :] = rows[j]
+            return carry
+
+        lax.fori_loop(0, SLOTS // 16, some, 0)
+        count = sid_scr[s, 4, 0]
+        sums = mm(jnp.concatenate(split(g_scr[...] * here_ref[s].astype(F32)), axis=1), ones)
+        for q in range(4):
+            got = jnp.where(row == lane, sums[q * INNER : (q + 1) * INNER], 0.0)
+            got = jnp.sum(got, axis=0, keepdims=True)
+            phase_scr[s, q : q + 1, :] = jnp.where(place + q * INNER < count, got, 0.0)
+
+    weights.own.wait()
+    gather_source(me)
+    phases.own.start()
+
+    def gather_next(i, carry):
+        weights.wait_source(i)
+        source = weights.source(i)
+        gather_source(source)
+        phases.copy(source, PEERS - 2 - i, me).start()
+        return carry
+
+    lax.fori_loop(0, PEERS - 1, gather_next, 0)
+    weights.wait_sends()
+
+    @pl.when(slot_at < 3)
+    def _():
+        for side in sides(side_sems, up_ref, prev_ref, above, 0):
+            side.start()
+
+    @pl.when(slot_at > 0)
+    def _():
+        for side in sides(side_sems, down_ref, next_ref, below, 1):
+            side.start()
+
+    phases.wait()
+    for s in range(PEERS):
+        table_scr[4 * s : 4 * s + 4, :] = landed[s]
+    acc = weigh(slot_ref, prec_ref, table_scr[...], p_scr)
+    for s in range(PEERS):
+        res_scr[s] = acc[4 * s : 4 * s + 4]
+    residuals.start()
+    residuals.wait()
+
+    @pl.when(slot_at < 3)
+    def _():
+        for side in sides(side_sems, up_ref, prev_ref, above, 0):
+            side.wait_send()
+        for side in sides(side_sems, down_ref, next_ref, below, 1):
+            side.wait_recv()
+
+    @pl.when(slot_at > 0)
+    def _():
+        for side in sides(side_sems, up_ref, prev_ref, above, 0):
+            side.wait_recv()
+        for side in sides(side_sems, down_ref, next_ref, below, 1):
+            side.wait_send()
+
+
+SIDE_PARTS = 4
+
+
+def sides(sems, src, dst, device, n):
+    copies = []
+    for p in range(SIDE_PARTS):
+        rows = pl.ds(p * (OUTER // SIDE_PARTS), OUTER // SIDE_PARTS)
+        copies.append(
+            pltpu.make_async_remote_copy(
+                src_ref=src.at[rows],
+                dst_ref=dst.at[rows],
+                send_sem=sems.at[0, n, p],
+                recv_sem=sems.at[1, n, p],
+                device_id={"tm": device},
+                device_id_type=MESH,
+            )
+        )
+    return copies
 
 
 def column_second_kernel(par, in_ref, amp_ref, own_ref, prev_ref, next_ref, ef, ei, back_ref, *scratch):
@@ -638,82 +754,8 @@
     lax.fori_loop(0, PEERS * SLOTS // INNER, narrow, 0, unroll=2)
 
 
-def gather_kernel(sid_ref, in_ref, w_ref, tw, f_ref, a_ref, m_ref, out_ref, g_scr, tiles_ref, z_scr, e_scr):
-    row_backward_kernel(False, in_ref, tw, f_ref, a_ref, m_ref, tiles_ref, z_scr, e_scr)
-
-    def source(s, carry):
-        def some(q, inner):
-            first = s * SLOTS + q * 16
-            line = s * ID_STRIDE + q * 16
-            ids = [sid_ref[line + j] for j in range(16)]
-            rows = [tiles_ref[pl.ds(ids[j], 1), :] for j in range(16)]
-            for j in range(16):
-                g_scr[pl.ds(first + j, 1), :] = rows[j]
-            return inner
-
-        return lax.fori_loop(0, lax.shift_right_logical(sid_ref[s * ID_STRIDE + SLOTS] + 15, 4), some, carry)
-
-    lax.fori_loop(0, PEERS, source, 0)
-    ones = jnp.ones((2 * INNER, INNER), BF16)
-    lane = lax.broadcasted_iota(jnp.int32, (INNER, INNER), 1)
-    diagonal = lane == lax.broadcasted_iota(jnp.int32, (INNER, INNER), 0)
-    place = lax.broadcasted_iota(jnp.int32, (1, INNER), 1)
-
-    def total(s, carry):
-        count = sid_ref[s * ID_STRIDE + SLOTS]
-        w = w_ref[pl.ds(pl.multiple_of(s * SLOTS, SLOTS), SLOTS), :].astype(F32)
-        g = g_scr[pl.ds(pl.multiple_of(s * SLOTS, SLOTS), SLOTS), :]
-        sums = mm(jnp.concatenate(split(g * w), axis=1), ones)
-        for q in range(4):
-            got = jnp.where(diagonal, sums[q * INNER : (q + 1) * INNER], 0.0)
-            got = jnp.sum(got, axis=0, keepdims=True)
-            out_ref[s, q : q + 1, :] = jnp.where(place + q * INNER < count, got, 0.0)
-        return carry
-
-    lax.fori_loop(0, PEERS, total, 0, unroll=2)
-
-
-SIDE_PARTS = 4
-
-
-def residual_kernel(slot_ref, prec_ref, phase_ref, up_ref, down_ref, out_ref, prev_ref, next_ref, *scratch):
-    p_scr, landed, table_scr, res_scr = scratch[0:4]
-    me = lax.axis_index("strip")
-    side_sems = scratch[10]
-    slot_at = lax.axis_index("tm")
-    above, below = lax.rem(slot_at + 1, 4), lax.rem(slot_at + 3, 4)
-    greet_peers(me, pltpu.get_barrier_semaphore(), ({"tm": above}, {"tm": below}))
-
-    def sides(n):
-        src, dst, device = ((up_ref, prev_ref, above), (down_ref, next_ref, below))[n]
-        for p in range(SIDE_PARTS):
-            rows = pl.ds(p * (OUTER // SIDE_PARTS), OUTER // SIDE_PARTS)
-            yield pltpu.make_async_remote_copy(
-                src_ref=src.at[rows],
-                dst_ref=dst.at[rows],
-                send_sem=side_sems.at[0, n, p],
-                recv_sem=side_sems.at[1, n, p],
-                device_id={"tm": device},
-                device_id_type=MESH,
-            )
-
-    phases = Exchange(me, phase_ref, landed, *scratch[4:7])
-    phases.start()
-    phases.wait()
-
-    @pl.when(slot_at < 3)
-    def _():
-        for side in sides(0):
-            side.start()
-
-    @pl.when(slot_at > 0)
-    def _():
-        for side in sides(1):
-            side.start()
-
-    for s in range(PEERS):
-        table_scr[4 * s : 4 * s + 4, :] = landed[s]
-    high, low = split(table_scr[...])
+def weigh(slot_ref, prec_ref, phase, p_scr):
+    high, low = split(phase)
     table = jnp.concatenate([high, low], axis=0)
     batch = 4
     index = lax.broadcasted_iota(jnp.int32, (INNER, batch * INNER), 0)
@@ -751,24 +793,7 @@
         return acc + mm_nt(jnp.concatenate([vh, vl], axis=0), hot)
 
     acc = lax.fori_loop(0, POINT_ROWS // batch, put, jnp.zeros((2 * INNER, INNER), F32), unroll=2)
-    acc = acc[0:INNER] + acc[INNER : 2 * INNER]
-    for s in range(PEERS):
-        res_scr[s] = acc[4 * s : 4 * s + 4]
-    residuals = Exchange(me, res_scr, out_ref, *scratch[7:10])
-    residuals.start()
-    residuals.wait()
-
-    @pl.when(slot_at < 3)
-    def _():
-        for up, down in zip(sides(0), sides(1)):
-            up.wait_send()
-            down.wait_recv()
-
-    @pl.when(slot_at > 0)
-    def _():
-        for up, down in zip(sides(0), sides(1)):
-            up.wait_recv()
-            down.wait_send()
+    return acc[0:INNER] + acc[INNER : 2 * INNER]
 
 
 COPIES = 8
@@ -964,65 +989,54 @@
     spectral = [pltpu.VMEM(PENCILS, F32), pltpu.VMEM(PENCILS, F32)]
     rows = [pltpu.VMEM((15 * INNER, 2 * INNER), F32), pltpu.VMEM((2, INNER, INNER), F32)]
     message = shape(MESSAGES, BF16)
-    back, own, up, down, arrived, here_ids, amp, par = call(
-        column_first_kernel,
-        "column_first",
+    points = pltpu.VMEM((PEERS * SLOTS, INNER), F32)
+    screen = pltpu.VMEM((SIDE, INNER), F32)
+    small = (PEERS, 4, INNER)
+    own, arrived, amp, resid, par, here_ids, from_prev, from_next = call(
+        first_kernel,
+        "first",
         [
-            message,
             shape(PENCILS),
+            shape((PEERS, SLOTS, INNER), BF16),
+            shape(PENCILS),
+            shape(small),
+            shape((8,)),
+            shape((PEERS, ID_ROWS, INNER), jnp.int32),
             shape(PENCILS, BF16),
             shape(PENCILS, BF16),
-            shape((PEERS, SLOTS, INNER), BF16),
-            shape((PEERS, ID_ROWS, INNER), jnp.int32),
-            shape(PENCILS),
-            shape((8,)),
         ],
         [prior_scale, flow_weight, wind, prior, x]
         + row_fine_tables
+        + row_inv_tables[1:]
         + col_fine_tables
-        + [sent.reshape(PEERS, SLOTS, INNER), ids],
+        + [slots, prec, sent.reshape(PEERS, SLOTS, INNER), ids],
         smem=4,
-        any_args=(11, 12),
-        any_outs=(0, 4, 5),
-        smem_outs=(7,),
+        any_args=(16, 17),
+        any_outs=(5, 6, 7),
+        smem_outs=(4,),
         collective_id=3,
         scratch=spectral
-        + [pltpu.VMEM(MESSAGES, BF16), pltpu.VMEM(MESSAGES, BF16), pltpu.VMEM((9, INNER, INNER), F32)]
+        + [pltpu.VMEM(MESSAGES, BF16)] * 3
+        + [pltpu.VMEM((9, INNER, INNER), F32)]
         + rows
-        + exchange_sems() * 4,
+        + [pltpu.VMEM(PENCILS, BF16)] * 2
+        + [
+            screen,
+            pltpu.VMEM((SLOTS, INNER), F32),
+            pltpu.VMEM(small, F32),
+            pltpu.VMEM(small, F32),
+            pltpu.VMEM((POINT_ROWS, INNER), F32),
+            pltpu.VMEM((INNER, INNER), F32),
+            pltpu.VMEM(small, F32),
+            pltpu.SMEM((PEERS, ID_ROWS, INNER), jnp.int32),
+            pltpu.SemaphoreType.DMA,
+            pltpu.SemaphoreType.DMA((2, 2, SIDE_PARTS)),
+        ]
+        + exchange_sems() * 6,
     )
     here = arrived.reshape(PEERS * SLOTS, INNER)
     here_ids = here_ids.reshape(PEERS * ID_STRIDE)
 
-    points = pltpu.VMEM((PEERS * SLOTS, INNER), F32)
-    screen = pltpu.VMEM((SIDE, INNER), F32)
-    small = (PEERS, 4, INNER)
-    phase = call(
-        gather_kernel,
-        "gather",
-        [shape(small)],
-        [here_ids, back, here] + row_inv_tables,
-        smem=1,
-        scratch=[points, screen] + rows,
-    )[0]
-    resid, from_prev, from_next = call(
-        residual_kernel,
-        "residual",
-        [shape(small), shape(PENCILS, BF16), shape(PENCILS, BF16)],
-        [slots, prec, phase, up, down],
-        any_args=(3, 4),
-        any_outs=(1, 2),
-        collective_id=2,
-        scratch=[
-            pltpu.VMEM((POINT_ROWS, INNER), F32),
-            pltpu.VMEM(small, F32),
-            pltpu.VMEM((INNER, INNER), F32),
-            pltpu.VMEM(small, F32),
-        ]
-        + exchange_sems()
-        + exchange_sems()
-        + [pltpu.SemaphoreType.DMA((2, 2, SIDE_PARTS))],
-    )
     pencils = call(
         scatter_kernel,
         "scatter",

time: 303 us -> 330 us (1.089)
  Pallas kernels: 290 us -> 316 us
    pallas_call x8 -> x6, Pallas kernels: 290 us -> 316 us  [call(): pl.pallas_call(kernel, out_shape=out_shapes, in_specs=[pl.BlockSpec(memor...]
  transfers between devices with their start and end apart: 1 -> 1, of which waited for: 0 -> 0; matrix products, arithmetic and copies ran while one was open for 2% -> 1% of each run, Pallas kernels for 6% -> 5%
where the time goes in v5:
time: 330 us; the launch traced here: 329 us
  Pallas kernels  316 us (96%)
  local copies, waits for them, and re-layouts  5.18 us (2%)
  starting transfers between devices  4.92 us (1%)
    pallas_call x6, Pallas kernels, call(): pl.pallas_call(kernel, out_shape=out_shapes, in_specs=[pl.BlockSpec(memor...  316 us
  transfers between devices with their start and end apart: 1, of which 0 were waited for; matrix products, arithmetic and copies ran while one was open for 1% of the time, Pallas kernels for 5%

profile of v5, /device:TPU:1, one launch (start us, length us, event | category | flops | bytes accessed | tf_op | source)
XLA Modules:
  0.0 328.6 jit_solution(15928249481388892776)
XLA Ops:
  0.7 0.7 convert_bitcast_fusion
  1.3 0.1 pad_maximum_fusion
  1.4 4.9 %collective-permute-start = (f32[3]{0:T(128)S(1)}, f32[3]{0:T(128)S(1)}, u32[]{:S(2)}, u32[]{:S(2)}) collective-permute-start(f32[3]{0:T(128)S(1)} %pad_maximum_fusion), channel_id=1, source_target_pairs={{0,32},{32,64},{64,96},{1,33},{33,65},{65,97},{2,34},{34,66},{66,9... | collective-permute-start | bytes 44 | tf_op jit(solution)/shard_map/ppermute | solution.py:972
  7.0 0.8 copy.26
  7.8 0.7 reshape.25.t_ref
  8.5 0.8 copy.27
  9.4 0.7 reshape.26.id_ref
  10.0 0.8 copy.28
  10.9 0.7 reshape.27.prec_ref
  11.6 4.6 %route.1 = (s32[64,128]{1,0:T(8,128)}, s32[32,8,128]{2,1,0:T(8,128)}) custom-call(s32[64,128]{1,0:T(8,128)} %reshape.25.t_ref, s32[64,128]{1,0:T(8,128)} %reshape.26.id_ref), custom_call_target="tpu_custom_call" | custom-call | flops 1024 | bytes 1024 | tf_op jit(solution)/shard_map/route/pallas_call | solution.py:858
  16.2 12.4 %pack.1 = bf16[16384,128]{1,0:T(8,128)(2,1)} custom-call(s32[8192]{0:T(1024)} %bitcast.19, bf16[8192,128]{1,0:T(8,128)(2,1)} %bitcast.18), custom_call_target="tpu_custom_call" | custom-call | flops 1024 | bytes 1024 | tf_op jit(solution)/shard_map/pack/pallas_call | solution.py:858
  28.6 0.0 collective-permute-done.prior
  28.6 0.0 copy-start
  28.6 0.6 copy-done
  29.2 201.1 %first.1 = (f32[32,128,128]{2,1,0:T(8,128)}, bf16[32,512,128]{2,1,0:T(8,128)(2,1)}, f32[32,128,128]{2,1,0:T(8,128)}, f32[32,4,128]{2,1,0:T(4,128)}, f32[8]{0:T(1...) custom-call(f32[1]{0:T(128)S(6)} %copy.29.scale, f32[1]{0:T(128)S(6)} %copy.30.rate, ...), custom_call_target="tpu_custom_call" | custom-call | flops 1024 | bytes 1024 | tf_op jit(solution)/shard_map/first/pallas_call | solution.py:858
  230.3 25.0 %scatter.1.in_ref = bf16[32,144,128]{2,1,0:T(8,128)(2,1)} custom-call(s32[32768]{0:T(1024)} %bitcast.20, f32[128,128]{1,0:T(8,128)} %bitcast.21, bf16[16384,128]{1,0:T(8,128)(2,1)} %bitcast.17, f32[2,16,128]{2,1,0:T(8,128)} %constant.26.clone.tw.refs_2_, bf16[2,256,256]{2,1,0:T(8,128)(2,1)} %constant.27.clone.f_ref, ...), custom_call_target="tpu_custom_call" | custom-call | flops 1024 | bytes 1024 | tf_op jit(solution)/shard_map/scatter/pallas_call | solution.py:858
  255.3 66.5 %column_second.1.refs_0_ = bf16[32,144,128]{2,1,0:T(8,128)(2,1)} custom-call(f32[8]{0:T(128)} %get-tuple-element.23.par, bf16[32,144,128]{2,1,0:T(8,128)(2,1)} %scatter.1.in_ref, f32[32,128,128]{2,1,0:T(8,128)} %get-tuple-element.27.amp_ref, f32[32,128,128]{2,1,0:T(8,128)} %get-tuple-element.28.own_ref, bf16[32,128,128]{2,1,0:T(8,128)(2,1)} %get-tuple-element.29.prev_ref, ...), custom_call_target="tpu_custom_call" | custom-call | flops 1024 | bytes 1024 | tf_op jit(solution)/shard_map/column_second/pallas_call | solution.py:858
  321.8 6.8 %row_backward.1 = f32[128,4096]{1,0:T(8,128)} custom-call(bf16[32,144,128]{2,1,0:T(8,128)(2,1)} %column_second.1.refs_0_, f32[128,4096]{1,0:T(8,128)} %bitcast.16, f32[2,16,128]{2,1,0:T(8,128)} %constant.26.clone.tw.refs_2_, bf16[2,256,256]{2,1,0:T(8,128)(2,1)} %constant.33.clone.fi_ref.refs_3_, bf16[2,128,128]{2,1,0:T(8,128)(2,1)} %constant.34.clone.ai_ref.refs_4_, ...), custom_call_target="tpu_custom_call" | custom-call | flops 1024 | bytes 1024 | tf_op jit(solution)/shard_map/row_backward/pallas_call | solution.py:858
Async XLA Ops:
  1.4 27.2 %collective-permute-start = (f32[3]{0:T(128)S(1)}, f32[3]{0:T(128)S(1)}, u32[]{:S(2)}, u32[]{:S(2)}) collective-permute-start(f32[3]{0:T(128)S(1)} %pad_maximum_fusion), channel_id=1, source_target_pairs={{0,32},{32,64},{64,96},{1,33},{33,65},{65,97},{2,34},{34,66},{66,9... | collective-permute-start | bytes 44 | tf_op jit(solution)/shard_map/ppermute | solution.py:972
  28.6 0.6 copy-start

commit v6 on v5

--- a/solution.py
+++ b/solution.py
@@ -307,20 +307,30 @@
     lax.fori_loop(0, 16, slab, 0, unroll=2)
 
 
-def take_all(in_ref, scr, fine):
-    def step(s, carry):
-        scr[s] = get_message(in_ref, s, fine)
-        return carry
-
-    lax.fori_loop(0, OUTER, step, 0, unroll=4)
-
-
-def give_all(scr, out_ref):
-    def step(s, carry):
-        put_message(out_ref, s, scr[s], False)
-        return carry
-
-    lax.fori_loop(0, OUTER, step, 0, unroll=4)
+def take_all(exchange, scr, fine):
+    exchange.own.wait()
+    scr[exchange.me] = get_message(exchange.out_ref, exchange.me, fine)
+
+    def step(i, carry):
+        exchange.wait_source(i)
+        source = exchange.source(i)
+        scr[source] = get_message(exchange.out_ref, source, fine)
+        return carry
+
+    lax.fori_loop(0, PEERS - 1, step, 0)
+    exchange.wait_sends()
+
+
+def give_all(scr, exchange):
+    def step(i, carry):
+        peer = exchange.peer(i)
+        put_message(exchange.in_ref, peer, scr[peer], False)
+        exchange.send(i)
+        return carry
+
+    lax.fori_loop(0, PEERS - 1, step, 0)
+    put_message(exchange.in_ref, exchange.me, scr[exchange.me], False)
+    exchange.own.start()
 
 
 def column_first_step(in_ref, y_scr, sign):
@@ -356,15 +366,18 @@
 
 
 class Exchange:
-    def __init__(self, me, in_ref, out_ref, send_sem, recv_sem, own_sem):
-        self.me, self.in_ref, self.out_ref = me, in_ref, out_ref
+    def __init__(self, me, in_ref, out_ref, send_sem, recv_sem, own_sem, flat=0):
+        self.me, self.in_ref, self.out_ref, self.flat = me, in_ref, out_ref, flat
         self.send_sem, self.recv_sem = send_sem, recv_sem
-        self.own = pltpu.make_async_copy(in_ref.at[me], out_ref.at[me], own_sem)
+        self.own = pltpu.make_async_copy(self.part(in_ref, me), self.part(out_ref, me), own_sem)
+
+    def part(self, ref, i):
+        return ref.at[pl.ds(pl.multiple_of(i * self.flat, self.flat), self.flat)] if self.flat else ref.at[i]
 
     def copy(self, peer, send, source):
         return pltpu.make_async_remote_copy(
-            src_ref=self.in_ref.at[peer],
-            dst_ref=self.out_ref.at[source],
+            src_ref=self.part(self.in_ref, peer),
+            dst_ref=self.part(self.out_ref, source),
             send_sem=self.send_sem.at[send],
             recv_sem=self.recv_sem.at[source],
             device_id={"strip": peer},
@@ -407,6 +420,19 @@
         self.own.wait()
         lax.fori_loop(0, PEERS - 1, step, 0)
         self.wait_sends()
+
+
+class Moves:
+    def __init__(self, pairs, sems):
+        self.copies = [pltpu.make_async_copy(src, dst, sems.at[i]) for i, (src, dst) in enumerate(pairs)]
+
+    def start(self):
+        for copy in self.copies:
+            copy.start()
+
+    def wait(self):
+        for copy in self.copies:
+            copy.wait()
 
 
 def exchange_sems():
@@ -463,19 +489,24 @@
 
 
 def first_kernel(
-    scale, rate, wind, prior, x_ref, tw, f_ref, a_ref, m_ref, fi_ref, ai_ref, mi_ref, ef, ei, slot_ref, prec_ref,
-    sent_ref, ids_ref,
-    own_ref, here_ref, amp_ref, resid_ref, par, here_ids_ref, prev_ref, next_ref, *scratch,
+    scale, rate, wind, prior, x_ref, tw, f_ref, a_ref, m_ref, fi_ref, ai_ref, mi_ref, slot_ref, prec_ref,
+    ef_any, ei_any, sent_ref, ids_ref,
+    resid_ref, par, own_any, here_any, amp_any, here_ids_ref, prev_ref, next_ref, *scratch,
 ):
     y_scr, z_scr, msg_scr, land_scr, back_scr, tab_ref, row_scr, row_edge = scratch[0:8]
     up_ref, down_ref, tiles_scr, g_scr, phase_scr, landed, p_scr, table_scr, res_scr = scratch[8:17]
     sid_scr, sid_sem, side_sems = scratch[17:20]
-    sems = scratch[20:]
+    ef, ei, own_ref, amp_ref, here_ref, in_sems, out_sems, here_sems = scratch[20:28]
+    sems = scratch[28:]
+    tables = Moves([(ef_any, ef), (ei_any, ei)], in_sems)
+    tables.start()
+    results = Moves([(own_ref, own_any), (amp_ref, amp_any)], out_sems)
+    weights_out = Moves([(here_ref, here_any)], here_sems)
     me = lax.axis_index("strip")
     slot_at = lax.axis_index("tm")
     above, below = lax.rem(slot_at + 1, 4), lax.rem(slot_at + 3, 4)
     greet_peers(me, pltpu.get_barrier_semaphore(), ({"tm": above}, {"tm": below}))
-    ids = Exchange(me, ids_ref, here_ids_ref, *sems[0:3])
+    ids = Exchange(me, ids_ref, here_ids_ref, *sems[0:3], flat=ID_STRIDE)
     weights = Exchange(me, sent_ref, here_ref, *sems[3:6])
     pencils = Exchange(me, msg_scr, land_scr, *sems[6:9])
     back = Exchange(me, msg_scr, back_scr, *sems[9:12])
@@ -487,8 +518,8 @@
     pencils.start()
     weights.start(EARLY, MIDDLE)
     tables_kernel(scale, rate, wind, prior, tab_ref, amp_ref, par)
-    pencils.wait()
-    take_all(land_scr, z_scr, True)
+    take_all(pencils, z_scr, True)
+    tables.wait()
     column_first_step(z_scr, y_scr, -1.0)
     flip = flip_lanes(INNER)
 
@@ -538,9 +569,9 @@
 
     lax.fori_loop(0, OUTER, inverse, 0, unroll=8)
     column_first_step(z_scr, y_scr, 1.0)
-    give_all(y_scr, msg_scr)
-    back.start()
+    give_all(y_scr, back)
     weights.start(MIDDLE, PEERS - 1)
+    results.start()
     ids.wait()
     fetch = pltpu.make_async_copy(here_ids_ref, sid_scr, sid_sem)
     fetch.start()
@@ -554,16 +585,15 @@
 
     def gather_source(s):
         def some(q, carry):
-            line = q // 8
-            first = (q % 8) * 16
-            picks = [sid_scr[s, line, first + j] for j in range(16)]
+            first = s * ID_STRIDE + q * 16
+            picks = [sid_scr[first + j] for j in range(16)]
             rows = [tiles_scr[pl.ds(picks[j], 1), :] for j in range(16)]
             for j in range(16):
                 g_scr[pl.ds(q * 16 + j, 1), :] = rows[j]
             return carry
 
         lax.fori_loop(0, SLOTS // 16, some, 0)
-        count = sid_scr[s, 4, 0]
+        count = sid_scr[s * ID_STRIDE + SLOTS]
         sums = mm(jnp.concatenate(split(g_scr[...] * here_ref[s].astype(F32)), axis=1), ones)
         for q in range(4):
             got = jnp.where(row == lane, sums[q * INNER : (q + 1) * INNER], 0.0)
@@ -583,6 +613,7 @@
 
     lax.fori_loop(0, PEERS - 1, gather_next, 0)
     weights.wait_sends()
+    weights_out.start()
 
     @pl.when(slot_at < 3)
     def _():
@@ -601,6 +632,8 @@
     for s in range(PEERS):
         res_scr[s] = acc[4 * s : 4 * s + 4]
     residuals.start()
+    results.wait()
+    weights_out.wait()
     residuals.wait()
 
     @pl.when(slot_at < 3)
@@ -638,15 +671,21 @@
     return copies
 
 
-def column_second_kernel(par, in_ref, amp_ref, own_ref, prev_ref, next_ref, ef, ei, back_ref, *scratch):
-    y_scr, z_scr, msg_scr = scratch[0:3]
+def column_second_kernel(par, in_ref, amp_any, own_any, prev_any, next_any, ef_any, ei_any, back_ref, *scratch):
+    y_scr, z_scr, msg_scr, out_scr = scratch[0:4]
+    amp_ref, own_ref, prev_ref, next_ref, ef, ei, in_sems = scratch[10:17]
+    inputs = Moves(
+        [(amp_any, amp_ref), (own_any, own_ref), (prev_any, prev_ref), (next_any, next_ref), (ef_any, ef), (ei_any, ei)],
+        in_sems,
+    )
+    inputs.start()
     me = lax.axis_index("strip")
     slot_at = lax.axis_index("tm")
     greet_peers(me, pltpu.get_barrier_semaphore())
-    pencils = Exchange(me, in_ref, msg_scr, *scratch[3:6])
+    pencils = Exchange(me, in_ref, msg_scr, *scratch[4:7])
     pencils.start()
-    pencils.wait()
-    take_all(msg_scr, z_scr, False)
+    take_all(pencils, z_scr, False)
+    inputs.wait()
     column_first_step(z_scr, y_scr, -1.0)
     flip = flip_lanes(INNER)
 
@@ -681,9 +720,8 @@
 
     lax.fori_loop(0, OUTER, inverse, 0, unroll=8)
     column_first_step(z_scr, y_scr, 1.0)
-    give_all(y_scr, msg_scr)
-    back = Exchange(me, msg_scr, back_ref, *scratch[6:9])
-    back.start()
+    back = Exchange(me, out_scr, back_ref, *scratch[7:10])
+    give_all(y_scr, back)
     back.wait()
 
 
@@ -992,28 +1030,29 @@
     points = pltpu.VMEM((PEERS * SLOTS, INNER), F32)
     screen = pltpu.VMEM((SIDE, INNER), F32)
     small = (PEERS, 4, INNER)
-    own, arrived, amp, resid, par, here_ids, from_prev, from_next = call(
+    resid, par, own, arrived, amp, here_ids, from_prev, from_next = call(
         first_kernel,
         "first",
         [
+            shape(small),
+            shape((8,)),
             shape(PENCILS),
             shape((PEERS, SLOTS, INNER), BF16),
             shape(PENCILS),
-            shape(small),
-            shape((8,)),
-            shape((PEERS, ID_ROWS, INNER), jnp.int32),
+            shape((PEERS * ID_STRIDE,), jnp.int32),
             shape(PENCILS, BF16),
             shape(PENCILS, BF16),
         ],
         [prior_scale, flow_weight, wind, prior, x]
         + row_fine_tables
         + row_inv_tables[1:]
+        + [slots, prec]
         + col_fine_tables
-        + [slots, prec, sent.reshape(PEERS, SLOTS, INNER), ids],
+        + [sent.reshape(PEERS, SLOTS, INNER), ids.reshape(-1)],
         smem=4,
-        any_args=(16, 17),
-        any_outs=(5, 6, 7),
-        smem_outs=(4,),
+        any_args=(14, 15, 16, 17),
+        any_outs=(2, 3, 4, 5, 6, 7),
+        smem_outs=(1,),
         collective_id=3,
         scratch=spectral
         + [pltpu.VMEM(MESSAGES, BF16)] * 3
@@ -1028,14 +1067,21 @@
             pltpu.VMEM((POINT_ROWS, INNER), F32),
             pltpu.VMEM((INNER, INNER), F32),
             pltpu.VMEM(small, F32),
-            pltpu.SMEM((PEERS, ID_ROWS, INNER), jnp.int32),
+            pltpu.SMEM((PEERS * ID_STRIDE,), jnp.int32),
             pltpu.SemaphoreType.DMA,
             pltpu.SemaphoreType.DMA((2, 2, SIDE_PARTS)),
+            pltpu.VMEM(col_fine_tables[0].shape, BF16),
+            pltpu.VMEM(col_fine_tables[1].shape, BF16),
+            pltpu.VMEM(PENCILS, F32),
+            pltpu.VMEM(PENCILS, F32),
+            pltpu.VMEM((PEERS, SLOTS, INNER), BF16),
+            pltpu.SemaphoreType.DMA((2,)),
+            pltpu.SemaphoreType.DMA((2,)),
+            pltpu.SemaphoreType.DMA((1,)),
         ]
         + exchange_sems() * 6,
     )
     here = arrived.reshape(PEERS * SLOTS, INNER)
-    here_ids = here_ids.reshape(PEERS * ID_STRIDE)
 
     pencils = call(
         scatter_kernel,
@@ -1051,10 +1097,17 @@
         [message],
         [par, pencils, amp, own, from_prev, from_next] + col_tables,
         smem=1,
-        any_args=(1,),
+        any_args=range(1, 8),
         any_outs=(0,),
         collective_id=1,
-        scratch=spectral + [pltpu.VMEM(MESSAGES, BF16)] + exchange_sems() + exchange_sems(),
+        scratch=spectral
+        + [pltpu.VMEM(MESSAGES, BF16)] * 2
+        + exchange_sems()
+        + exchange_sems()
+        + spectral
+        + [pltpu.VMEM(PENCILS, BF16)] * 2
+        + [pltpu.VMEM(t.shape, BF16) for t in col_tables]
+        + [pltpu.SemaphoreType.DMA((6,))],
     )[0]
     return row_backward(out_pencils, x, row_inv_tables)[None]
 

time: 330 us -> 294 us (0.89)
  Pallas kernels: 316 us -> 281 us
    pallas_call x6, Pallas kernels: 316 us -> 281 us  [call(): pl.pallas_call(kernel, out_shape=out_shapes, in_specs=[pl.BlockSpec(memor...]
  transfers between devices with their start and end apart: 1 -> 1, of which waited for: 0 -> 0; matrix products, arithmetic and copies ran while one was open for 1% -> 2% of each run, Pallas kernels for 5% -> 6%
where the time goes in v6:
time: 294 us; the launch traced here: 293 us
  Pallas kernels  281 us (96%)
  local copies, waits for them, and re-layouts  5.18 us (2%)
  starting transfers between devices  4.92 us (2%)
    pallas_call x6, Pallas kernels, call(): pl.pallas_call(kernel, out_shape=out_shapes, in_specs=[pl.BlockSpec(memor...  281 us
  transfers between devices with their start and end apart: 1, of which 0 were waited for; matrix products, arithmetic and copies ran while one was open for 2% of the time, Pallas kernels for 6%

profile of v6, /device:TPU:1, one launch (start us, length us, event | category | flops | bytes accessed | tf_op | source)
XLA Modules:
  0.0 293.3 jit_solution(6736218464420311544)
XLA Ops:
  0.7 0.7 convert_bitcast_fusion
  1.3 0.1 pad_maximum_fusion
  1.4 4.9 %collective-permute-start = (f32[3]{0:T(128)S(1)}, f32[3]{0:T(128)S(1)}, u32[]{:S(2)}, u32[]{:S(2)}) collective-permute-start(f32[3]{0:T(128)S(1)} %pad_maximum_fusion), channel_id=1, source_target_pairs={{0,32},{32,64},{64,96},{1,33},{33,65},{65,97},{2,34},{34,66},{66,9... | collective-permute-start | bytes 44 | tf_op jit(solution)/shard_map/ppermute | solution.py:1010
  7.0 0.8 copy.26
  7.8 0.7 reshape.25.t_ref
  8.5 0.8 copy.27
  9.4 0.7 reshape.26.id_ref
  10.0 0.8 copy.28
  10.9 0.7 reshape.27.prec_ref
  11.6 4.6 %route.1 = (s32[64,128]{1,0:T(8,128)}, s32[32,8,128]{2,1,0:T(8,128)}) custom-call(s32[64,128]{1,0:T(8,128)} %reshape.25.t_ref, s32[64,128]{1,0:T(8,128)} %reshape.26.id_ref), custom_call_target="tpu_custom_call" | custom-call | flops 1024 | bytes 1024 | tf_op jit(solution)/shard_map/route/pallas_call | solution.py:896
  16.2 12.4 %pack.1 = bf16[16384,128]{1,0:T(8,128)(2,1)} custom-call(s32[8192]{0:T(1024)} %bitcast.20, bf16[8192,128]{1,0:T(8,128)(2,1)} %bitcast.18), custom_call_target="tpu_custom_call" | custom-call | flops 1024 | bytes 1024 | tf_op jit(solution)/shard_map/pack/pallas_call | solution.py:896
  28.6 0.0 collective-permute-done.prior
  28.6 0.0 copy-start
  28.6 0.6 copy-done
  29.2 167.5 %first.1 = (f32[32,4,128]{2,1,0:T(4,128)}, f32[8]{0:T(128)}, f32[32,128,128]{2,1,0:T(8,128)}, bf16[32,512,128]{2,1,0:T(8,128)(2,1)}, f32[32,128,128]{2,1,0:T(8,1...) custom-call(f32[1]{0:T(128)S(6)} %copy.29.scale, f32[1]{0:T(128)S(6)} %copy.30.rate, ...), custom_call_target="tpu_custom_call" | custom-call | flops 1024 | bytes 1024 | tf_op jit(solution)/shard_map/first/pallas_call | solution.py:896
  196.7 36.0 %scatter.1.in_ref = bf16[32,144,128]{2,1,0:T(8,128)(2,1)} custom-call(s32[32768]{0:T(1024)} %get-tuple-element.24.sid_ref, f32[128,128]{1,0:T(8,128)} %bitcast.21, bf16[16384,128]{1,0:T(8,128)(2,1)} %bitcast.17, f32[2,16,128]{2,1,0:T(8,128)} %constant.26.clone.tw.refs_2_, bf16[2,256,256]{2,1,0:T(8,128)(2,1)} %constant.27.clone.f_ref, ...), custom_call_target="tpu_custom_call" | custom-call | flops 1024 | bytes 1024 | tf_op jit(solution)/shard_map/scatter/pallas_call | solution.py:896
  232.7 53.8 %column_second.1.refs_0_ = bf16[32,144,128]{2,1,0:T(8,128)(2,1)} custom-call(f32[8]{0:T(128)} %get-tuple-element.23.par, bf16[32,144,128]{2,1,0:T(8,128)(2,1)} %scatter.1.in_ref, f32[32,128,128]{2,1,0:T(8,128)} %get-tuple-element.27.amp_any, f32[32,128,128]{2,1,0:T(8,128)} %get-tuple-element.28.own_any, bf16[32,128,128]{2,1,0:T(8,128)(2,1)} %get-tuple-element.29.prev_any, ...), custom_call_target="tpu_custom_call" | custom-call | flops 1024 | bytes 1024 | tf_op jit(solution)/shard_map/column_second/pallas_call | solution.py:896
  286.5 6.8 %row_backward.1 = f32[128,4096]{1,0:T(8,128)} custom-call(bf16[32,144,128]{2,1,0:T(8,128)(2,1)} %column_second.1.refs_0_, f32[128,4096]{1,0:T(8,128)} %bitcast.16, f32[2,16,128]{2,1,0:T(8,128)} %constant.26.clone.tw.refs_2_, bf16[2,256,256]{2,1,0:T(8,128)(2,1)} %constant.33.clone.fi_ref.refs_3_, bf16[2,128,128]{2,1,0:T(8,128)(2,1)} %constant.34.clone.ai_ref.refs_4_, ...), custom_call_target="tpu_custom_call" | custom-call | flops 1024 | bytes 1024 | tf_op jit(solution)/shard_map/row_backward/pallas_call | solution.py:896
Async XLA Ops:
  1.4 27.2 %collective-permute-start = (f32[3]{0:T(128)S(1)}, f32[3]{0:T(128)S(1)}, u32[]{:S(2)}, u32[]{:S(2)}) collective-permute-start(f32[3]{0:T(128)S(1)} %pad_maximum_fusion), channel_id=1, source_target_pairs={{0,32},{32,64},{64,96},{1,33},{33,65},{65,97},{2,34},{34,66},{66,9... | collective-permute-start | bytes 44 | tf_op jit(solution)/shard_map/ppermute | solution.py:1010
  28.6 0.6 copy-start

commit v7 on v6

--- a/solution.py
+++ b/solution.py
@@ -484,8 +484,8 @@
     return c * value + s * (pltpu.roll(value, HALF, 1) * flip)
 
 
-EARLY = 8
-MIDDLE = 18
+EARLY = 4
+MIDDLE = 16
 
 
 def first_kernel(
@@ -516,9 +516,9 @@
     weights.start(0, EARLY)
     row_forward_kernel(False, True, x_ref, tw, f_ref, a_ref, m_ref, msg_scr, row_scr, row_edge)
     pencils.start()
-    weights.start(EARLY, MIDDLE)
     tables_kernel(scale, rate, wind, prior, tab_ref, amp_ref, par)
     take_all(pencils, z_scr, True)
+    weights.start(EARLY, MIDDLE)
     tables.wait()
     column_first_step(z_scr, y_scr, -1.0)
     flip = flip_lanes(INNER)
@@ -570,12 +570,12 @@
     lax.fori_loop(0, OUTER, inverse, 0, unroll=8)
     column_first_step(z_scr, y_scr, 1.0)
     give_all(y_scr, back)
-    weights.start(MIDDLE, PEERS - 1)
     results.start()
     ids.wait()
     fetch = pltpu.make_async_copy(here_ids_ref, sid_scr, sid_sem)
     fetch.start()
     back.wait()
+    weights.start(MIDDLE, PEERS - 1)
     row_backward_kernel(False, back_scr, tw, fi_ref, ai_ref, mi_ref, tiles_scr, row_scr, row_edge)
     fetch.wait()
     ones = jnp.ones((2 * INNER, INNER), BF16)
@@ -725,7 +725,13 @@
     back.wait()
 
 
-def route_kernel(t_ref, id_ref, slot_ref, tail_ref):
+def side_by_side(ref):
+    return jnp.concatenate([ref[0:POINT_ROWS, :], ref[POINT_ROWS : 2 * POINT_ROWS, :]], axis=1)
+
+
+def route_kernel(t_any, id_any, slot_ref, tail_ref, t_ref, id_ref):
+    t_ref[...] = side_by_side(t_any)
+    id_ref[...] = side_by_side(id_any)
     row = lax.broadcasted_iota(jnp.int32, (INNER, 2 * INNER), 0)
     col = lax.broadcasted_iota(jnp.int32, (INNER, 2 * INNER), 1)
     tri = jnp.where(jnp.logical_or(row < col, col >= INNER), 1.0, 0.0).astype(BF16)
@@ -777,7 +783,8 @@
     def some(q, carry):
         first = q * 32
         slots = [slot_ref[first + j] for j in range(32)]
-        rows = [w_scr[pl.ds(first + j, 1), :] for j in range(32)]
+        line = (q // 4 + (q % 4) // 2 * POINT_ROWS) * HALF + (q % 2) * 32
+        rows = [w_scr[pl.ds(line + j, 1), :] for j in range(32)]
         for j in range(32):
             buf[pl.ds(slots[j], 1), :] = rows[j]
         return carry
@@ -815,7 +822,7 @@
     row = lax.broadcasted_iota(jnp.int32, (INNER, INNER), 0)
     lane = lax.broadcasted_iota(jnp.int32, (INNER, INNER), 1)
     same = jnp.where((row < HALF) == (lane < HALF), 1.0, 0.0).astype(BF16)
-    prec = prec_ref[...]
+    prec = side_by_side(prec_ref)
     phase = p_scr[...]
 
     def total(value):
@@ -1002,9 +1009,9 @@
 
     x = screen_vec[0]
     weights = pierce_weights[0].reshape(POINT_ROWS * INNER, INNER)
-    target = pierce_point_strip.reshape(POINT_ROWS, INNER)
-    block = pierce_block.reshape(POINT_ROWS, INNER)
-    prec = noise_prec.reshape(POINT_ROWS, INNER)
+    target = pierce_point_strip.reshape(INNER, HALF)
+    block = pierce_block.reshape(INNER, HALF)
+    prec = noise_prec.reshape(INNER, HALF)
 
     mine = jnp.concatenate([flow_weight, wind[0].astype(F32)])
     prior = lax.ppermute(mine, "tm", [(i, i + 1) for i in range(lax.axis_size("tm") - 1)])
@@ -1013,6 +1020,7 @@
         "route",
         [shape((POINT_ROWS, INNER), jnp.int32), shape((PEERS, ID_ROWS, INNER), jnp.int32)],
         [target, block],
+        scratch=[pltpu.VMEM((POINT_ROWS, INNER), jnp.int32)] * 2,
     )
     ids, prior, prec = lax.optimization_barrier((ids, prior, prec))
     sent = call(

time: 294 us -> 288 us (0.980)
  Pallas kernels: 281 us -> 275 us
    pallas_call x6, Pallas kernels: 281 us -> 275 us  [call(): pl.pallas_call(kernel, out_shape=out_shapes, in_specs=[pl.BlockSpec(memor...]
  transfers between devices with their start and end apart: 1 -> 1, of which waited for: 0 -> 0; matrix products, arithmetic and copies ran while one was open for 2% -> 2% of each run, Pallas kernels for 6% -> 7%
where the time goes in v7:
time: 288 us; the launch traced here: 287 us
  Pallas kernels  275 us (95%)
  local copies, waits for them, and re-layouts  4.94 us (2%)
  starting transfers between devices  4.92 us (2%)
    pallas_call x6, Pallas kernels, call(): pl.pallas_call(kernel, out_shape=out_shapes, in_specs=[pl.BlockSpec(memor...  275 us
  transfers between devices with their start and end apart: 1, of which 0 were waited for; matrix products, arithmetic and copies ran while one was open for 2% of the time, Pallas kernels for 7%

profile of v7, /device:TPU:1, one launch (start us, length us, event | category | flops | bytes accessed | tf_op | source)
XLA Modules:
  0.0 287.3 jit_solution(18146395360646816062)
XLA Ops:
  0.7 0.7 convert_bitcast_fusion
  1.3 0.1 pad_maximum_fusion
  1.4 4.9 %collective-permute-start = (f32[3]{0:T(128)S(1)}, f32[3]{0:T(128)S(1)}, u32[]{:S(2)}, u32[]{:S(2)}) collective-permute-start(f32[3]{0:T(128)S(1)} %pad_maximum_fusion), channel_id=1, source_target_pairs={{0,32},{32,64},{64,96},{1,33},{33,65},{65,97},{2,34},{34,66},{66,9... | collective-permute-start | bytes 44 | tf_op jit(solution)/shard_map/ppermute | solution.py:1017
  7.0 1.5 copy.23
  8.4 1.5 copy.24
  9.9 1.5 copy.25
  11.4 4.8 %route.1 = (s32[64,128]{1,0:T(8,128)}, s32[32,8,128]{2,1,0:T(8,128)}) custom-call(s32[128,64]{1,0:T(8,128)} %bitcast.19, s32[128,64]{1,0:T(8,128)} %bitcast.20), custom_call_target="tpu_custom_call" | custom-call | flops 1024 | bytes 1024 | tf_op jit(solution)/shard_map/route/pallas_call | solution.py:903
  16.2 15.6 %pack.1 = bf16[16384,128]{1,0:T(8,128)(2,1)} custom-call(s32[8192]{0:T(1024)} %bitcast.22, bf16[8192,128]{1,0:T(8,128)(2,1)} %bitcast.17), custom_call_target="tpu_custom_call" | custom-call | flops 1024 | bytes 1024 | tf_op jit(solution)/shard_map/pack/pallas_call | solution.py:903
  31.8 0.0 collective-permute-done.prior
  31.8 0.0 copy-start
  31.8 0.5 copy-done
  32.3 153.7 %first.1 = (f32[32,4,128]{2,1,0:T(4,128)}, f32[8]{0:T(128)}, f32[32,128,128]{2,1,0:T(8,128)}, bf16[32,512,128]{2,1,0:T(8,128)(2,1)}, f32[32,128,128]{2,1,0:T(8,1...) custom-call(f32[1]{0:T(128)S(6)} %copy.26.scale, f32[1]{0:T(128)S(6)} %copy.27.rate, ...), custom_call_target="tpu_custom_call" | custom-call | flops 1024 | bytes 1024 | tf_op jit(solution)/shard_map/first/pallas_call | solution.py:903
  186.1 29.3 %scatter.1.in_ref = bf16[32,144,128]{2,1,0:T(8,128)(2,1)} custom-call(s32[32768]{0:T(1024)} %get-tuple-element.24.sid_ref, f32[128,128]{1,0:T(8,128)} %bitcast.23, bf16[16384,128]{1,0:T(8,128)(2,1)} %bitcast.16, f32[2,16,128]{2,1,0:T(8,128)} %constant.26.clone.tw.refs_2_, bf16[2,256,256]{2,1,0:T(8,128)(2,1)} %constant.27.clone.f_ref, ...), custom_call_target="tpu_custom_call" | custom-call | flops 1024 | bytes 1024 | tf_op jit(solution)/shard_map/scatter/pallas_call | solution.py:903
  215.4 65.1 %column_second.1.refs_0_ = bf16[32,144,128]{2,1,0:T(8,128)(2,1)} custom-call(f32[8]{0:T(128)} %get-tuple-element.23.par, bf16[32,144,128]{2,1,0:T(8,128)(2,1)} %scatter.1.in_ref, f32[32,128,128]{2,1,0:T(8,128)} %get-tuple-element.27.amp_any, f32[32,128,128]{2,1,0:T(8,128)} %get-tuple-element.28.own_any, bf16[32,128,128]{2,1,0:T(8,128)(2,1)} %get-tuple-element.29.prev_any, ...), custom_call_target="tpu_custom_call" | custom-call | flops 1024 | bytes 1024 | tf_op jit(solution)/shard_map/column_second/pallas_call | solution.py:903
  280.5 6.8 %row_backward.1 = f32[128,4096]{1,0:T(8,128)} custom-call(bf16[32,144,128]{2,1,0:T(8,128)(2,1)} %column_second.1.refs_0_, f32[128,4096]{1,0:T(8,128)} %bitcast.15, f32[2,16,128]{2,1,0:T(8,128)} %constant.26.clone.tw.refs_2_, bf16[2,256,256]{2,1,0:T(8,128)(2,1)} %constant.33.clone.fi_ref.refs_3_, bf16[2,128,128]{2,1,0:T(8,128)(2,1)} %constant.34.clone.ai_ref.refs_4_, ...), custom_call_target="tpu_custom_call" | custom-call | flops 1024 | bytes 1024 | tf_op jit(solution)/shard_map/row_backward/pallas_call | solution.py:903
Async XLA Ops:
  1.4 30.4 %collective-permute-start = (f32[3]{0:T(128)S(1)}, f32[3]{0:T(128)S(1)}, u32[]{:S(2)}, u32[]{:S(2)}) collective-permute-start(f32[3]{0:T(128)S(1)} %pad_maximum_fusion), channel_id=1, source_target_pairs={{0,32},{32,64},{64,96},{1,33},{33,65},{65,97},{2,34},{34,66},{66,9... | collective-permute-start | bytes 44 | tf_op jit(solution)/shard_map/ppermute | solution.py:1017
  31.8 0.5 copy-start

commit v8 on v6

--- a/solution.py
+++ b/solution.py
@@ -484,8 +484,8 @@
     return c * value + s * (pltpu.roll(value, HALF, 1) * flip)
 
 
-EARLY = 8
-MIDDLE = 18
+EARLY = 4
+MIDDLE = 16
 
 
 def first_kernel(
@@ -516,9 +516,9 @@
     weights.start(0, EARLY)
     row_forward_kernel(False, True, x_ref, tw, f_ref, a_ref, m_ref, msg_scr, row_scr, row_edge)
     pencils.start()
-    weights.start(EARLY, MIDDLE)
     tables_kernel(scale, rate, wind, prior, tab_ref, amp_ref, par)
     take_all(pencils, z_scr, True)
+    weights.start(EARLY, MIDDLE)
     tables.wait()
     column_first_step(z_scr, y_scr, -1.0)
     flip = flip_lanes(INNER)
@@ -570,12 +570,12 @@
     lax.fori_loop(0, OUTER, inverse, 0, unroll=8)
     column_first_step(z_scr, y_scr, 1.0)
     give_all(y_scr, back)
-    weights.start(MIDDLE, PEERS - 1)
     results.start()
     ids.wait()
     fetch = pltpu.make_async_copy(here_ids_ref, sid_scr, sid_sem)
     fetch.start()
     back.wait()
+    weights.start(MIDDLE, PEERS - 1)
     row_backward_kernel(False, back_scr, tw, fi_ref, ai_ref, mi_ref, tiles_scr, row_scr, row_edge)
     fetch.wait()
     ones = jnp.ones((2 * INNER, INNER), BF16)
@@ -585,14 +585,14 @@
 
     def gather_source(s):
         def some(q, carry):
-            first = s * ID_STRIDE + q * 16
-            picks = [sid_scr[first + j] for j in range(16)]
-            rows = [tiles_scr[pl.ds(picks[j], 1), :] for j in range(16)]
-            for j in range(16):
-                g_scr[pl.ds(q * 16 + j, 1), :] = rows[j]
+            first = s * ID_STRIDE + q * 32
+            picks = [sid_scr[first + j] for j in range(32)]
+            rows = [tiles_scr[pl.ds(picks[j], 1), :] for j in range(32)]
+            for j in range(32):
+                g_scr[pl.ds(q * 32 + j, 1), :] = rows[j]
             return carry
 
-        lax.fori_loop(0, SLOTS // 16, some, 0)
+        lax.fori_loop(0, SLOTS // 32, some, 0)
         count = sid_scr[s * ID_STRIDE + SLOTS]
         sums = mm(jnp.concatenate(split(g_scr[...] * here_ref[s].astype(F32)), axis=1), ones)
         for q in range(4):
@@ -775,9 +775,12 @@
     lax.fori_loop(0, POINT_ROWS * INNER // 64, widen, 0, unroll=2)
 
     def some(q, carry):
-        first = q * 32
-        slots = [slot_ref[first + j] for j in range(32)]
-        rows = [w_scr[pl.ds(first + j, 1), :] for j in range(32)]
+        antenna, direction = (q // 8) * 4, (q % 8) * 8
+        first = direction * INNER + antenna
+        line = pl.multiple_of(antenna * HALF + direction, 8)
+        pairs = [(a, d) for a in range(4) for d in range(8)]
+        slots = [slot_ref[first + d * INNER + a] for a, d in pairs]
+        rows = [w_scr[pl.ds(line + a * HALF + d, 1), :] for a, d in pairs]
         for j in range(32):
             buf[pl.ds(slots[j], 1), :] = rows[j]
         return carry
@@ -811,17 +814,12 @@
             p_scr[pl.ds(i * batch + j, 1), :] = got[:, j * INNER : (j + 1) * INNER]
         return carry
 
-    lax.fori_loop(0, POINT_ROWS // batch, pick, 0, unroll=2)
-    row = lax.broadcasted_iota(jnp.int32, (INNER, INNER), 0)
-    lane = lax.broadcasted_iota(jnp.int32, (INNER, INNER), 1)
-    same = jnp.where((row < HALF) == (lane < HALF), 1.0, 0.0).astype(BF16)
+    lax.fori_loop(0, POINT_ROWS // batch, pick, 0, unroll=4)
     prec = prec_ref[...]
     phase = p_scr[...]
 
-    def total(value):
-        return sum(mm(p, same) for p in reversed(split_into(value, 3)))
-
-    p_scr[...] = prec * (phase - total(prec * phase) / total(prec))
+    centre = jnp.sum(prec * phase, axis=0, keepdims=True) / jnp.sum(prec, axis=0, keepdims=True)
+    p_scr[...] = prec * (phase - centre)
 
     def put(i, acc):
         slot = wide(slot_ref, i)
@@ -830,7 +828,7 @@
         vh, vl = split(v)
         return acc + mm_nt(jnp.concatenate([vh, vl], axis=0), hot)
 
-    acc = lax.fori_loop(0, POINT_ROWS // batch, put, jnp.zeros((2 * INNER, INNER), F32), unroll=2)
+    acc = lax.fori_loop(0, POINT_ROWS // batch, put, jnp.zeros((2 * INNER, INNER), F32), unroll=4)
     return acc[0:INNER] + acc[INNER : 2 * INNER]
 
 
@@ -838,8 +836,10 @@
 
 
 def scatter_kernel(
-    sid_ref, r_ref, w_ref, tw, f_ref, a_ref, m_ref, out_ref, rt_scr, u_scr, y_scr, e_scr, *accs
+    sid_ref, r_ref, w_any, tw, f_ref, a_ref, m_ref, out_ref, rt_scr, u_scr, y_scr, e_scr, w_ref, w_sems, *accs
 ):
+    fetch = Moves([(w_any, w_ref)], w_sems)
+    fetch.start()
     def clear(i, carry):
         rows = pl.ds(pl.multiple_of(i * 64, 64), 64)
         for acc in accs:
@@ -848,6 +848,7 @@
 
     lax.fori_loop(0, SIDE // 64, clear, 0)
     rt_scr[...] = r_ref[...].T
+    fetch.wait()
     lane = lax.broadcasted_iota(jnp.int32, (INNER, INNER), 1)
     row = lax.broadcasted_iota(jnp.int32, (INNER, INNER), 0)
 
@@ -863,17 +864,17 @@
 
     def source(s, carry):
         def some(q, inner):
-            first = s * SLOTS + q * 16
-            line = s * ID_STRIDE + q * 16
-            ids = [sid_ref[line + j] for j in range(16)]
-            us = [u_scr[pl.ds(first + j, 1), :] for j in range(16)]
-            for h in range(0, 16, COPIES):
+            first = s * SLOTS + q * 32
+            line = s * ID_STRIDE + q * 32
+            ids = [sid_ref[line + j] for j in range(32)]
+            us = [u_scr[pl.ds(first + j, 1), :] for j in range(32)]
+            for h in range(0, 32, COPIES):
                 sums = [accs[j][pl.ds(ids[h + j], 1), :] + us[h + j] for j in range(COPIES)]
                 for j in range(COPIES):
                     accs[j][pl.ds(ids[h + j], 1), :] = sums[j]
             return inner
 
-        return lax.fori_loop(0, lax.shift_right_logical(sid_ref[s * ID_STRIDE + SLOTS] + 15, 4), some, carry)
+        return lax.fori_loop(0, lax.shift_right_logical(sid_ref[s * ID_STRIDE + SLOTS] + 31, 5), some, carry)
 
     lax.fori_loop(0, PEERS, source, 0)
 
@@ -1002,9 +1003,9 @@
 
     x = screen_vec[0]
     weights = pierce_weights[0].reshape(POINT_ROWS * INNER, INNER)
-    target = pierce_point_strip.reshape(POINT_ROWS, INNER)
-    block = pierce_block.reshape(POINT_ROWS, INNER)
-    prec = noise_prec.reshape(POINT_ROWS, INNER)
+    target = pierce_point_strip.reshape(INNER, HALF).T
+    block = pierce_block.reshape(INNER, HALF).T
+    prec = noise_prec.reshape(INNER, HALF).T
 
     mine = jnp.concatenate([flow_weight, wind[0].astype(F32)])
     prior = lax.ppermute(mine, "tm", [(i, i + 1) for i in range(lax.axis_size("tm") - 1)])
@@ -1089,7 +1090,11 @@
         [message],
         [here_ids, resid.reshape(INNER, INNER), here] + row_fwd_tables,
         smem=1,
-        scratch=[pltpu.VMEM((INNER, INNER), F32), points] + rows + [screen] * COPIES,
+        any_args=(2,),
+        scratch=[pltpu.VMEM((INNER, INNER), F32), points]
+        + rows
+        + [pltpu.VMEM((PEERS * SLOTS, INNER), BF16), pltpu.SemaphoreType.DMA((1,))]
+        + [screen] * COPIES,
     )[0]
     out_pencils = call(
         column_second_kernel,

time: 294 us -> 275 us (0.935)
  Pallas kernels: 281 us -> 267 us
  local copies, waits for them, and re-layouts: 5.18 us -> 0.59 us
    pallas_call x6, Pallas kernels: 281 us -> 267 us  [call(): pl.pallas_call(kernel, out_shape=out_shapes, in_specs=[pl.BlockSpec(memor...]
  transfers between devices with their start and end apart: 1 -> 1, of which waited for: 0 -> 0; matrix products, arithmetic and copies ran while one was open for 2% -> 0% of each run, Pallas kernels for 6% -> 7%
where the time goes in v8:
time: 275 us
  Pallas kernels  267 us (97%)
  starting transfers between devices  4.92 us (2%)
    pallas_call x6, Pallas kernels, call(): pl.pallas_call(kernel, out_shape=out_shapes, in_specs=[pl.BlockSpec(memor...  267 us
  transfers between devices with their start and end apart: 1, of which 0 were waited for; matrix products, arithmetic and copies ran while one was open for 0% of the time, Pallas kernels for 7%

profile of v8, /device:TPU:1, one launch (start us, length us, event | category | flops | bytes accessed | tf_op | source)
XLA Modules:
  0.0 274.8 jit_solution(17621941501734022854)
XLA Ops:
  0.7 0.7 convert_bitcast_fusion
  1.3 0.1 pad_maximum_fusion
  1.4 4.9 %collective-permute-start = (f32[3]{0:T(128)S(1)}, f32[3]{0:T(128)S(1)}, u32[]{:S(2)}, u32[]{:S(2)}) collective-permute-start(f32[3]{0:T(128)S(1)} %pad_maximum_fusion), channel_id=1, source_target_pairs={{0,32},{32,64},{64,96},{1,33},{33,65},{65,97},{2,34},{34,66},{66,9... | collective-permute-start | bytes 44 | tf_op jit(solution)/shard_map/ppermute | solution.py:1011
  7.0 4.6 %route.1 = (s32[64,128]{1,0:T(8,128)}, s32[32,8,128]{2,1,0:T(8,128)}) custom-call(s32[64,128]{1,0:T(8,128)} %bitcast.28, s32[64,128]{1,0:T(8,128)} %bitcast.29), custom_call_target="tpu_custom_call" | custom-call | flops 1024 | bytes 1024 | tf_op jit(solution)/shard_map/route/pallas_call | solution.py:897
  11.6 13.8 %pack.1 = bf16[16384,128]{1,0:T(8,128)(2,1)} custom-call(s32[8192]{0:T(1024)} %bitcast.25, bf16[8192,128]{1,0:T(8,128)(2,1)} %bitcast.23), custom_call_target="tpu_custom_call" | custom-call | flops 1024 | bytes 1024 | tf_op jit(solution)/shard_map/pack/pallas_call | solution.py:897
  25.4 0.0 collective-permute-done.prior
  25.4 0.0 copy-start
  25.4 0.6 copy-done
  26.0 151.0 %first.1 = (f32[32,4,128]{2,1,0:T(4,128)}, f32[8]{0:T(128)}, f32[32,128,128]{2,1,0:T(8,128)}, bf16[32,512,128]{2,1,0:T(8,128)(2,1)}, f32[32,128,128]{2,1,0:T(8,1...) custom-call(f32[1]{0:T(128)S(6)} %copy.23.scale, f32[1]{0:T(128)S(6)} %copy.24.rate, ...), custom_call_target="tpu_custom_call" | custom-call | flops 1024 | bytes 1024 | tf_op jit(solution)/shard_map/first/pallas_call | solution.py:897
  177.1 22.4 %scatter.1.in_ref = bf16[32,144,128]{2,1,0:T(8,128)(2,1)} custom-call(s32[32768]{0:T(1024)} %get-tuple-element.24.sid_ref, f32[128,128]{1,0:T(8,128)} %bitcast.26, bf16[16384,128]{1,0:T(8,128)(2,1)} %bitcast.22, f32[2,16,128]{2,1,0:T(8,128)} %constant.26.clone.tw.refs_2_, bf16[2,256,256]{2,1,0:T(8,128)(2,1)} %constant.27.clone.f_ref, ...), custom_call_target="tpu_custom_call" | custom-call | flops 1024 | bytes 1024 | tf_op jit(solution)/shard_map/scatter/pallas_call | solution.py:897
  199.5 68.5 %column_second.1.refs_0_ = bf16[32,144,128]{2,1,0:T(8,128)(2,1)} custom-call(f32[8]{0:T(128)} %get-tuple-element.23.par, bf16[32,144,128]{2,1,0:T(8,128)(2,1)} %scatter.1.in_ref, f32[32,128,128]{2,1,0:T(8,128)} %get-tuple-element.27.amp_any, f32[32,128,128]{2,1,0:T(8,128)} %get-tuple-element.28.own_any, bf16[32,128,128]{2,1,0:T(8,128)(2,1)} %get-tuple-element.29.prev_any, ...), custom_call_target="tpu_custom_call" | custom-call | flops 1024 | bytes 1024 | tf_op jit(solution)/shard_map/column_second/pallas_call | solution.py:897
  268.0 6.8 %row_backward.1 = f32[128,4096]{1,0:T(8,128)} custom-call(bf16[32,144,128]{2,1,0:T(8,128)(2,1)} %column_second.1.refs_0_, f32[128,4096]{1,0:T(8,128)} %bitcast.21, f32[2,16,128]{2,1,0:T(8,128)} %constant.26.clone.tw.refs_2_, bf16[2,256,256]{2,1,0:T(8,128)(2,1)} %constant.33.clone.fi_ref.refs_3_, bf16[2,128,128]{2,1,0:T(8,128)(2,1)} %constant.34.clone.ai_ref.refs_4_, ...), custom_call_target="tpu_custom_call" | custom-call | flops 1024 | bytes 1024 | tf_op jit(solution)/shard_map/row_backward/pallas_call | solution.py:897
Async XLA Ops:
  1.4 24.0 %collective-permute-start = (f32[3]{0:T(128)S(1)}, f32[3]{0:T(128)S(1)}, u32[]{:S(2)}, u32[]{:S(2)}) collective-permute-start(f32[3]{0:T(128)S(1)} %pad_maximum_fusion), channel_id=1, source_target_pairs={{0,32},{32,64},{64,96},{1,33},{33,65},{65,97},{2,34},{34,66},{66,9... | collective-permute-start | bytes 44 | tf_op jit(solution)/shard_map/ppermute | solution.py:1011
  25.4 0.6 copy-start

commit v9 on v8

--- a/solution.py
+++ b/solution.py
@@ -365,6 +365,10 @@
     pl.semaphore_wait(barrier, PEERS - 1 + len(extra))
 
 
+STRIDE = 11
+REPLY = 45
+
+
 class Exchange:
     def __init__(self, me, in_ref, out_ref, send_sem, recv_sem, own_sem, flat=0):
         self.me, self.in_ref, self.out_ref, self.flat = me, in_ref, out_ref, flat
@@ -385,10 +389,13 @@
         )
 
     def peer(self, i):
-        return lax.rem(self.me + 1 + i, PEERS)
+        return lax.rem(self.me + 1 + lax.rem(i * STRIDE, PEERS - 1), PEERS)
 
     def source(self, i):
-        return lax.rem(self.me + PEERS - 1 - i, PEERS)
+        return lax.rem(self.me + PEERS - 1 - lax.rem(i * STRIDE, PEERS - 1), PEERS)
+
+    def reply(self, i):
+        return lax.rem(REPLY - i, PEERS - 1)
 
     def send(self, i):
         self.copy(self.peer(i), i, self.me).start()
@@ -583,35 +590,45 @@
     lane = lax.broadcasted_iota(jnp.int32, (INNER, INNER), 1)
     place = lax.broadcasted_iota(jnp.int32, (1, INNER), 1)
 
-    def gather_source(s):
+    def pick(s, place_at):
         def some(q, carry):
             first = s * ID_STRIDE + q * 32
             picks = [sid_scr[first + j] for j in range(32)]
             rows = [tiles_scr[pl.ds(picks[j], 1), :] for j in range(32)]
             for j in range(32):
-                g_scr[pl.ds(q * 32 + j, 1), :] = rows[j]
+                g_scr[pl.ds(place_at + q * 32 + j, 1), :] = rows[j]
             return carry
 
         lax.fori_loop(0, SLOTS // 32, some, 0)
-        count = sid_scr[s * ID_STRIDE + SLOTS]
-        sums = mm(jnp.concatenate(split(g_scr[...] * here_ref[s].astype(F32)), axis=1), ones)
-        for q in range(4):
-            got = jnp.where(row == lane, sums[q * INNER : (q + 1) * INNER], 0.0)
-            got = jnp.sum(got, axis=0, keepdims=True)
-            phase_scr[s, q : q + 1, :] = jnp.where(place + q * INNER < count, got, 0.0)
-
+
+    def gather_pair(pair):
+        for n, s in enumerate(pair):
+            pick(s, n * SLOTS)
+        for n, s in enumerate(pair):
+            count = sid_scr[s * ID_STRIDE + SLOTS]
+            picked = g_scr[n * SLOTS : (n + 1) * SLOTS, :]
+            sums = mm(jnp.concatenate(split(picked * here_ref[s].astype(F32)), axis=1), ones)
+            for q in range(4):
+                got = jnp.where(row == lane, sums[q * INNER : (q + 1) * INNER], 0.0)
+                got = jnp.sum(got, axis=0, keepdims=True)
+                phase_scr[s, q : q + 1, :] = jnp.where(place + q * INNER < count, got, 0.0)
+
+    def gather_next(h, carry):
+        steps = (2 * h, 2 * h + 1)
+        for i in steps:
+            weights.wait_source(i)
+        gather_pair([weights.source(i) for i in steps])
+        for i in steps:
+            phases.copy(weights.source(i), phases.reply(i), me).start()
+        return carry
+
+    lax.fori_loop(0, PEERS // 2 - 1, gather_next, 0)
     weights.own.wait()
-    gather_source(me)
+    weights.wait_source(PEERS - 2)
+    last = weights.source(PEERS - 2)
+    gather_pair([last, me])
+    phases.copy(last, phases.reply(PEERS - 2), me).start()
     phases.own.start()
-
-    def gather_next(i, carry):
-        weights.wait_source(i)
-        source = weights.source(i)
-        gather_source(source)
-        phases.copy(source, PEERS - 2 - i, me).start()
-        return carry
-
-    lax.fori_loop(0, PEERS - 1, gather_next, 0)
     weights.wait_sends()
     weights_out.start()
 
@@ -1062,7 +1079,7 @@
         + [pltpu.VMEM(PENCILS, BF16)] * 2
         + [
             screen,
-            pltpu.VMEM((SLOTS, INNER), F32),
+            pltpu.VMEM((2 * SLOTS, INNER), F32),
             pltpu.VMEM(small, F32),
             pltpu.VMEM(small, F32),
             pltpu.VMEM((POINT_ROWS, INNER), F32),

time: 275 us -> 252 us (0.916); the launches traced: 275 us -> 248 us
  Pallas kernels: 267 us -> 241 us
    pallas_call x6, Pallas kernels: 267 us -> 241 us  [call(): pl.pallas_call(kernel, out_shape=out_shapes, in_specs=[pl.BlockSpec(memor...]
where the time goes in v9:
time: 252 us; the launch traced here: 248 us
  Pallas kernels  241 us (96%)
  starting transfers between devices  4.92 us (2%)
    pallas_call x6, Pallas kernels, call(): pl.pallas_call(kernel, out_shape=out_shapes, in_specs=[pl.BlockSpec(memor...  241 us
  transfers between devices with their start and end apart: 1, of which 0 were waited for; matrix products, arithmetic and copies ran while one was open for 0% of the time, Pallas kernels for 7%

profile of v9, /device:TPU:1, one launch (start us, length us, event | category | flops | bytes accessed | tf_op | source)
XLA Modules:
  0.0 248.2 jit_solution(16259956714474202182)
XLA Ops:
  0.7 0.7 convert_bitcast_fusion
  1.3 0.1 pad_maximum_fusion
  1.4 4.9 %collective-permute-start = (f32[3]{0:T(128)S(1)}, f32[3]{0:T(128)S(1)}, u32[]{:S(2)}, u32[]{:S(2)}) collective-permute-start(f32[3]{0:T(128)S(1)} %pad_maximum_fusion), channel_id=1, source_target_pairs={{0,32},{32,64},{64,96},{1,33},{33,65},{65,97},{2,34},{34,66},{66,9... | collective-permute-start | bytes 44 | tf_op jit(solution)/shard_map/ppermute | solution.py:1028
  7.0 4.6 %route.1 = (s32[64,128]{1,0:T(8,128)}, s32[32,8,128]{2,1,0:T(8,128)}) custom-call(s32[64,128]{1,0:T(8,128)} %bitcast.28, s32[64,128]{1,0:T(8,128)} %bitcast.29), custom_call_target="tpu_custom_call" | custom-call | flops 1024 | bytes 1024 | tf_op jit(solution)/shard_map/route/pallas_call | solution.py:914
  11.6 13.8 %pack.1 = bf16[16384,128]{1,0:T(8,128)(2,1)} custom-call(s32[8192]{0:T(1024)} %bitcast.25, bf16[8192,128]{1,0:T(8,128)(2,1)} %bitcast.23), custom_call_target="tpu_custom_call" | custom-call | flops 1024 | bytes 1024 | tf_op jit(solution)/shard_map/pack/pallas_call | solution.py:914
  25.4 0.0 collective-permute-done.prior
  25.4 0.0 copy-start
  25.4 0.6 copy-done
  26.0 133.7 %first.1 = (f32[32,4,128]{2,1,0:T(4,128)}, f32[8]{0:T(128)}, f32[32,128,128]{2,1,0:T(8,128)}, bf16[32,512,128]{2,1,0:T(8,128)(2,1)}, f32[32,128,128]{2,1,0:T(8,1...) custom-call(f32[1]{0:T(128)S(6)} %copy.23.scale, f32[1]{0:T(128)S(6)} %copy.24.rate, ...), custom_call_target="tpu_custom_call" | custom-call | flops 1024 | bytes 1024 | tf_op jit(solution)/shard_map/first/pallas_call | solution.py:914
  159.7 22.8 %scatter.1.in_ref = bf16[32,144,128]{2,1,0:T(8,128)(2,1)} custom-call(s32[32768]{0:T(1024)} %get-tuple-element.24.sid_ref, f32[128,128]{1,0:T(8,128)} %bitcast.26, bf16[16384,128]{1,0:T(8,128)(2,1)} %bitcast.22, f32[2,16,128]{2,1,0:T(8,128)} %constant.26.clone.tw.refs_2_, bf16[2,256,256]{2,1,0:T(8,128)(2,1)} %constant.27.clone.f_ref, ...), custom_call_target="tpu_custom_call" | custom-call | flops 1024 | bytes 1024 | tf_op jit(solution)/shard_map/scatter/pallas_call | solution.py:914
  182.5 58.7 %column_second.1.refs_0_ = bf16[32,144,128]{2,1,0:T(8,128)(2,1)} custom-call(f32[8]{0:T(128)} %get-tuple-element.23.par, bf16[32,144,128]{2,1,0:T(8,128)(2,1)} %scatter.1.in_ref, f32[32,128,128]{2,1,0:T(8,128)} %get-tuple-element.27.amp_any, f32[32,128,128]{2,1,0:T(8,128)} %get-tuple-element.28.own_any, bf16[32,128,128]{2,1,0:T(8,128)(2,1)} %get-tuple-element.29.prev_any, ...), custom_call_target="tpu_custom_call" | custom-call | flops 1024 | bytes 1024 | tf_op jit(solution)/shard_map/column_second/pallas_call | solution.py:914
  241.3 6.8 %row_backward.1 = f32[128,4096]{1,0:T(8,128)} custom-call(bf16[32,144,128]{2,1,0:T(8,128)(2,1)} %column_second.1.refs_0_, f32[128,4096]{1,0:T(8,128)} %bitcast.21, f32[2,16,128]{2,1,0:T(8,128)} %constant.26.clone.tw.refs_2_, bf16[2,256,256]{2,1,0:T(8,128)(2,1)} %constant.33.clone.fi_ref.refs_3_, bf16[2,128,128]{2,1,0:T(8,128)(2,1)} %constant.34.clone.ai_ref.refs_4_, ...), custom_call_target="tpu_custom_call" | custom-call | flops 1024 | bytes 1024 | tf_op jit(solution)/shard_map/row_backward/pallas_call | solution.py:914
Async XLA Ops:
  1.4 24.0 %collective-permute-start = (f32[3]{0:T(128)S(1)}, f32[3]{0:T(128)S(1)}, u32[]{:S(2)}, u32[]{:S(2)}) collective-permute-start(f32[3]{0:T(128)S(1)} %pad_maximum_fusion), channel_id=1, source_target_pairs={{0,32},{32,64},{64,96},{1,33},{33,65},{65,97},{2,34},{34,66},{66,9... | collective-permute-start | bytes 44 | tf_op jit(solution)/shard_map/ppermute | solution.py:1028
  25.4 0.6 copy-start

commit v10 on v9

--- a/solution.py
+++ b/solution.py
@@ -308,28 +308,40 @@
 
 
 def take_all(exchange, scr, fine):
+    def unpack(pair):
+        values = [get_message(exchange.out_ref, source, fine) for source in pair]
+        for source, value in zip(pair, values):
+            scr[source] = value
+
+    def step(h, carry):
+        steps = (2 * h, 2 * h + 1)
+        for i in steps:
+            exchange.wait_source(i)
+        unpack([exchange.source(i) for i in steps])
+        return carry
+
+    lax.fori_loop(0, PEERS // 2 - 1, step, 0)
     exchange.own.wait()
-    scr[exchange.me] = get_message(exchange.out_ref, exchange.me, fine)
-
-    def step(i, carry):
-        exchange.wait_source(i)
-        source = exchange.source(i)
-        scr[source] = get_message(exchange.out_ref, source, fine)
-        return carry
-
-    lax.fori_loop(0, PEERS - 1, step, 0)
+    exchange.wait_source(PEERS - 2)
+    unpack([exchange.source(PEERS - 2), exchange.me])
     exchange.wait_sends()
 
 
 def give_all(scr, exchange):
-    def step(i, carry):
-        peer = exchange.peer(i)
-        put_message(exchange.in_ref, peer, scr[peer], False)
-        exchange.send(i)
-        return carry
-
-    lax.fori_loop(0, PEERS - 1, step, 0)
-    put_message(exchange.in_ref, exchange.me, scr[exchange.me], False)
+    def pack(pair):
+        for peer in pair:
+            put_message(exchange.in_ref, peer, scr[peer], False)
+
+    def step(h, carry):
+        steps = (2 * h, 2 * h + 1)
+        pack([exchange.peer(i) for i in steps])
+        for i in steps:
+            exchange.send(i)
+        return carry
+
+    lax.fori_loop(0, PEERS // 2 - 1, step, 0)
+    pack([exchange.peer(PEERS - 2), exchange.me])
+    exchange.send(PEERS - 2)
     exchange.own.start()
 
 
@@ -492,7 +504,7 @@
 
 
 EARLY = 4
-MIDDLE = 16
+MIDDLE = 18
 
 
 def first_kernel(
@@ -504,7 +516,8 @@
     up_ref, down_ref, tiles_scr, g_scr, phase_scr, landed, p_scr, table_scr, res_scr = scratch[8:17]
     sid_scr, sid_sem, side_sems = scratch[17:20]
     ef, ei, own_ref, amp_ref, here_ref, in_sems, out_sems, here_sems = scratch[20:28]
-    sems = scratch[28:]
+    fix_scr = scratch[28]
+    sems = scratch[29:]
     tables = Moves([(ef_any, ef), (ei_any, ei)], in_sems)
     tables.start()
     results = Moves([(own_ref, own_any), (amp_ref, amp_any)], out_sems)
@@ -554,18 +567,16 @@
         mask, _ = edge_lanes()
         e0 = a0 * u0
         e2 = a2 * u2
-        fixed = [par[0] * (e0 + e2)]
+        change = par[0] * (e0 + e2)
         e0 = a0 * e0
         e2 = a2 * e2
-        fixed.append(par[3] * (e0 + e2))
-        fixed.append(par[1] * turn(tab_ref[4], tab_ref[5], e0 + par[4] * e2, flip))
-        fixed.append(par[2] * turn(tab_ref[6], tab_ref[7], e0 + par[5] * e2, flip))
+        fix_scr[0] = par[3] * (e0 + e2)
+        fix_scr[1] = par[1] * turn(tab_ref[4], tab_ref[5], e0 + par[4] * e2, flip)
+        fix_scr[2] = par[2] * turn(tab_ref[6], tab_ref[7], e0 + par[5] * e2, flip)
 
         def put(k1, carry):
             back = lax.rem(INNER - k1, INNER)
-            for ref, value in zip((z_scr, own_ref, up_ref, down_ref), fixed):
-                value = jnp.where(mask, pltpu.roll(value, back, 1), ref[k1].astype(F32))
-                ref[k1] = value.astype(ref.dtype)
+            z_scr[k1] = jnp.where(mask, pltpu.roll(change, back, 1), z_scr[k1])
             return carry
 
         lax.fori_loop(0, OUTER, put, 0, unroll=4)
@@ -577,6 +588,20 @@
     lax.fori_loop(0, OUTER, inverse, 0, unroll=8)
     column_first_step(z_scr, y_scr, 1.0)
     give_all(y_scr, back)
+
+    @pl.when(me == 0)
+    def _():
+        mask, _ = edge_lanes()
+
+        def put(k1, carry):
+            place_at = lax.rem(INNER - k1, INNER)
+            for n, ref in enumerate((own_ref, up_ref, down_ref)):
+                value = jnp.where(mask, pltpu.roll(fix_scr[n], place_at, 1), ref[k1].astype(F32))
+                ref[k1] = value.astype(ref.dtype)
+            return carry
+
+        lax.fori_loop(0, OUTER, put, 0, unroll=2)
+
     results.start()
     ids.wait()
     fetch = pltpu.make_async_copy(here_ids_ref, sid_scr, sid_sem)
@@ -877,7 +902,7 @@
             u_scr[rows, :] = jnp.where(used, w_ref[rows, :].astype(F32) * col, 0.0)
         return carry
 
-    lax.fori_loop(0, PEERS, scaled, 0, unroll=2)
+    lax.fori_loop(0, PEERS, scaled, 0, unroll=4)
 
     def source(s, carry):
         def some(q, inner):
@@ -1096,6 +1121,7 @@
             pltpu.SemaphoreType.DMA((2,)),
             pltpu.SemaphoreType.DMA((2,)),
             pltpu.SemaphoreType.DMA((1,)),
+            pltpu.VMEM((3, INNER, INNER), F32),
         ]
         + exchange_sems() * 6,
     )

time: 252 us -> 250 us (level)
  no operation moved by 1% of the time
where the time goes in v10:
time: 250 us; the launch traced here: 248 us
  Pallas kernels  241 us (96%)
  starting transfers between devices  4.92 us (2%)
    pallas_call x6, Pallas kernels, call(): pl.pallas_call(kernel, out_shape=out_shapes, in_specs=[pl.BlockSpec(memor...  241 us
  transfers between devices with their start and end apart: 1, of which 0 were waited for; matrix products, arithmetic and copies ran while one was open for 0% of the time, Pallas kernels for 7%

profile of v10, /device:TPU:1, one launch (start us, length us, event | category | flops | bytes accessed | tf_op | source)
XLA Modules:
  0.0 248.3 jit_solution(4364629201021867145)
XLA Ops:
  0.7 0.7 convert_bitcast_fusion
  1.3 0.1 pad_maximum_fusion
  1.4 4.9 %collective-permute-start = (f32[3]{0:T(128)S(1)}, f32[3]{0:T(128)S(1)}, u32[]{:S(2)}, u32[]{:S(2)}) collective-permute-start(f32[3]{0:T(128)S(1)} %pad_maximum_fusion), channel_id=1, source_target_pairs={{0,32},{32,64},{64,96},{1,33},{33,65},{65,97},{2,34},{34,66},{66,9... | collective-permute-start | bytes 44 | tf_op jit(solution)/shard_map/ppermute | solution.py:1053
  7.0 4.6 %route.1 = (s32[64,128]{1,0:T(8,128)}, s32[32,8,128]{2,1,0:T(8,128)}) custom-call(s32[64,128]{1,0:T(8,128)} %bitcast.28, s32[64,128]{1,0:T(8,128)} %bitcast.29), custom_call_target="tpu_custom_call" | custom-call | flops 1024 | bytes 1024 | tf_op jit(solution)/shard_map/route/pallas_call | solution.py:939
  11.6 13.8 %pack.1 = bf16[16384,128]{1,0:T(8,128)(2,1)} custom-call(s32[8192]{0:T(1024)} %bitcast.25, bf16[8192,128]{1,0:T(8,128)(2,1)} %bitcast.23), custom_call_target="tpu_custom_call" | custom-call | flops 1024 | bytes 1024 | tf_op jit(solution)/shard_map/pack/pallas_call | solution.py:939
  25.4 0.0 collective-permute-done.prior
  25.4 0.0 copy-start
  25.4 0.6 copy-done
  26.0 132.9 %first.1 = (f32[32,4,128]{2,1,0:T(4,128)}, f32[8]{0:T(128)}, f32[32,128,128]{2,1,0:T(8,128)}, bf16[32,512,128]{2,1,0:T(8,128)(2,1)}, f32[32,128,128]{2,1,0:T(8,1...) custom-call(f32[1]{0:T(128)S(6)} %copy.23.scale, f32[1]{0:T(128)S(6)} %copy.24.rate, ...), custom_call_target="tpu_custom_call" | custom-call | flops 1024 | bytes 1024 | tf_op jit(solution)/shard_map/first/pallas_call | solution.py:939
  159.0 21.9 %scatter.1.in_ref = bf16[32,144,128]{2,1,0:T(8,128)(2,1)} custom-call(s32[32768]{0:T(1024)} %get-tuple-element.24.sid_ref, f32[128,128]{1,0:T(8,128)} %bitcast.26, bf16[16384,128]{1,0:T(8,128)(2,1)} %bitcast.22, f32[2,16,128]{2,1,0:T(8,128)} %constant.26.clone.tw.refs_2_, bf16[2,256,256]{2,1,0:T(8,128)(2,1)} %constant.27.clone.f_ref, ...), custom_call_target="tpu_custom_call" | custom-call | flops 1024 | bytes 1024 | tf_op jit(solution)/shard_map/scatter/pallas_call | solution.py:939
  180.9 60.6 %column_second.1.refs_0_ = bf16[32,144,128]{2,1,0:T(8,128)(2,1)} custom-call(f32[8]{0:T(128)} %get-tuple-element.23.par, bf16[32,144,128]{2,1,0:T(8,128)(2,1)} %scatter.1.in_ref, f32[32,128,128]{2,1,0:T(8,128)} %get-tuple-element.27.amp_any, f32[32,128,128]{2,1,0:T(8,128)} %get-tuple-element.28.own_any, bf16[32,128,128]{2,1,0:T(8,128)(2,1)} %get-tuple-element.29.prev_any, ...), custom_call_target="tpu_custom_call" | custom-call | flops 1024 | bytes 1024 | tf_op jit(solution)/shard_map/column_second/pallas_call | solution.py:939
  241.4 6.8 %row_backward.1 = f32[128,4096]{1,0:T(8,128)} custom-call(bf16[32,144,128]{2,1,0:T(8,128)(2,1)} %column_second.1.refs_0_, f32[128,4096]{1,0:T(8,128)} %bitcast.21, f32[2,16,128]{2,1,0:T(8,128)} %constant.26.clone.tw.refs_2_, bf16[2,256,256]{2,1,0:T(8,128)(2,1)} %constant.33.clone.fi_ref.refs_3_, bf16[2,128,128]{2,1,0:T(8,128)(2,1)} %constant.34.clone.ai_ref.refs_4_, ...), custom_call_target="tpu_custom_call" | custom-call | flops 1024 | bytes 1024 | tf_op jit(solution)/shard_map/row_backward/pallas_call | solution.py:939
Async XLA Ops:
  1.4 24.0 %collective-permute-start = (f32[3]{0:T(128)S(1)}, f32[3]{0:T(128)S(1)}, u32[]{:S(2)}, u32[]{:S(2)}) collective-permute-start(f32[3]{0:T(128)S(1)} %pad_maximum_fusion), channel_id=1, source_target_pairs={{0,32},{32,64},{64,96},{1,33},{33,65},{65,97},{2,34},{34,66},{66,9... | collective-permute-start | bytes 44 | tf_op jit(solution)/shard_map/ppermute | solution.py:1053
  25.4 0.6 copy-start

commit v11 on v10

--- a/solution.py
+++ b/solution.py
@@ -504,7 +504,7 @@
 
 
 EARLY = 4
-MIDDLE = 18
+MIDDLE = 21
 
 
 def first_kernel(

time: 250 us -> 250 us (level)
  no operation moved by 1% of the time
where the time goes in v11:
time: 250 us; the launch traced here: 246 us
  Pallas kernels  239 us (96%)
  starting transfers between devices  4.92 us (2%)
    pallas_call x6, Pallas kernels, call(): pl.pallas_call(kernel, out_shape=out_shapes, in_specs=[pl.BlockSpec(memor...  239 us
  transfers between devices with their start and end apart: 1, of which 0 were waited for; matrix products, arithmetic and copies ran while one was open for 0% of the time, Pallas kernels for 7%

profile of v11, /device:TPU:1, one launch (start us, length us, event | category | flops | bytes accessed | tf_op | source)
XLA Modules:
  0.0 246.5 jit_solution(11513224580553266324)
XLA Ops:
  0.7 0.7 convert_bitcast_fusion
  1.3 0.1 pad_maximum_fusion
  1.4 4.9 %collective-permute-start = (f32[3]{0:T(128)S(1)}, f32[3]{0:T(128)S(1)}, u32[]{:S(2)}, u32[]{:S(2)}) collective-permute-start(f32[3]{0:T(128)S(1)} %pad_maximum_fusion), channel_id=1, source_target_pairs={{0,32},{32,64},{64,96},{1,33},{33,65},{65,97},{2,34},{34,66},{66,9... | collective-permute-start | bytes 44 | tf_op jit(solution)/shard_map/ppermute | solution.py:1053
  7.0 4.6 %route.1 = (s32[64,128]{1,0:T(8,128)}, s32[32,8,128]{2,1,0:T(8,128)}) custom-call(s32[64,128]{1,0:T(8,128)} %bitcast.28, s32[64,128]{1,0:T(8,128)} %bitcast.29), custom_call_target="tpu_custom_call" | custom-call | flops 1024 | bytes 1024 | tf_op jit(solution)/shard_map/route/pallas_call | solution.py:939
  11.6 13.8 %pack.1 = bf16[16384,128]{1,0:T(8,128)(2,1)} custom-call(s32[8192]{0:T(1024)} %bitcast.25, bf16[8192,128]{1,0:T(8,128)(2,1)} %bitcast.23), custom_call_target="tpu_custom_call" | custom-call | flops 1024 | bytes 1024 | tf_op jit(solution)/shard_map/pack/pallas_call | solution.py:939
  25.4 0.0 collective-permute-done.prior
  25.4 0.0 copy-start
  25.4 0.6 copy-done
  26.0 133.5 %first.1 = (f32[32,4,128]{2,1,0:T(4,128)}, f32[8]{0:T(128)}, f32[32,128,128]{2,1,0:T(8,128)}, bf16[32,512,128]{2,1,0:T(8,128)(2,1)}, f32[32,128,128]{2,1,0:T(8,1...) custom-call(f32[1]{0:T(128)S(6)} %copy.23.scale, f32[1]{0:T(128)S(6)} %copy.24.rate, ...), custom_call_target="tpu_custom_call" | custom-call | flops 1024 | bytes 1024 | tf_op jit(solution)/shard_map/first/pallas_call | solution.py:939
  159.6 23.1 %scatter.1.in_ref = bf16[32,144,128]{2,1,0:T(8,128)(2,1)} custom-call(s32[32768]{0:T(1024)} %get-tuple-element.24.sid_ref, f32[128,128]{1,0:T(8,128)} %bitcast.26, bf16[16384,128]{1,0:T(8,128)(2,1)} %bitcast.22, f32[2,16,128]{2,1,0:T(8,128)} %constant.26.clone.tw.refs_2_, bf16[2,256,256]{2,1,0:T(8,128)(2,1)} %constant.27.clone.f_ref, ...), custom_call_target="tpu_custom_call" | custom-call | flops 1024 | bytes 1024 | tf_op jit(solution)/shard_map/scatter/pallas_call | solution.py:939
  182.7 57.0 %column_second.1.refs_0_ = bf16[32,144,128]{2,1,0:T(8,128)(2,1)} custom-call(f32[8]{0:T(128)} %get-tuple-element.23.par, bf16[32,144,128]{2,1,0:T(8,128)(2,1)} %scatter.1.in_ref, f32[32,128,128]{2,1,0:T(8,128)} %get-tuple-element.27.amp_any, f32[32,128,128]{2,1,0:T(8,128)} %get-tuple-element.28.own_any, bf16[32,128,128]{2,1,0:T(8,128)(2,1)} %get-tuple-element.29.prev_any, ...), custom_call_target="tpu_custom_call" | custom-call | flops 1024 | bytes 1024 | tf_op jit(solution)/shard_map/column_second/pallas_call | solution.py:939
  239.6 6.8 %row_backward.1 = f32[128,4096]{1,0:T(8,128)} custom-call(bf16[32,144,128]{2,1,0:T(8,128)(2,1)} %column_second.1.refs_0_, f32[128,4096]{1,0:T(8,128)} %bitcast.21, f32[2,16,128]{2,1,0:T(8,128)} %constant.26.clone.tw.refs_2_, bf16[2,256,256]{2,1,0:T(8,128)(2,1)} %constant.33.clone.fi_ref.refs_3_, bf16[2,128,128]{2,1,0:T(8,128)(2,1)} %constant.34.clone.ai_ref.refs_4_, ...), custom_call_target="tpu_custom_call" | custom-call | flops 1024 | bytes 1024 | tf_op jit(solution)/shard_map/row_backward/pallas_call | solution.py:939
Async XLA Ops:
  1.4 24.0 %collective-permute-start = (f32[3]{0:T(128)S(1)}, f32[3]{0:T(128)S(1)}, u32[]{:S(2)}, u32[]{:S(2)}) collective-permute-start(f32[3]{0:T(128)S(1)} %pad_maximum_fusion), channel_id=1, source_target_pairs={{0,32},{32,64},{64,96},{1,33},{33,65},{65,97},{2,34},{34,66},{66,9... | collective-permute-start | bytes 44 | tf_op jit(solution)/shard_map/ppermute | solution.py:1053
  25.4 0.6 copy-start
